TPU v7x, 32 devices: a whole 2x2x4 slice. The times are simulated.
32 devices in a mesh: batch: 8 (over z, core), rows: 4 (over y, x).
Axes of the slice: x: 2, y: 2, z: 4, core: 2. Of those that a mesh axis runs over, the one named last changes fastest.
Arguments:
- velocity: float32 [16, 2, 128, 128], P('batch', None, 'rows'), may hold values from -4 to 4
- targets: float32 [16, 2, 2, 128, 128], P('batch', None, None, 'rows'), may hold values from -4 to 4
- keyframes: int32 [16, 2], P('batch'), may hold values from 0 to 4, as said below
- boxes: int32 [16, 2, 4], P('batch'), may hold values from 0 to 128, as said below
- w_in: float32 [64, 3, 3, 3], replicated, may hold values from -1.25 to 1.25
- w_mid: float32 [5, 9, 4096], replicated, may hold values from -0.25 to 0.25
- norm_params: float32 [2, 5, 64], replicated, may hold values from 0.5 to 1.5
- head_params: float32 [2, 65], replicated, may hold values from -0.75 to 0.75
- m_in: float32 [64, 3, 3, 3], replicated, may hold values from -3.8146973e-06 to 3.8146973e-06
- m_mid: float32 [5, 9, 4096], replicated, may hold values from -3.8146973e-06 to 3.8146973e-06
- m_norm: float32 [2, 5, 64], replicated, may hold values from -3.8146973e-06 to 3.8146973e-06
- m_head: float32 [2, 65], replicated, may hold values from -3.8146973e-06 to 3.8146973e-06
- v_in: float32 [64, 3, 3, 3], replicated, may hold values from 2.8155747e-13 to 1.1240887e-12
- v_mid: float32 [5, 9, 4096], replicated, may hold values from 2.8155747e-13 to 1.1240887e-12
- v_norm: float32 [2, 5, 64], replicated, may hold values from 2.8155747e-13 to 1.1240887e-12
- v_head: float32 [2, 65], replicated, may hold values from 2.8155747e-13 to 1.1240887e-12
Outputs:
- new_w_in: float32 [64, 3, 3, 3], replicated
- new_w_mid: float32 [5, 9, 4096], replicated
- new_norm: float32 [2, 5, 64], replicated
- new_head: float32 [2, 65], replicated
- new_m_in: float32 [64, 3, 3, 3], replicated
- new_m_mid: float32 [5, 9, 4096], replicated
- new_m_norm: float32 [2, 5, 64], replicated
- new_m_head: float32 [2, 65], replicated
- new_v_in: float32 [64, 3, 3, 3], replicated
- new_v_mid: float32 [5, 9, 4096], replicated
- new_v_norm: float32 [2, 5, 64], replicated
- new_v_head: float32 [2, 65], replicated
- low_w_in: bfloat16 [64, 3, 3, 3], replicated
- low_w_mid: bfloat16 [5, 9, 4096], replicated
- low_head: bfloat16 [2, 65], replicated
- loss_sum: float32 [], replicated
- frame_cells: float32 [], replicated
- grad_norm: float32 [], replicated
Inputs may be any that keep to these rules, and one draw needn't show every extreme that they name: `keyframes`: 0 marks an unused slot; slot 0 of every sample is used. `boxes`: each box has a first index below its end index, spans 8 to 32 lines along each side.
All inputs are finite; a program needn't handle non-finite values.
Results may differ from a plain program's by a relative error of at most 0.0089.
The roundings to bfloat16 on the way count: a program that leaves them out, or rounds other values in their place, can miss the bound.
Values may be sent and summed in bfloat16 or wider, within the bound.
A program may use at most 576 MiB of HBM per device.

v0:
```python
import jax
import jax.numpy as jnp
from jax import lax
from jax.sharding import PartitionSpec as P

CH = 64
GROUPS = 8
LAYERS = 4
STEPS = 4
JACOBI = 4
STEP_NUM = 10


EPS_NORM = 1e-05
DT_FORCE = 0.5
DT_ADV = 0.2
CLIP_NORM = 0.001
BETA_ONE = 0.9
BETA_TWO = 0.95
ADAM_EPS = 1e-08
DECAY = 0.01
RATES = (0.2, 0.05, 1.0, 0.15)
NUMBERS = ("NCHW", "OIHW", "NCHW")


def with_halo(cells, sides, width):
    for axis, dim in sides:
        count = lax.axis_size(axis)
        ends = count - 1
        head = lax.slice_in_dim(cells, 0, width, axis=dim)
        tail = lax.slice_in_dim(cells, cells.shape[dim] - width, cells.shape[dim], axis=dim)
        cells = jnp.concatenate(
            [
                lax.ppermute(tail, axis, [(i, (i + 1) % count) for i in range(ends)]),
                cells,
                lax.ppermute(head, axis, [((i + 1) % count, i) for i in range(ends)]),
            ],
            axis=dim,
        )
    return cells


def open_mask(boxes, rows_at, cols_at):
    r = rows_at[None, None, :, None]
    c = cols_at[None, None, None, :]
    b = boxes[:, :, :, None, None]
    inside = (r >= b[:, :, 0]) & (r < b[:, :, 1]) & (c >= b[:, :, 2]) & (c < b[:, :, 3])
    return 1.0 - jnp.max(inside.astype(jnp.float32), axis=1)


def kernel_of(flat):
    return jnp.transpose(flat.reshape(3, 3, CH, CH), (2, 3, 0, 1))


def flat_of(kernel):
    return jnp.transpose(kernel, (2, 3, 0, 1)).reshape(9, CH * CH)


def pad_cols(x):
    return jnp.pad(x, ((0, 0), (0, 0), (0, 0), (1, 1)))


def framed(x):
    return pad_cols(with_halo(x, (("rows", 2),), 1))


def drows(q):
    return 0.5 * (q[:, :, 2:, 1:-1] - q[:, :, :-2, 1:-1])


def dcols(q):
    return 0.5 * (q[:, :, 1:-1, 2:] - q[:, :, 1:-1, :-2])


def nsum(q):
    return q[:, :, 2:, 1:-1] + q[:, :, :-2, 1:-1] + q[:, :, 1:-1, 2:] + q[:, :, 1:-1, :-2]


def advect_local(q):
    inner = q[:, :, 1:-1, 1:-1]
    return inner - DT_ADV * (inner[:, 0:1] * drows(q) + inner[:, 1:2] * dcols(q))


def project_core(v):
    q = framed(v)
    div = drows(q[:, 0:1]) + dcols(q[:, 1:2])
    press = -0.25 * div
    for sweep in range(JACOBI - 1):
        press = 0.25 * (nsum(framed(press)) - div)
    r = framed(press)
    return v - jnp.concatenate([drows(r), dcols(r)], axis=1)


def rim_return(grad_q):
    edges = jnp.concatenate([grad_q[:, :, 0:1, 1:-1], grad_q[:, :, -1:, 1:-1]], axis=2)
    beside_all = with_halo(edges, (("rows", 2),), 1)
    inner = grad_q[:, :, 1:-1, 1:-1]
    inner = inner.at[:, :, 0:1].add(beside_all[:, :, 0:1])
    return inner.at[:, :, -1:].add(beside_all[:, :, 3:4])


def into_fluid(x, adjoint):
    if adjoint:
        moved = lax.all_to_all(x, "rows", split_axis=3, concat_axis=2, tiled=True)
    else:
        moved = lax.all_to_all(x, "rows", split_axis=3, concat_axis=2, tiled=True)
    result = jnp.swapaxes(moved, 2, 3)[:, ::-1]
    return result


def out_of_fluid(x, adjoint):
    turned = jnp.swapaxes(x[:, ::-1], 2, 3)
    if adjoint:
        result = lax.all_to_all(turned, "rows", split_axis=2, concat_axis=3, tiled=True)
    else:
        result = lax.all_to_all(turned, "rows", split_axis=2, concat_axis=3, tiled=True)
    return result


def block_sum(x):
    samples, chans, tile, width = x.shape
    return jnp.sum(x.reshape(samples, chans, tile // 2, 2, width // 2, 2), axis=(3, 5))


def upsample(h):
    return jnp.repeat(jnp.repeat(h, 2, axis=2), 2, axis=3)


def layer_forward(h, weight, gain, shift):
    padded = pad_cols(with_halo(h, (("rows", 2),), 1))
    z = lax.conv_general_dilated(
        padded,
        weight,
        (1, 1),
        "VALID",
        dimension_numbers=NUMBERS,
        preferred_element_type=jnp.float32,
    )
    samples, chans, tile, width = z.shape
    grouped = z.reshape(samples, GROUPS, chans // GROUPS, tile, width)
    sums, squares = lax.psum(
        (jnp.sum(grouped, axis=(2, 3, 4)), jnp.sum(grouped * grouped, axis=(2, 3, 4))), "rows"
    )
    members = chans // GROUPS * tile * width * lax.axis_size("rows")
    mean = (sums / members)[:, :, None, None, None]
    inverse = lax.rsqrt(squares[:, :, None, None, None] / members - mean * mean + EPS_NORM)
    scaled = ((grouped - mean) * inverse).reshape(z.shape)
    normed = scaled * gain[None, :, None, None] + shift[None, :, None, None]
    return (jax.nn.silu(normed).astype(jnp.bfloat16), (padded, scaled, inverse, normed))


def layer_backward(h_bar, kept, weight, gain):
    padded, scaled, inverse, normed = kept
    sig = jax.nn.sigmoid(normed)
    n_bar = h_bar * sig * (1.0 + normed * (1.0 - sig))
    g_gain = jnp.sum(n_bar * scaled, axis=(0, 2, 3))
    g_shift = jnp.sum(n_bar, axis=(0, 2, 3))
    samples, chans, tile, width = scaled.shape
    shape_groups = (samples, GROUPS, chans // GROUPS, tile, width)
    x_bar = (n_bar * gain[None, :, None, None]).reshape(shape_groups)
    x_hat = scaled.reshape(shape_groups)
    total_bar, total_cross = lax.psum(
        (jnp.sum(x_bar, axis=(2, 3, 4)), jnp.sum(x_bar * x_hat, axis=(2, 3, 4))), "rows"
    )
    members = chans // GROUPS * tile * width * lax.axis_size("rows")
    z_bar = inverse * (
        x_bar
        - total_bar[:, :, None, None, None] / members
        - x_hat * total_cross[:, :, None, None, None] / members
    )
    z_low = z_bar.reshape(scaled.shape).astype(jnp.bfloat16)
    g_weight = jnp.stack(
        [
            jnp.stack(
                [
                    jnp.einsum(
                        "soyx,siyx->oi",
                        z_low,
                        padded[:, :, ky : ky + tile, kx : kx + width],
                        preferred_element_type=jnp.float32,
                    )
                    for kx in range(3)
                ],
                axis=-1,
            )
            for ky in range(3)
        ],
        axis=-2,
    )
    beside_all = pad_cols(with_halo(z_low, (("rows", 2),), 1))
    flipped = jnp.swapaxes(jnp.flip(weight, axis=(2, 3)), 0, 1)
    h_in_bar = lax.conv_general_dilated(
        beside_all,
        flipped,
        (1, 1),
        "VALID",
        dimension_numbers=NUMBERS,
        preferred_element_type=jnp.float32,
    )
    return (h_in_bar, g_weight, g_gain, g_shift)


def net_forward(h0, weights, norm_params):
    h1, kept0 = layer_forward(h0, weights[0], norm_params[0, 0], norm_params[1, 0])
    skip, kept1 = layer_forward(h1, weights[1], norm_params[0, 1], norm_params[1, 1])
    pooled = (0.25 * block_sum(skip.astype(jnp.float32))).astype(jnp.bfloat16)
    h3, kept2 = layer_forward(pooled, weights[2], norm_params[0, 2], norm_params[1, 2])
    h4, kept3 = layer_forward(h3, weights[3], norm_params[0, 3], norm_params[1, 3])
    joined = jnp.concatenate([upsample(h4), skip], axis=1)
    h5, kept4 = layer_forward(joined, weights[4], norm_params[0, 4], norm_params[1, 4])
    return (h5, [kept0, kept1, kept2, kept3, kept4])


def net_backward(h_bar, kept_layers, weights, norm_params, g_weights, g_gains, g_shifts):

    def through(bar, layer):
        bar_in, g_weight, g_gain, g_shift = layer_backward(
            bar, kept_layers[layer], weights[layer], norm_params[0, layer]
        )
        g_weights[layer] = g_weights[layer] + g_weight
        g_gains[layer] = g_gains[layer] + g_gain
        g_shifts[layer] = g_shifts[layer] + g_shift
        return bar_in

    joined_bar = through(h_bar, 4)
    skip_bar = joined_bar[:, CH:]
    h4_bar = block_sum(joined_bar[:, :CH])
    h3_bar = through(h4_bar, 3)
    pooled_bar = through(h3_bar, 2)
    skip_bar = skip_bar + 0.25 * upsample(pooled_bar)
    h1_bar = through(skip_bar, 1)
    return through(h1_bar, 0)


def shards(
    velocity,
    targets,
    keyframes,
    boxes,
    w_in,
    w_mid,
    norm_params,
    head_params,
    m_in,
    m_mid,
    m_norm,
    m_head,
    v_in,
    v_mid,
    v_norm,
    v_head,
):
    samples, comps, tile, width = velocity.shape
    parts = lax.axis_size("rows")
    place = lax.axis_index("rows")
    opened = open_mask(boxes, place * tile + jnp.arange(tile), jnp.arange(width))[:, None]
    slab = width // parts
    turned = jnp.stack([boxes[:, :, 2], boxes[:, :, 3], boxes[:, :, 0], boxes[:, :, 1]], axis=2)
    fluid_open = open_mask(turned, place * slab + jnp.arange(slab), jnp.arange(tile * parts))[
        :, None
    ]
    live_cells = jnp.sum(
        (keyframes > 0).astype(jnp.float32) * jnp.sum(opened, axis=(1, 2, 3))[:, None]
    )
    count = lax.psum(live_cells, ("batch", "rows"))
    last_kernel = jnp.concatenate([kernel_of(w_mid[3]), kernel_of(w_mid[4])], axis=1)
    weights = (
        [w_in.astype(jnp.bfloat16)]
        + [kernel_of(w_mid[k]).astype(jnp.bfloat16) for k in range(3)]
        + [last_kernel.astype(jnp.bfloat16)]
    )
    head_low = head_params[:, :CH].astype(jnp.bfloat16)
    u = velocity
    loss_local = jnp.zeros((), jnp.float32)
    kept_steps = []
    for step in range(STEPS):
        h0 = jnp.concatenate([u, opened], axis=1).astype(jnp.bfloat16)
        h, kept_layers = net_forward(h0, weights, norm_params)
        force = (
            jnp.einsum("oc,schw->sohw", head_low, h, preferred_element_type=jnp.float32)
            + head_params[:, CH][None, :, None, None]
        )
        pushed = (u + DT_FORCE * force) * opened
        framed_in = framed(into_fluid(pushed, False))
        settled = fluid_open * project_core(advect_local(framed_in))
        u = out_of_fluid(settled, False)
        live = (keyframes == step + 1).astype(jnp.float32)[:, :, None, None, None]
        miss = u[:, None] - targets
        loss_local = loss_local + jnp.sum(live * opened[:, None] * miss * miss)
        kept_steps.append((kept_layers, h, framed_in, miss, live))
    u_bar = jnp.zeros_like(velocity)
    g_weights = [jnp.zeros(w.shape, jnp.float32) for w in weights]
    g_gains = [jnp.zeros((CH,), jnp.float32) for k in range(LAYERS + 1)]
    g_shifts = [jnp.zeros((CH,), jnp.float32) for k in range(LAYERS + 1)]
    g_head = jnp.zeros((2, CH), jnp.float32)
    g_bias = jnp.zeros((2,), jnp.float32)
    for step in reversed(range(STEPS)):
        kept_layers, h_last, framed_in, miss, live = kept_steps[step]
        u_bar = u_bar + 2.0 / count * opened * jnp.sum(live * miss, axis=1)
        settled_bar = project_core(fluid_open * into_fluid(u_bar, True))
        advected, pull = jax.vjp(advect_local, framed_in)
        (q_bar,) = pull(settled_bar)
        pushed_bar = out_of_fluid(rim_return(q_bar), True)
        force_bar = DT_FORCE * opened * pushed_bar
        u_bar = opened * pushed_bar
        g_bias = g_bias + jnp.sum(force_bar, axis=(0, 2, 3))
        force_low = force_bar.astype(jnp.bfloat16)
        g_head = g_head + jnp.einsum(
            "sohw,schw->oc", force_low, h_last, preferred_element_type=jnp.float32
        )
        h_bar = jnp.einsum("oc,sohw->schw", head_low, force_low, preferred_element_type=jnp.float32)
        h_bar = net_backward(h_bar, kept_layers, weights, norm_params, g_weights, g_gains, g_shifts)
        u_bar = u_bar + h_bar[:, 0:2]
    g_last = g_weights[4]
    g_mid = jnp.stack(
        [
            flat_of(g_weights[1]),
            flat_of(g_weights[2]),
            flat_of(g_weights[3]),
            flat_of(g_last[:, :CH]),
            flat_of(g_last[:, CH:]),
        ]
    )
    g_norm = jnp.stack([jnp.stack(g_gains), jnp.stack(g_shifts)])
    g_head_all = jnp.concatenate([g_head, g_bias[:, None]], axis=1)
    grads_in, grads_mid, grads_norm, grads_head, loss_sum = lax.psum(
        (g_weights[0], g_mid, g_norm, g_head_all, loss_local), ("batch", "rows")
    )
    grads = (grads_in, grads_mid, grads_norm, grads_head)
    params = (w_in, w_mid, norm_params, head_params)
    norm = jnp.sqrt(sum((jnp.sum(g * g) for g in grads)))
    scale = jnp.minimum(1.0, CLIP_NORM / norm)
    new_w, new_m, new_v = ([], [], [])
    for weight, moment, second, g, rate in zip(
        params, (m_in, m_mid, m_norm, m_head), (v_in, v_mid, v_norm, v_head), grads, RATES
    ):
        g = g * scale
        moment_new = BETA_ONE * moment + (1 - BETA_ONE) * g
        second_new = BETA_TWO * second + (1 - BETA_TWO) * g * g
        mhat = moment_new / (1 - BETA_ONE**STEP_NUM)
        vhat = second_new / (1 - BETA_TWO**STEP_NUM)
        new_w.append(weight - rate * (mhat / (jnp.sqrt(vhat) + ADAM_EPS) + DECAY * weight))
        new_m.append(moment_new)
        new_v.append(second_new)
    return (
        new_w[0],
        new_w[1],
        new_w[2],
        new_w[3],
        new_m[0],
        new_m[1],
        new_m[2],
        new_m[3],
        new_v[0],
        new_v[1],
        new_v[2],
        new_v[3],
        new_w[0].astype(jnp.bfloat16),
        new_w[1].astype(jnp.bfloat16),
        new_w[3].astype(jnp.bfloat16),
        loss_sum,
        count,
        norm,
    )


def solution(mesh):
    return jax.shard_map(
        shards,
        mesh=mesh,
        in_specs=(
            P("batch", None, "rows", None),
            P("batch", None, None, "rows", None),
            P("batch", None),
            P("batch", None, None),
            P(),
            P(),
            P(),
            P(),
            P(),
            P(),
            P(),
            P(),
            P(),
            P(),
            P(),
            P(),
        ),
        out_specs=(
            P(),
            P(),
            P(),
            P(),
            P(),
            P(),
            P(),
            P(),
            P(),
            P(),
            P(),
            P(),
            P(),
            P(),
            P(),
            P(),
            P(),
            P(),
        ),
        check_vma=False,
    )
```

profile of v0, /device:TPU:0, one launch (start us, length us, event | category | flops | bytes accessed | tf_op | source)
XLA Modules:
  0.0 3250.2 jit_solution(6150493271214808605)
XLA Ops:
  50.6 11.0 multiply_convert_fusion.11
  99.5 11.4 all-reduce.131
  113.4 11.6 add_divide_fusion.10
  255.4 10.7 all-reduce.128
  268.6 11.1 add_divide_fusion.9
  349.5 11.3 all_to_all.286
  397.8 10.9 multiply_convert_fusion.8
  444.1 10.6 all-reduce.126
  457.3 11.6 add_divide_fusion.7
  597.6 10.7 all-reduce.123
  610.9 10.9 add_divide_fusion.6
  692.4 11.3 all_to_all.288
  739.4 11.0 multiply_convert_fusion.5
  785.6 10.5 all-reduce.121
  798.7 11.6 add_divide_fusion.4
  938.1 10.7 all-reduce.118
  951.4 10.9 add_divide_fusion.3
  1031.4 11.3 all_to_all.290
  1079.1 10.9 multiply_convert_fusion.2
  1124.7 10.8 all-reduce.116
  1138.1 11.6 multiply_convert_fusion.1
  1276.3 10.5 all-reduce.113
  1289.4 14.8 multiply_convert_fusion
  1352.4 41.7 %psum.642 = f32[]{:T(128)} all-reduce(f32[]{:T(128)} %fusion.818), channel_id=1, replica_groups=mesh['batch'=8,'rows'=4] {'batch','rows'}, use_global_device_ids=true, to_apply=%region_128.129 | all-reduce | flops 1 | bytes 8 | tf_op jit(solution)/shard_map/psum | solution.py:265
  1788.5 11.3 all-reduce.111
  1868.8 10.5 all-reduce.109
  1939.1 10.5 all-reduce.108
  1952.1 16.6 fusion.40
  1991.3 25.9 fusion.357
  2176.1 10.4 all-reduce.106
  2216.2 10.5 all-reduce.105
  2259.3 10.7 all-reduce.104
  2329.5 10.7 all-reduce.103
  2342.7 16.6 fusion.34
  2381.6 25.9 fusion.360
  2566.1 10.5 all-reduce.101
  2606.1 10.7 all-reduce.100
  2649.3 10.5 all-reduce.99
  2719.4 10.5 all-reduce.98
  2732.4 16.6 fusion.28
  2771.6 25.9 fusion.363
  2965.6 10.4 all-reduce.96
  3008.6 10.6 all-reduce.95
  3052.6 10.5 all-reduce.94
  3113.6 17.2 select_reduce_fusion.4
  3140.3 10.5 all-reduce.93
  3153.4 16.6 fusion.22
  3180.3 40.1 %all-reduce.92 = (f32[64,3,3,3]{0,1,3,2:T(4,128)S(1)}, f32[2,5,64]{2,1,0:T(8,128)S(1)}, f32[2,65]{1,0:T(2,128)S(1)}, f32[]{:T(128)}) all-reduce(f32[64,3,3,3]{0,1,3,2:T(4,128)S(1)} %fusion.806, f32[2,5,64]{2,1,0:T(8,128)S(1)} %pad_maximum_fusion.230, ...), channel_id=1, replica_groups=mesh['batch'=8,'rows'=4] {'batch','rows'}, use_global_device_ids=true, to_apply=%region_265.266 | all-reduce | flops 2499 | bytes 19992 | tf_op jit(solution)/shard_map/psum | solution.py:326
  (3659 shorter events, 2552.5 us)
Async XLA Ops:
  13.0 8.3 collective-permute-start
  62.5 10.6 collective-permute-start.2
  65.0 8.2 collective-permute-start.3
  218.3 7.3 collective-permute-start.9
  560.6 7.3 collective-permute-start.31
  901.8 7.3 collective-permute-start.53
  1238.0 7.3 collective-permute-start.75
  1344.7 50.1 %collective-permute-start.82 = (f32[2,1,1,128]{3,2,1,0:T(1,128)S(1)}, f32[2,1,1,128]{3,2,1,0:T(1,128)S(1)}, u32[]{:S(2)}, u32[]{:S(2)}) collective-permute-start(f32[2,1,1,128]{3,2,1,0:T(1,128)S(1)} %get-tuple-element.842), channel_id=1, source_target_pairs={{1,0},{2,1},{3,2},{5,4},{6,5},{7,6},{9,8},{10,9},{11,10},{13,12},{... | collective-permute-start | bytes 3080 | tf_op jit(solution)/shard_map/ppermute | solution.py:36
  1346.0 48.8 %collective-permute-start.83 = (f32[2,1,1,128]{3,2,1,0:T(1,128)S(1)}, f32[2,1,1,128]{3,2,1,0:T(1,128)S(1)}, u32[]{:S(2)}, u32[]{:S(2)}) collective-permute-start(f32[2,1,1,128]{3,2,1,0:T(1,128)S(1)} %get-tuple-element.841), channel_id=1, source_target_pairs={{0,1},{1,2},{2,3},{4,5},{5,6},{6,7},{8,9},{9,10},{10,11},{12,13},{... | collective-permute-start | bytes 3080 | tf_op jit(solution)/shard_map/ppermute | solution.py:34
  1402.6 8.3 collective-permute-start.86
  1412.2 57.5 %all-to-all-start.7 = ((f32[4,1,4096]{2,1,0:T(1,128)}), f32[4,1,4096]{2,1,0:T(1,128)S(1)}, u32[]{:S(2)}, u32[]{:S(2)}) async-start(f32[4,1,4096]{2,1,0:T(1,128)} %reshape.2571), calls=%async_computation.7 | async-start | bytes 131072 | tf_op jit(solution)/shard_map/all_to_all | solution.py:116
  1473.2 55.4 %all-to-all-start.8 = ((f32[4,1,4096]{2,1,0:T(1,128)}), f32[4,1,4096]{2,1,0:T(1,128)S(1)}, u32[]{:S(2)}, u32[]{:S(2)}) async-start(f32[4,1,4096]{2,1,0:T(1,128)} %reshape.2573), calls=%async_computation.8 | async-start | bytes 131072 | tf_op jit(solution)/shard_map/all_to_all | solution.py:104
  1537.5 23.6 collective-permute-start.90
  1538.8 22.4 collective-permute-start.91
  1561.3 44.1 %collective-permute-start.92 = (f32[2,1,1,128]{3,2,1,0:T(1,128)S(1)}, f32[2,1,1,128]{3,2,1,0:T(1,128)S(1)}, u32[]{:S(2)}, u32[]{:S(2)}) collective-permute-start(f32[2,1,1,128]{3,2,1,0:T(1,128)S(1)} %get-tuple-element.829), channel_id=1, source_target_pairs={{1,0},{2,1},{3,2},{5,4},{6,5},{7,6},{9,8},{10,9},{11,10},{13,12},{... | collective-permute-start | bytes 3080 | tf_op jit(solution)/shard_map/ppermute | solution.py:36
  1562.8 42.7 %collective-permute-start.93 = (f32[2,1,1,128]{3,2,1,0:T(1,128)S(1)}, f32[2,1,1,128]{3,2,1,0:T(1,128)S(1)}, u32[]{:S(2)}, u32[]{:S(2)}) collective-permute-start(f32[2,1,1,128]{3,2,1,0:T(1,128)S(1)} %get-tuple-element.828), channel_id=1, source_target_pairs={{0,1},{1,2},{2,3},{4,5},{5,6},{6,7},{8,9},{9,10},{10,11},{12,13},{... | collective-permute-start | bytes 3080 | tf_op jit(solution)/shard_map/ppermute | solution.py:34
  1605.6 7.6 collective-permute-start.94
  1613.9 18.4 collective-permute-start.96
  1615.2 17.1 collective-permute-start.97
  1644.7 52.7 %all-to-all-start.9 = ((f32[4,1,4096]{2,1,0:T(1,128)}), f32[4,1,4096]{2,1,0:T(1,128)}, u32[]{:S(2)}, u32[]{:S(2)}) async-start(f32[4,1,4096]{2,1,0:T(1,128)} %reshape.2575), calls=%async_computation.9 | async-start | bytes 131072 | tf_op jit(solution)/shard_map/all_to_all | solution.py:114
  1745.0 8.2 collective-permute-start.100
  1805.8 7.8 collective-permute-start.102
  1903.9 8.2 collective-permute-start.107
  2020.1 9.0 all-to-all-start.10
  2053.8 7.4 collective-permute-start.116
  2062.3 7.6 collective-permute-start.118
  2084.4 9.0 all-to-all-start.11
  2132.8 9.8 collective-permute-start.122
  2192.5 7.3 collective-permute-start.124
  2294.5 8.2 collective-permute-start.129
  2410.5 9.0 all-to-all-start.12
  2436.0 7.1 collective-permute-start.136
  2444.2 7.4 collective-permute-start.138
  2452.7 7.6 collective-permute-start.140
  2474.8 9.0 all-to-all-start.13
  2523.3 9.8 collective-permute-start.144
  2582.6 7.3 collective-permute-start.146
  2684.4 8.2 collective-permute-start.151
  2800.5 9.0 all-to-all-start.14
  2825.9 7.1 collective-permute-start.158
  2834.2 7.4 collective-permute-start.160
  2842.7 7.6 collective-permute-start.162
  2864.7 9.0 all-to-all-start.15
  2868.9 353.4 %all-reduce.135.cloned.1.call-start = ((), (), s32[]{:S(2)}) async-start(), calls=%async_computation.16 | async-start | bytes 2621440 | tf_op jit(solution)/shard_map/psum | solution.py:326
  2920.8 11.7 collective-permute-start.166
  2923.9 8.5 collective-permute-start.167
  2982.2 7.6 collective-permute-start.168
  3092.7 8.8 collective-permute-start.173
  (789 other events, 8130.3 us)
Sparse Core Ops, SparseCore 0:
  3091.2 130.5 all-reduce.134
where the time goes:
time: 3270 us; the launch traced here: 3250 us
  local copies, waits for them, and re-layouts  884 us (27%)
  other arithmetic  683 us (21%)
  blocking collectives  557 us (17%)
  starting transfers between devices  495 us (15%)
  matrix products  375 us (11%)
  waiting for transfers between devices  218 us (7%)
  between operations  37.3 us (1%)
    ppermute x87, starting transfers between devices, with_halo(): lax.ppermute(tail, axis, [(i, (i + 1) % count) for i in range(ends)])  343 us
    unnamed x1467, local copies, waits for them, and re-layouts  295 us
    psum x20, blocking collectives, layer_forward(): lax.psum((jnp.sum(grouped, axis=(2, 3, 4)), jnp.sum(grouped * grouped, ax...  207 us
    psum x20, blocking collectives, layer_backward(): lax.psum((jnp.sum(x_bar, axis=(2, 3, 4)), jnp.sum(x_bar * x_hat, axis=(2,...  204 us
    ppermute x87, waiting for transfers between devices, with_halo(): lax.ppermute(head, axis, [((i + 1) % count, i) for i in range(ends)])  150 us
    conv_general_dilated x19, matrix products, layer_backward(): lax.conv_general_dilated(beside_all, flipped, (1, 1), 'VALID', dimension_...  147 us
    ppermute x87, starting transfers between devices, with_halo(): lax.ppermute(head, axis, [((i + 1) % count, i) for i in range(ends)])  113 us
    convert_element_type x20, other arithmetic, layer_backward(): z_low = z_bar.reshape(scaled.shape).astype(jnp.bfloat16)  104 us
  transfers between devices with their start and end apart: 184, of which 92 were waited for; matrix products, arithmetic and copies ran while one was open for 12% of the time, Pallas kernels for 0%

commit v1 on v0

v1 whole, which is shorter than its diff:
```python
import functools

import jax
import jax.numpy as jnp
from jax import lax
from jax.experimental import pallas as pl
from jax.experimental.pallas import tpu as pltpu
from jax.sharding import PartitionSpec as P

CH = 64
GROUPS = 8
LAYERS = 4
STEPS = 4
JACOBI = 4
STEP_NUM = 10
LANES = 128
EDGE = 8

EPS_NORM = 1e-05
DT_FORCE = 0.5
DT_ADV = 0.2
CLIP_NORM = 0.001
BETA_ONE = 0.9
BETA_TWO = 0.95
ADAM_EPS = 1e-08
DECAY = 0.01
RATES = (0.2, 0.05, 1.0, 0.15)

BF = jnp.bfloat16
F32 = jnp.float32
MESH = pl.DeviceIdType.MESH
FULL_SLOT = {0: 0, 1: 1, 4: 2}
HALF_SLOT = {2: 0, 3: 1}


def nt_dot(a, b):
    return lax.dot_general(a, b, (((1,), (1,)), ((), ())), preferred_element_type=F32)


def nn_dot(a, b):
    return jnp.dot(a, b, preferred_element_type=F32)


def beside(rows):
    return jnp.concatenate(rows, axis=1)


def lane_of(shape):
    return lax.broadcasted_iota(jnp.int32, shape, len(shape) - 1)


def from_left(x, by):
    return jnp.where(lane_of(x.shape) < by, 0.0, pltpu.roll(x, by, x.ndim - 1))


def from_right(x, by):
    return jnp.where(
        lane_of(x.shape) >= LANES - by, 0.0, pltpu.roll(x, LANES - by, x.ndim - 1)
    )


def pair_sum(x):
    even = lane_of(x.shape) % 2 == 0
    last = x.ndim - 1
    return x + jnp.where(even, pltpu.roll(x, LANES - 1, last), pltpu.roll(x, 1, last))


def drows(x):
    count = x.shape[0]
    return 0.5 * (pltpu.roll(x, count - 1, 0) - pltpu.roll(x, 1, 0))


def dcols(x):
    return 0.5 * (from_right(x, 1) - from_left(x, 1))


def nsum(x):
    count = x.shape[0]
    return (
        pltpu.roll(x, count - 1, 0) + pltpu.roll(x, 1, 0) + from_right(x, 1) + from_left(x, 1)
    )


def project(vr, vc, grid):
    div = grid * (drows(vr) + dcols(vc))
    press = -0.25 * div
    for sweep in range(JACOBI - 1):
        press = grid * (0.25 * (nsum(press) - div))
    return vr - drows(press), vc - dcols(press)


def sublanes(x):
    return jnp.sum(x.reshape(x.shape[0] // 8, 8, LANES), axis=0)


def group_rows(x):
    return jnp.sum(x.reshape(GROUPS, CH // GROUPS, LANES), axis=1)


def spread(x):
    return jnp.concatenate(
        [jnp.broadcast_to(x[g : g + 1], (CH // GROUPS, LANES)) for g in range(GROUPS)], axis=0
    )


def train_kernel(
    ranks,
    vel,
    tgt,
    meta,
    wf,
    wb,
    w0f,
    w0b,
    norms,
    headf,
    headb,
    bias,
    gw,
    gw0,
    gnorm,
    ghead,
    misc,
    u_ext,
    t_own,
    m_own,
    opened,
    grid_mask,
    s0,
    s0b,
    q_ext,
    u_kept,
    w_ext,
    u_bar,
    frows,
    taps,
    h1,
    skip,
    pooled,
    h3,
    h4,
    xh_full,
    xh_half,
    inv_kept,
    zbuf,
    skip_bar,
    half_bar,
    sg,
    sgh,
    edges,
    g_halo,
    coef,
    acc,
    st_send,
    st_recv,
    in_send,
    in_recv,
    in_local,
    halo_send,
    halo_recv,
    st_ss,
    st_rs,
):
    quarter = ranks // 4
    parts = ranks // 2
    tile = vel.shape[2]
    rows = 2 * tile
    half = rows // 2
    batch_at = lax.axis_index("batch")
    row_at = lax.axis_index("rows")
    core = lax.rem(batch_at, 2)
    plane = batch_at - core
    sample = row_at // quarter
    part = 2 * lax.rem(row_at, quarter) + core

    def owner(which, piece):
        return (plane + lax.rem(piece, 2), which * quarter + piece // 2)

    u_ext[...] = jnp.zeros_like(u_ext)
    q_ext[...] = jnp.zeros_like(q_ext)
    w_ext[...] = jnp.zeros_like(w_ext)
    g_halo[...] = jnp.zeros_like(g_halo)
    for kept, count in ((h1, rows), (skip, rows), (pooled, half), (h3, half), (h4, half)):
        for t in range(STEPS):
            kept[t, 0] = jnp.zeros((CH, LANES), BF)
            kept[t, count + 1] = jnp.zeros((CH, LANES), BF)

    barrier = pltpu.get_barrier_semaphore()
    members = 2 * ranks
    mine = core * ranks + row_at

    def greet(d, carry):
        other = lax.rem(mine + d, members)
        pl.semaphore_signal(
            barrier,
            inc=1,
            device_id=(plane + other // ranks, lax.rem(other, ranks)),
            device_id_type=MESH,
        )
        return carry

    lax.fori_loop(1, members, greet, 0)
    pl.semaphore_wait(barrier, members - 1)

    def incoming(place):
        at = pl.ds(pl.multiple_of(EDGE + place * tile, 8), tile)
        here = pl.ds(pl.multiple_of(place * tile, 8), tile)
        return u_ext.at[:, at, :], t_own.at[:, :, here, :], m_own.at[place]

    place = lax.rem(row_at, 2)
    for j in range(2):
        to_batch, to_row = owner(2 * core + j, row_at // 2)
        stays = (to_batch == batch_at) & (to_row == row_at)
        for k, (src, dst) in enumerate(zip((vel.at[j], tgt.at[j], meta.at[j]), incoming(place))):

            @pl.when(stays)
            def _():
                pltpu.make_async_copy(src, dst, in_local.at[k]).start()

            @pl.when(jnp.logical_not(stays))
            def _():
                pltpu.make_async_remote_copy(
                    src_ref=src,
                    dst_ref=dst,
                    send_sem=in_send.at[j, k],
                    recv_sem=in_recv.at[place, k],
                    device_id=(to_batch, to_row),
                    device_id_type=MESH,
                ).start()

    for j in range(2):
        to_batch, to_row = owner(2 * core + j, row_at // 2)
        stays = (to_batch == batch_at) & (to_row == row_at)
        for k, src in enumerate((vel.at[j], tgt.at[j], meta.at[j])):

            @pl.when(stays)
            def _():
                pltpu.make_async_copy(src, src, in_local.at[k]).wait()

            @pl.when(jnp.logical_not(stays))
            def _():
                pltpu.make_async_copy(src, src, in_send.at[j, k]).wait()

    for i in range(2):
        from_batch = plane + sample // 2
        from_row = 2 * part + i
        stays = (from_batch == batch_at) & (from_row == row_at)
        for k, dst in enumerate(incoming(i)):

            @pl.when(jnp.logical_not(stays))
            def _():
                pltpu.make_async_copy(dst, dst, in_recv.at[i, k]).wait()

    has_prev = part > 0
    has_next = part < parts - 1
    prev_id = owner(sample, jnp.maximum(part - 1, 0))
    next_id = owner(sample, jnp.minimum(part + 1, parts - 1))

    def halo_copies(slot, low_src, high_src, top_dst, bottom_dst):
        to_prev = pltpu.make_async_remote_copy(
            src_ref=low_src,
            dst_ref=bottom_dst,
            send_sem=halo_send.at[slot, 0],
            recv_sem=halo_recv.at[slot, 0],
            device_id=prev_id,
            device_id_type=MESH,
        )
        to_next = pltpu.make_async_remote_copy(
            src_ref=high_src,
            dst_ref=top_dst,
            send_sem=halo_send.at[slot, 1],
            recv_sem=halo_recv.at[slot, 1],
            device_id=next_id,
            device_id_type=MESH,
        )
        return to_prev, to_next

    def halo_start(*args):
        to_prev, to_next = halo_copies(*args)

        @pl.when(has_prev)
        def _():
            to_prev.start()

        @pl.when(has_next)
        def _():
            to_next.start()

    def halo_wait(*args):
        to_prev, to_next = halo_copies(*args)

        @pl.when(has_prev)
        def _():
            to_prev.wait_send()
            to_next.wait_recv()

        @pl.when(has_next)
        def _():
            to_next.wait_send()
            to_prev.wait_recv()

    def ext_halo(slot, ref):
        args = (
            slot,
            ref.at[:, pl.ds(EDGE, EDGE), :],
            ref.at[:, pl.ds(rows, EDGE), :],
            ref.at[:, pl.ds(0, EDGE), :],
            ref.at[:, pl.ds(rows + EDGE, EDGE), :],
        )
        halo_start(*args)
        halo_wait(*args)

    def group_totals(slot, first, second):
        local = jnp.concatenate([group_rows(first), group_rows(second)], axis=0)
        st_send[slot] = local
        copies = []
        for d in range(1, parts):
            copies.append(
                pltpu.make_async_remote_copy(
                    src_ref=st_send.at[slot],
                    dst_ref=st_recv.at[slot, d - 1],
                    send_sem=st_ss.at[slot, d - 1],
                    recv_sem=st_rs.at[slot, d - 1],
                    device_id=owner(sample, lax.rem(part + d, parts)),
                    device_id_type=MESH,
                )
            )
        for copy in copies:
            copy.start()
        total = local
        for d, copy in enumerate(copies):
            copy.wait()
            total = total + st_recv[slot, d]
        total = jnp.broadcast_to(jnp.sum(total, axis=1, keepdims=True), total.shape)
        return total[:GROUPS], total[GROUPS:]

    ext = rows + 2 * EDGE
    row_is = lax.broadcasted_iota(jnp.int32, (ext, LANES), 0) - EDGE + part * rows
    inside_grid = ((row_is >= 0) & (row_is < parts * rows)).astype(F32)
    row_f = row_is.astype(F32)
    col_f = lane_of((ext, LANES)).astype(F32)
    covered = jnp.zeros((ext, LANES), F32)
    facts = m_own[0]
    for b in range(2):
        bounds = [facts[2 + 4 * b + k : 3 + 4 * b + k] for k in range(4)]
        inside = (
            (row_f >= bounds[0])
            & (row_f < bounds[1])
            & (col_f >= bounds[2])
            & (col_f < bounds[3])
        )
        covered = jnp.maximum(covered, inside.astype(F32))
    grid_mask[...] = inside_grid
    opened[...] = inside_grid * (1.0 - covered)
    own = pl.ds(EDGE, rows)
    misc[...] = jnp.zeros_like(misc)
    live_slots = (facts[0:1] > 0.5).astype(F32) + (facts[1:2] > 0.5).astype(F32)
    misc[1] = sublanes(opened[own, :] * live_slots)
    gw[...] = jnp.zeros_like(gw)
    gw0[...] = jnp.zeros_like(gw0)
    gnorm[...] = jnp.zeros_like(gnorm)
    ghead[...] = jnp.zeros_like(ghead)
    s0[...] = jnp.zeros_like(s0)
    frows[...] = jnp.zeros_like(frows)
    u_bar[...] = jnp.zeros_like(u_bar)

    ext_halo(10, u_ext)

    for kx in range(3):
        field = opened[...]
        s0[:, 3 * kx + 2, :] = (from_left(field, 1), field, from_right(field, 1))[kx]

    def put_shifted(dst, at, x, by, order):
        copies = (from_left(x, by), x, from_right(x, by))
        for place_at, which in enumerate(order):
            dst[at, place_at * CH : (place_at + 1) * CH, :] = copies[which].astype(BF)

    FORWARD = (0, 1, 2)
    BACKWARD = (2, 1, 0)

    def spread_halo(dst, lines, count, by, order):
        for at, line in ((0, lines[0]), (count + 1, lines[1])):
            put_shifted(dst, at, line.astype(F32), by, order)

    def for_blocks(count, size, body):
        size = min(size, count)

        def step(i, carry):
            body(pl.multiple_of(i * size, size), size)
            return carry

        lax.fori_loop(0, count // size, step, 0)

    def channel_blocks():
        return [slice(16 * c, 16 * c + 16) for c in range(CH // 16)]

    def make_norm(layer, t, sums, squares, count):
        size = CH // GROUPS * count * LANES * parts
        mean = sums / size
        inverse = lax.rsqrt(squares / size - mean * mean + EPS_NORM)
        coef[0] = spread(inverse)
        coef[1] = spread(-mean * inverse)
        coef[2] = norms[0, layer]
        coef[3] = norms[1, layer]
        inv_kept[t, layer] = coef[0]

    def activate(z, c):
        xhat = z * coef[0, c] + coef[1, c]
        n = xhat * coef[2, c] + coef[3, c]
        return xhat, n * (0.5 * jnp.tanh(0.5 * n) + 0.5)

    def conv_sums(count, size, rows_of):
        size = min(size, count)
        zero = jnp.zeros((CH, LANES), F32)

        def step(i, carry):
            sums, squares = carry
            base = pl.multiple_of(i * size, size)
            for j, z in enumerate(rows_of(base, size)):
                zbuf[base + j] = z
                sums = sums + z
                squares = squares + z * z
            return sums, squares

        return lax.fori_loop(0, count // size, step, (zero, zero))

    def tap_rows(y, j, at):
        return y[at * CH : (at + 1) * CH, j * LANES : (j + 1) * LANES]

    def conv_of(src, layer):
        def rows_of(base, size):
            y = nn_dot(wf[layer], beside([src[base + j] for j in range(size + 2)]))
            return [
                tap_rows(y, j, 0) + tap_rows(y, j + 1, 1) + tap_rows(y, j + 2, 2)
                for j in range(size)
            ]

        return rows_of

    def conv_last(base, size):
        y = nn_dot(wf[4], beside([sg[base + j] for j in range(size + 2)]))
        low = base // 2
        x = nn_dot(wf[3], beside([sgh[low + j] for j in range(size // 2 + 2)]))
        result = []
        for j in range(size):
            z = tap_rows(y, j, 0) + tap_rows(y, j + 1, 1) + tap_rows(y, j + 2, 2)
            for ky in range(3):
                z = z + tap_rows(x, (j + ky - 1) // 2 + 1, ky)
            result.append(z)
        return result

    def finish_plain(t, layer, count, kept, xh, xh_at, dst, by, slot):
        def edge(which, line):
            xhat, h = activate(zbuf[line], slice(0, CH))
            edges[slot, which] = h.astype(BF)

        edge(0, 0)
        edge(1, count - 1)
        args = (slot, edges.at[slot, 0], edges.at[slot, 1], kept.at[t, 0], kept.at[t, count + 1])
        halo_start(*args)

        def block(base, size):
            for c in channel_blocks():
                xhat, h = activate(zbuf[pl.ds(base, size), c, :], c)
                xh[xh_at, t, pl.ds(base, size), c, :] = xhat.astype(BF)
                low = h.astype(BF)
                kept[t, pl.ds(base + 1, size), c, :] = low
                at = pl.ds(base + 1, size)
                dst[at, c, :] = from_left(h, by).astype(BF)
                dst[at, slice(CH + c.start, CH + c.stop), :] = low
                dst[at, slice(2 * CH + c.start, 2 * CH + c.stop), :] = from_right(h, by).astype(BF)

        for_blocks(count, 8, block)
        halo_wait(*args)
        spread_halo(dst, (kept[t, 0], kept[t, count + 1]), count, by, FORWARD)

    def pool_of(first, second):
        pair = first.astype(BF).astype(F32) + second.astype(BF).astype(F32)
        return 0.25 * pair_sum(pair)

    def finish_skip(t):
        def edge(which, line):
            xhat, first = activate(zbuf[line], slice(0, CH))
            xhat, second = activate(zbuf[line + 1], slice(0, CH))
            edges[1, which] = (first, second)[which].astype(BF)
            edges[2, which] = pool_of(first, second).astype(BF)

        edge(0, 0)
        edge(1, rows - 2)
        skip_args = (1, edges.at[1, 0], edges.at[1, 1], skip.at[t, 0], skip.at[t, rows + 1])
        pool_args = (2, edges.at[2, 0], edges.at[2, 1], pooled.at[t, 0], pooled.at[t, half + 1])
        halo_start(*pool_args)
        halo_start(*skip_args)

        def block(base, size):
            for c in channel_blocks():
                xhat, h = activate(zbuf[pl.ds(base, size), c, :], c)
                xh_full[1, t, pl.ds(base, size), c, :] = xhat.astype(BF)
                low = h.astype(BF)
                at = pl.ds(base + 1, size)
                skip[t, at, c, :] = low
                sg[at, c, :] = from_left(h, 1).astype(BF)
                sg[at, slice(CH + c.start, CH + c.stop), :] = low
                sg[at, slice(2 * CH + c.start, 2 * CH + c.stop), :] = from_right(h, 1).astype(BF)
                pairs = low.astype(F32).reshape(size // 2, 2, 16, LANES)
                mean = 0.25 * pair_sum(pairs[:, 0] + pairs[:, 1])
                at = pl.ds(base // 2 + 1, size // 2)
                small = mean.astype(BF)
                pooled[t, at, c, :] = small
                sgh[at, c, :] = from_left(mean, 2).astype(BF)
                sgh[at, slice(CH + c.start, CH + c.stop), :] = small
                sgh[at, slice(2 * CH + c.start, 2 * CH + c.stop), :] = from_right(mean, 2).astype(BF)

        for_blocks(rows, 8, block)
        halo_wait(*pool_args)
        halo_wait(*skip_args)
        spread_halo(sgh, (pooled[t, 0], pooled[t, half + 1]), half, 2, FORWARD)
        spread_halo(sg, (skip[t, 0], skip[t, rows + 1]), rows, 1, FORWARD)

    def finish_last(t):
        def block(base, size):
            lows = []
            for c in channel_blocks():
                xhat, h = activate(zbuf[pl.ds(base, size), c, :], c)
                xh_full[2, t, pl.ds(base, size), c, :] = xhat.astype(BF)
                lows.append(h.astype(BF))
            low = jnp.concatenate(lows, axis=1)
            force = nn_dot(headf[...], beside([low[j] for j in range(size)]))
            for j in range(size):
                frows[base + j] = force[:, j * LANES : (j + 1) * LANES]

        for_blocks(rows, 8, block)

    def forward_step(t, carry):
        for c in range(2):
            field = u_ext[c]
            for kx, moved in enumerate((from_left(field, 1), field, from_right(field, 1))):
                s0[:, 3 * kx + c, :] = moved
        s0b[t] = s0[...].astype(BF)

        def first_rows(base, size):
            x = beside(
                [s0b[t, pl.ds(base + EDGE - 1 + j, 3)].reshape(48, LANES) for j in range(size)]
            )
            z = nn_dot(w0f[...], x)
            return [z[:, j * LANES : (j + 1) * LANES] for j in range(size)]

        make_norm(0, t, *group_totals(0, *conv_sums(rows, 16, first_rows)), rows)
        finish_plain(t, 0, rows, h1, xh_full, 0, sg, 1, 0)
        make_norm(1, t, *group_totals(1, *conv_sums(rows, 16, conv_of(sg, 0))), rows)
        finish_skip(t)
        make_norm(2, t, *group_totals(2, *conv_sums(half, 16, conv_of(sgh, 1))), half)
        finish_plain(t, 2, half, h3, xh_half, 0, sgh, 2, 3)
        make_norm(3, t, *group_totals(3, *conv_sums(half, 16, conv_of(sgh, 2))), half)
        finish_plain(t, 3, half, h4, xh_half, 1, sgh, 1, 4)
        make_norm(4, t, *group_totals(4, *conv_sums(rows, 16, conv_last)), rows)
        finish_last(t)

        for c in range(2):
            force = frows[:, c, :] + bias[c]
            q_ext[t, c, own, :] = (u_ext[c, own, :] + DT_FORCE * force) * opened[own, :]
        ext_halo(11, q_ext.at[t])
        qr, qc = q_ext[t, 0], q_ext[t, 1]
        grid = grid_mask[...]
        vr = grid * (qr - DT_ADV * (qr * drows(qr) + qc * dcols(qr)))
        vc = grid * (qc - DT_ADV * (qr * drows(qc) + qc * dcols(qc)))
        facts = m_own[0]
        at = (t + 1).astype(F32)
        for c, moved in enumerate(project(vr, vc, grid)):
            u_ext[c] = opened[...] * moved
            u_now = u_ext[c, own, :]
            u_kept[t, c] = u_now
            for k in range(2):
                live = (facts[k : k + 1] == at).astype(F32)
                miss = u_now - t_own[k, c]
                misc[0] += sublanes(live * opened[own, :] * miss * miss)
        return carry

    lax.fori_loop(0, STEPS, forward_step, 0)

    def bar_block(layer, xh, xh_at, t, base, size, c, h_bar):
        xhat = xh[xh_at, t, pl.ds(base, size), c, :].astype(F32)
        n = xhat * norms[0, layer, c] + norms[1, layer, c]
        sig = 0.5 * jnp.tanh(0.5 * n) + 0.5
        n_bar = h_bar * (sig * (1.0 + n * (1.0 - sig)))
        zbuf[pl.ds(base, size), c, :] = n_bar
        acc[0, c, :] += jnp.sum(n_bar, axis=0)
        acc[1, c, :] += jnp.sum(n_bar * xhat, axis=0)
        return n * sig

    def first_pass(layer, t, count, xh, xh_at, h_bar_of):
        acc[...] = jnp.zeros_like(acc)

        def block(base, size):
            for c in channel_blocks():
                bar_block(layer, xh, xh_at, t, base, size, c, h_bar_of(base, size, c))

        for_blocks(count, 8, block)

    def first_pass_last(t):
        acc[...] = jnp.zeros_like(acc)

        def block(base, size):
            low = beside([frows[base + j].astype(BF) for j in range(size)])
            h_bar = nn_dot(headb[...], low)
            lows = []
            for c in channel_blocks():
                bar = jnp.stack(
                    [h_bar[c, j * LANES : (j + 1) * LANES] for j in range(size)], axis=0
                )
                h = bar_block(4, xh_full, 2, t, base, size, c, bar)
                lows.append(h.astype(BF))
            h = jnp.concatenate(lows, axis=1)
            ghead[...] += nt_dot(low, beside([h[j] for j in range(size)]))

        for_blocks(rows, 8, block)

    def second_pass(layer, t, count, xh, xh_at, dst, by):
        gain = norms[0, layer]
        sums, cross = acc[0], acc[1]
        gnorm[0, layer] += cross
        gnorm[1, layer] += sums
        size_all = CH // GROUPS * count * LANES * parts
        total, total_cross = group_totals(5 + layer, gain * sums, gain * cross)
        inverse = inv_kept[t, layer]
        coef[0] = gain * inverse
        coef[1] = -inverse * spread(total_cross / size_all)
        coef[2] = -inverse * spread(total / size_all)

        def z_bar(at, c):
            xhat = xh[xh_at, t, at, c, :].astype(F32)
            return zbuf[at, c, :] * coef[0, c] + xhat * coef[1, c] + coef[2, c]

        slot = 5 + layer
        for which, line in enumerate((0, count - 1)):
            edges[slot, which] = z_bar(line, slice(0, CH)).astype(BF)
        args = (
            slot,
            edges.at[slot, 0],
            edges.at[slot, 1],
            g_halo.at[layer, 0],
            g_halo.at[layer, 1],
        )
        halo_start(*args)

        def block(base, size):
            at = pl.ds(base + 1, size)
            for c in channel_blocks():
                z = z_bar(pl.ds(base, size), c)
                dst[at, slice(CH + c.start, CH + c.stop), :] = z.astype(BF)
                if by:
                    dst[at, c, :] = from_right(z, by).astype(BF)
                    right = slice(2 * CH + c.start, 2 * CH + c.stop)
                    dst[at, right, :] = from_left(z, by).astype(BF)

        for_blocks(count, 8, block)
        halo_wait(*args)
        if by:
            spread_halo(dst, (g_halo[layer, 0], g_halo[layer, 1]), count, by, BACKWARD)
        else:
            dst[0, CH : 2 * CH, :] = g_halo[layer, 0]
            dst[count + 1, CH : 2 * CH, :] = g_halo[layer, 1]

    def bar_rows(weight, g, size):
        y = nn_dot(weight, g)
        return [
            tap_rows(y, j + 2, 0) + tap_rows(y, j + 1, 1) + tap_rows(y, j, 2) for j in range(size)
        ]

    def products(t, layer, count, src, kept, out):
        def block(base, size):
            g = beside([src[base + j] for j in range(size + 2)])
            for j, bar in enumerate(bar_rows(wb[layer], g, size)):
                out[base + j] = bar
            h = beside([kept[t, pl.ds(base + j, 3)].reshape(3 * CH, LANES) for j in range(size)])
            gw[layer] += nt_dot(g[:, LANES : (size + 1) * LANES], h)

        for_blocks(count, 16, block)

    def products_last(t):
        def block(base, size):
            g = beside([sg[base + j] for j in range(size + 2)])
            inner = g[:, LANES : (size + 1) * LANES]
            low = base // 2
            for j, bar in enumerate(bar_rows(wb[4], g, size)):
                skip_bar[base + j] = bar
            ups = bar_rows(wb[3], g, size)
            for j in range(size // 2):
                half_bar[low + j] = pair_sum(ups[2 * j] + ups[2 * j + 1])
            h = beside([skip[t, pl.ds(base + j, 3)].reshape(3 * CH, LANES) for j in range(size)])
            gw[4] += nt_dot(inner, h)
            up = beside(
                [
                    jnp.concatenate([h4[t, low + (j + ky - 1) // 2 + 1] for ky in range(3)], axis=0)
                    for j in range(size)
                ]
            )
            gw[3] += nt_dot(inner, up)

        for_blocks(rows, 16, block)

    def products_first(t):
        def block(base, size):
            g = beside([sg[base + j, CH : 2 * CH, :] for j in range(size)])
            y = nn_dot(w0b[...], g)
            for j in range(size):
                taps[base + j] = y[:, j * LANES : (j + 1) * LANES]

        for_blocks(rows, 16, block)
        g = beside([sg[rows + j, CH : 2 * CH, :] for j in range(2)])
        y = nn_dot(w0b[...], g)
        for j in range(2):
            taps[rows + j] = y[:, j * LANES : (j + 1) * LANES]

        def weights(base, size):
            g = beside([sg[base + 1 + j, CH : 2 * CH, :] for j in range(size)])
            x = beside(
                [s0b[t, pl.ds(base + EDGE - 1 + j, 3)].reshape(48, LANES) for j in range(size)]
            )
            gw0[...] += nt_dot(g, x)

        for_blocks(rows, 16, weights)

    def backward_step(i, carry):
        t = STEPS - 1 - i
        facts = m_own[0]
        at = (t + 1).astype(F32)
        open_own = opened[own, :]
        for c in range(2):
            pull = jnp.zeros((rows, LANES), F32)
            for k in range(2):
                live = (facts[k : k + 1] == at).astype(F32)
                pull = pull + live * (u_kept[t, c] - t_own[k, c])
            w_ext[c, own, :] = open_own * (u_bar[c] + 2.0 * open_own * pull)
        ext_halo(12, w_ext)
        grid = grid_mask[...]
        gr, gc = project(w_ext[0], w_ext[1], grid)
        gr, gc = grid * gr, grid * gc
        qr, qc = q_ext[t, 0], q_ext[t, 1]
        bar_r = gr + DT_ADV * (
            drows(gr * qr) + dcols(gr * qc) - (gr * drows(qr) + gc * drows(qc))
        )
        bar_c = gc + DT_ADV * (
            drows(gc * qr) + dcols(gc * qc) - (gr * dcols(qr) + gc * dcols(qc))
        )
        for c, bar in enumerate((bar_r, bar_c)):
            passed = opened[...] * bar
            q_ext[t, c] = passed
            passed = q_ext[t, c, own, :]
            u_bar[c] = passed
            force_bar = DT_FORCE * passed
            misc[2 + c] += sublanes(force_bar)
            frows[:, c, :] = force_bar
        for c in range(2, 16):
            frows[:, c, :] = jnp.zeros((rows, LANES), F32)

        first_pass_last(t)
        second_pass(4, t, rows, xh_full, 2, sg, 1)
        products_last(t)
        first_pass(3, t, half, xh_half, 1, lambda b, s, c: half_bar[pl.ds(b, s), c, :])
        second_pass(3, t, half, xh_half, 1, sgh, 2)
        products(t, 2, half, sgh, h3, half_bar)
        first_pass(2, t, half, xh_half, 0, lambda b, s, c: half_bar[pl.ds(b, s), c, :])
        second_pass(2, t, half, xh_half, 0, sgh, 2)
        products(t, 1, half, sgh, pooled, half_bar)

        def skip_total(base, size, c):
            bars = skip_bar[pl.ds(base, size), c, :].reshape(size // 2, 2, 16, LANES)
            small = half_bar[pl.ds(base // 2, size // 2), c, :]
            return (bars + 0.25 * small[:, None]).reshape(size, 16, LANES)

        first_pass(1, t, rows, xh_full, 1, skip_total)
        second_pass(1, t, rows, xh_full, 1, sg, 1)
        products(t, 0, rows, sg, h1, skip_bar)
        first_pass(0, t, rows, xh_full, 0, lambda b, s, c: skip_bar[pl.ds(b, s), c, :])
        second_pass(0, t, rows, xh_full, 0, sg, 0)
        products_first(t)
        for c in range(2):
            columns = []
            for kx in range(3):
                total = jnp.zeros((rows, LANES), F32)
                for ky in range(3):
                    total = total + taps[pl.ds(2 - ky, rows), 16 * ky + 3 * kx + c, :]
                columns.append(total)
            u_bar[c] += from_right(columns[0], 1) + columns[1] + from_left(columns[2], 1)
        return carry

    lax.fori_loop(0, STEPS, backward_step, 0)


def train(velocity, targets, meta, wf, wb, w0f, w0b, norms, headf, headb, bias):
    ranks = lax.axis_size("rows")
    parts = ranks // 2
    tile = velocity.shape[2]
    rows, half, ext = 2 * tile, tile, 2 * tile + 2 * EDGE
    vmem = pl.BlockSpec(memory_space=pltpu.VMEM)

    def kept(count):
        return pltpu.VMEM((STEPS, count + 2, CH, LANES), BF)

    args = (velocity, targets, meta, wf, wb, w0f, w0b, norms, headf, headb, bias)
    return pl.pallas_call(
        functools.partial(train_kernel, ranks),
        out_shape=(
            jax.ShapeDtypeStruct((LAYERS + 1, 3 * CH, 3 * CH), F32),
            jax.ShapeDtypeStruct((CH, 48), F32),
            jax.ShapeDtypeStruct((2, LAYERS + 1, CH, LANES), F32),
            jax.ShapeDtypeStruct((16, CH), F32),
            jax.ShapeDtypeStruct((4, 8, LANES), F32),
        ),
        in_specs=[vmem] * len(args),
        out_specs=(vmem,) * 5,
        scratch_shapes=[
            pltpu.VMEM((2, ext, LANES), F32),
            pltpu.VMEM((2, 2, rows, LANES), F32),
            pltpu.VMEM((2, 16, LANES), F32),
            pltpu.VMEM((ext, LANES), F32),
            pltpu.VMEM((ext, LANES), F32),
            pltpu.VMEM((ext, 16, LANES), F32),
            pltpu.VMEM((STEPS, ext, 16, LANES), BF),
            pltpu.VMEM((STEPS, 2, ext, LANES), F32),
            pltpu.VMEM((STEPS, 2, rows, LANES), F32),
            pltpu.VMEM((2, ext, LANES), F32),
            pltpu.VMEM((2, rows, LANES), F32),
            pltpu.VMEM((rows, 16, LANES), F32),
            pltpu.VMEM((rows + 2, 48, LANES), F32),
            kept(rows),
            kept(rows),
            kept(half),
            kept(half),
            kept(half),
            pltpu.VMEM((3, STEPS, rows, CH, LANES), BF),
            pltpu.VMEM((2, STEPS, half, CH, LANES), BF),
            pltpu.VMEM((STEPS, LAYERS + 1, CH, LANES), F32),
            pltpu.VMEM((rows, CH, LANES), F32),
            pltpu.VMEM((rows, CH, LANES), F32),
            pltpu.VMEM((half, CH, LANES), F32),
            pltpu.VMEM((rows + 2, 3 * CH, LANES), BF),
            pltpu.VMEM((half + 2, 3 * CH, LANES), BF),
            pltpu.VMEM((10, 2, CH, LANES), BF),
            pltpu.VMEM((LAYERS + 1, 2, CH, LANES), BF),
            pltpu.VMEM((4, CH, LANES), F32),
            pltpu.VMEM((2, CH, LANES), F32),
            pltpu.VMEM((10, 16, LANES), F32),
            pltpu.VMEM((10, parts - 1, 16, LANES), F32),
            pltpu.SemaphoreType.DMA((2, 3)),
            pltpu.SemaphoreType.DMA((2, 3)),
            pltpu.SemaphoreType.DMA((3,)),
            pltpu.SemaphoreType.DMA((13, 2)),
            pltpu.SemaphoreType.DMA((13, 2)),
            pltpu.SemaphoreType.DMA((10, parts - 1)),
            pltpu.SemaphoreType.DMA((10, parts - 1)),
        ],
        compiler_params=pltpu.CompilerParams(
            collective_id=0, has_side_effects=True, vmem_limit_bytes=60 * 2**20
        ),
        name="train",
    )(*args)


def shards(
    velocity,
    targets,
    keyframes,
    boxes,
    w_in,
    w_mid,
    norm_params,
    head_params,
    m_in,
    m_mid,
    m_norm,
    m_head,
    v_in,
    v_mid,
    v_norm,
    v_head,
):
    samples = velocity.shape[0]
    facts = jnp.concatenate(
        [keyframes, boxes.reshape(samples, 8), jnp.zeros((samples, 6), jnp.int32)], axis=1
    ).astype(F32)
    meta = jnp.broadcast_to(facts[:, :, None], (samples, 16, LANES))
    mid = w_mid.reshape(LAYERS + 1, 3, 3, CH, CH)
    wf = jnp.transpose(mid, (0, 1, 3, 2, 4)).reshape(LAYERS + 1, 3 * CH, 3 * CH).astype(BF)
    wb = jnp.transpose(mid, (0, 1, 4, 2, 3)).reshape(LAYERS + 1, 3 * CH, 3 * CH).astype(BF)
    first = jnp.transpose(w_in, (0, 2, 3, 1)).reshape(CH, 3, 9)
    w0f = jnp.pad(first, ((0, 0), (0, 0), (0, 7))).reshape(CH, 48).astype(BF)
    norms = jnp.broadcast_to(norm_params[..., None], norm_params.shape + (LANES,))
    headf = jnp.pad(head_params[:, :CH], ((0, 14), (0, 0))).astype(BF)
    bias = jnp.broadcast_to(head_params[:, CH:, None], (2, 1, LANES))
    gw, gw0, gnorm, ghead, misc = train(
        velocity, targets, meta, wf, wb, w0f, w0f.T, norms, headf, headf.T, bias
    )
    halves = jnp.array([1.0, 0.5, 0.5, 1.0, 1.0], F32)
    g_mid = jnp.transpose(
        gw.reshape(LAYERS + 1, 3, CH, 3, CH) * halves[:, None, None, None, None], (0, 3, 1, 2, 4)
    ).reshape(w_mid.shape)
    g_in = jnp.transpose(gw0.reshape(CH, 3, 16)[:, :, :9].reshape(CH, 3, 3, 3), (0, 3, 1, 2))
    layer_halves = jnp.array([1.0, 1.0, 0.5, 0.5, 1.0], F32)
    g_norm = jnp.sum(gnorm, axis=-1) * layer_halves[None, :, None]
    sums = jnp.sum(misc, axis=(1, 2))
    g_head = jnp.concatenate([ghead[:2], sums[2:4, None]], axis=1)
    grads_in, grads_mid, grads_norm, grads_head, totals = lax.psum(
        (g_in, g_mid, g_norm, g_head, sums[:2]), ("batch", "rows")
    )
    loss_sum, count = totals[0], totals[1]
    grads = tuple(g / count for g in (grads_in, grads_mid, grads_norm, grads_head))
    params = (w_in, w_mid, norm_params, head_params)
    norm = jnp.sqrt(sum((jnp.sum(g * g) for g in grads)))
    scale = jnp.minimum(1.0, CLIP_NORM / norm)
    new_w, new_m, new_v = ([], [], [])
    for weight, moment, second, g, rate in zip(
        params, (m_in, m_mid, m_norm, m_head), (v_in, v_mid, v_norm, v_head), grads, RATES
    ):
        g = g * scale
        moment_new = BETA_ONE * moment + (1 - BETA_ONE) * g
        second_new = BETA_TWO * second + (1 - BETA_TWO) * g * g
        mhat = moment_new / (1 - BETA_ONE**STEP_NUM)
        vhat = second_new / (1 - BETA_TWO**STEP_NUM)
        new_w.append(weight - rate * (mhat / (jnp.sqrt(vhat) + ADAM_EPS) + DECAY * weight))
        new_m.append(moment_new)
        new_v.append(second_new)
    return (
        *new_w,
        *new_m,
        *new_v,
        new_w[0].astype(BF),
        new_w[1].astype(BF),
        new_w[3].astype(BF),
        loss_sum,
        count,
        norm,
    )


def solution(mesh):
    return jax.shard_map(
        shards,
        mesh=mesh,
        in_specs=(
            P("batch", None, "rows", None),
            P("batch", None, None, "rows", None),
            P("batch", None),
            P("batch", None, None),
        )
        + (P(),) * 12,
        out_specs=(P(),) * 18,
        check_vma=False,
    )
```

time: 3270 us -> 396 us (0.12)
  local copies, waits for them, and re-layouts: 884 us -> 24.7 us
  other arithmetic: 683 us -> 22.3 us
  blocking collectives: 557 us -> 40.7 us
  starting transfers between devices: 495 us -> 0.04 us
  matrix products: 375 us -> 0 us
  Pallas kernels: 0 us -> 214 us
  waiting for transfers between devices: 218 us -> 75 us
    ppermute x174 -> x0, starting transfers between devices: 455 us -> none  [the longest x87 343 us: with_halo(): lax.ppermute(tail, axis, [(i, (i + 1) % count) for i in range(ends)])]
    psum x42 -> x1, blocking collectives: 493 us -> 40.7 us  [shards(): lax.psum((g_in, g_mid, g_norm, g_head, sums[:2]), ('batch', 'rows'))]
    unnamed x1467 -> x33, local copies, waits for them, and re-layouts: 295 us -> 5.16 us
    conv_general_dilated x39 -> x0, matrix products: 241 us -> none  [the longest x19 147 us: layer_backward(): lax.conv_general_dilated(beside_all, flipped, (1, 1), 'VALID', dimension_...]
    pallas_call x0 -> x1, Pallas kernels: none -> 214 us  [train(): pl.pallas_call(functools.partial(train_kernel, ranks), out_shape=(jax.Sha...]
    ppermute x174 -> x0, waiting for transfers between devices: 192 us -> none  [the longest x87 150 us: with_halo(): lax.ppermute(head, axis, [((i + 1) % count, i) for i in range(ends)])]
    convert_element_type x43 -> x5, other arithmetic: 191 us -> 8.77 us  [the longest x1 4.55 us: shards(): new_w[1].astype(BF)]
    mul x188 -> x0, local copies, waits for them, and re-layouts: 170 us -> none  [the longest x67 70.3 us: layer_forward(): scaled = ((grouped - mean) * inverse).reshape(z.shape)]
  transfers between devices with their start and end apart: 184 -> 1, of which waited for: 92 -> 1; matrix products, arithmetic and copies ran while one was open for 12% -> 4% of each run, Pallas kernels for 0% -> 0%
where the time goes in v1:
time: 396 us; the launch traced here: 395 us
  Pallas kernels  214 us (54%)
  waiting for transfers between devices  75 us (19%)
  blocking collectives  40.7 us (10%)
  local copies, waits for them, and re-layouts  24.7 us (6%)
  other arithmetic  22.3 us (6%)
  between operations  18.1 us (5%)
    pallas_call x1, Pallas kernels, train(): pl.pallas_call(functools.partial(train_kernel, ranks), out_shape=(jax.Sha...  214 us
    psum x1, waiting for transfers between devices, shards(): lax.psum((g_in, g_mid, g_norm, g_head, sums[:2]), ('batch', 'rows'))  75 us
    psum x1, blocking collectives, shards(): lax.psum((g_in, g_mid, g_norm, g_head, sums[:2]), ('batch', 'rows'))  40.7 us
    reduce_sum x4, other arithmetic, shards(): norm = jnp.sqrt(sum((jnp.sum(g * g) for g in grads)))  8.56 us
  transfers between devices with their start and end apart: 1, of which 1 were waited for; matrix products, arithmetic and copies ran while one was open for 4% of the time, Pallas kernels for 0%

profile of v1, /device:TPU:0, one launch (start us, length us, event | category | flops | bytes accessed | tf_op | source)
XLA Modules:
  0.0 395.1 jit_solution(8322408179724407652)
XLA Ops:
  7.2 1.4 convert_element_type.39
  8.6 0.8 convert_element_type.40
  9.4 0.6 copy.133
  10.1 0.8 copy.85
  10.9 0.1 copy.110
  11.0 0.6 pad_bitcast_fusion.headb
  11.6 0.1 copy.127
  11.7 0.2 slice_reduce_fusion
  11.9 1.3 convert_element_type.42.wf
  13.2 1.3 convert_element_type.44.wb
  14.6 0.7 copy.90.w0f
  15.3 0.6 pad.11.clone.headf
  16.1 0.9 broadcast_in_dim.11.norms
  17.0 0.7 broadcast_in_dim.10.meta
  17.7 0.6 broadcast_in_dim.13.bias
  18.3 214.3 %train.1 = (f32[5,192,192]{2,1,0:T(8,128)}, f32[64,48]{1,0:T(8,128)}, f32[2,5,64,128]{3,2,1,0:T(8,128)}, f32[16,64]{1,0:T(8,128)}, f32[4,8,128]{2,1,0:T(8,128)}) custom-call(f32[2,2,32,128]{3,2,1,0:T(8,128)} %vel.1, f32[2,2,2,32,128]{4,3,2,1,0:T(8,128)} %tgt.1, f32[2,16,128]{2,1,0:T(8,128)} %broadcast_in_dim.10.meta, ...), custom_call_target="tpu_custom_call" | custom-call | tf_op jit(solution)/shard_map/train/pallas_call | solution.py:802
  232.6 2.4 reshape.91
  235.1 0.5 multiply_bitcast_fusion
  235.6 0.2 copy.94
  235.8 1.5 reshape.92
  237.3 0.7 copy-done.6
  238.0 0.6 reduce_sum.54
  238.6 1.2 slice_bitcast_fusion
  239.8 0.1 copy.95
  239.9 0.7 slice.30
  240.6 1.4 copy.92
  242.1 1.4 copy.93
  243.4 1.1 reduce_sum.57
  244.6 0.6 pad_maximum_fusion
  245.2 0.7 broadcast_multiply_fusion
  245.9 40.7 %all-reduce.2 = (f32[64,3,3,3]{0,2,1,3:T(4,128)}, f32[2]{0:T(128)}, f32[2,5,64]{2,1,0:T(8,128)S(1)}, f32[2,65]{1,0:T(2,128)}) all-reduce(f32[64,3,3,3]{0,2,1,3:T(4,128)} %bitcast.35, f32[2]{0:T(128)} %get-tuple-element.106, f32[2,5,64]{2,1,0:T(8,128)S(1)} %broadcast_multiply_fusion, ...), channel_id=1, replica_groups=mesh['batch'=8,'rows'=4] {'batch','rows'}, use_global_device_ids=true, to_apply=%region_0.1 | all-reduce | flops 2500 | bytes 20000 | tf_op jit(solution)/shard_map/psum | solution.py:904
  286.6 1.3 fusion.15
  287.9 1.3 multiply_reduce_fusion.2
  289.1 2.0 multiply_reduce_fusion.1
  291.1 2.5 multiply_reduce_fusion.3
  293.6 75.0 %all-reduce.5.cloned.1.call-done = f32[5,9,4096]{2,0,1:T(8,128)} async-done(((f32[5,9,4096]{2,0,1:T(8,128)}), f32[5,9,4096]{2,0,1:T(8,128)}) %all-reduce.5.cloned.1.call-update) | async-done | bytes 737296 | tf_op jit(solution)/shard_map/psum | solution.py:904
  368.6 2.8 multiply_reduce_fusion
  374.2 1.4 add_subtract_fusion
  375.6 0.6 copy.104
  376.2 0.6 copy.106
  376.8 0.6 copy.108
  377.3 1.5 fusion.10
  378.8 0.6 copy.103
  379.4 0.6 copy.105
  380.0 0.6 copy.107
  380.7 0.6 copy.109
  381.3 1.3 fusion.6
  382.6 4.6 %fusion.8 = (bf16[5,9,4096]{2,0,1:T(8,128)(2,1)}, f32[5,9,4096]{2,0,1:T(8,128)}, f32[5,9,4096]{2,0,1:T(8,128)}, f32[5,9,4096]{2,0,1:T(8,128)}) fusion(f32[5,9,4096]{2,0,1:T(8,128)S(1)} %copy-done, f32[]{:T(128)S(6)} %min.3, f32[5,9,4096]{2,0,1:T(8,128)} %all-reduce.5.cloned.1.call-done, f32[]{:T(128)} %bitcast.10, f32[5,9,4096]{2,0,1:T(8,128)S(1)} %copy-done.1, ...), kind=kLoop, calls=%fused_computation.38 | loop fusion | flops 3317760 | bytes 5529608 | tf_op jit(solution)/shard_map/convert_element_type | solution.py:929
  (33 shorter events, 0.4 us)
Async XLA Ops:
  7.2 361.5 %all-reduce.5.cloned.1.call-start = ((), (), s32[]{:S(2)}) async-start(), calls=%async_computation | async-start | bytes 2359296 | tf_op jit(solution)/shard_map/psum | solution.py:904
  10.1 0.8 copy-start.9
  11.9 2.7 copy-start.4
  11.9 4.0 %copy-start.5 = (f32[2,5,64]{2,0,1:T(2,128)S(1)}, f32[2,5,64]{2,0,1:T(2,128)}, u32[]{:S(2)}) copy-start(f32[2,5,64]{2,0,1:T(2,128)} %param.24) | copy-start | bytes 7684
  11.9 4.0 %copy-start.7 = (s32[2,2,4]{2,1,0:T(2,128)S(1)}, s32[2,2,4]{2,1,0:T(2,128)}, u32[]{:S(2)}) copy-start(s32[2,2,4]{2,1,0:T(2,128)} %param.21) | copy-start | bytes 196
  13.2 2.8 copy-start.8
  14.6 3.7 copy-start.3
  232.6 2.4 copy-start.10
  235.8 146.8 %copy-start.2 = (f32[5,9,4096]{2,0,1:T(8,128)S(1)}, f32[5,9,4096]{2,0,1:T(8,128)}, u32[]{:S(2)}) copy-start(f32[5,9,4096]{2,0,1:T(8,128)} %param.31) | copy-start | bytes 2211844
  237.3 0.7 copy-start.6
  237.3 145.3 %copy-start.1 = (f32[5,9,4096]{2,0,1:T(8,128)S(1)}, f32[5,9,4096]{2,0,1:T(8,128)}, u32[]{:S(2)}) copy-start(f32[5,9,4096]{2,0,1:T(8,128)} %param.27) | copy-start | bytes 2211844
  237.3 145.3 %copy-start = (f32[5,9,4096]{2,0,1:T(8,128)S(1)}, f32[5,9,4096]{2,0,1:T(8,128)}, u32[]{:S(2)}) copy-start(f32[5,9,4096]{2,0,1:T(8,128)} %param.23) | copy-start | bytes 2211844
Sparse Core Ops, SparseCore 0:
  237.4 131.1 all-reduce.4

commit v2 on v1

--- a/solution.py
+++ b/solution.py
@@ -105,6 +105,7 @@
 
 def train_kernel(
     ranks,
+    planes,
     vel,
     tgt,
     meta,
@@ -116,6 +117,8 @@
     headf,
     headb,
     bias,
+    g_all,
+    scalars,
     gw,
     gw0,
     gnorm,
@@ -153,6 +156,12 @@
     acc,
     st_send,
     st_recv,
+    g_send,
+    p_recv,
+    z_send,
+    z_recv,
+    m_plane,
+    m_line,
     in_send,
     in_recv,
     in_local,
@@ -160,6 +169,10 @@
     halo_recv,
     st_ss,
     st_rs,
+    p_ss,
+    p_rs,
+    z_ss,
+    z_rs,
 ):
     quarter = ranks // 4
     parts = ranks // 2
@@ -189,18 +202,26 @@
     members = 2 * ranks
     mine = core * ranks + row_at
 
+    def plane_id(d):
+        other = lax.rem(mine + d, members)
+        return (plane + other // ranks, lax.rem(other, ranks))
+
     def greet(d, carry):
-        other = lax.rem(mine + d, members)
-        pl.semaphore_signal(
-            barrier,
-            inc=1,
-            device_id=(plane + other // ranks, lax.rem(other, ranks)),
-            device_id_type=MESH,
-        )
+        pl.semaphore_signal(barrier, inc=1, device_id=plane_id(d), device_id_type=MESH)
         return carry
 
     lax.fori_loop(1, members, greet, 0)
-    pl.semaphore_wait(barrier, members - 1)
+    level = batch_at // 2
+
+    def line_id(d):
+        return (2 * lax.rem(level + d, planes) + core, row_at)
+
+    def greet_line(d, carry):
+        pl.semaphore_signal(barrier, inc=1, device_id=line_id(d), device_id_type=MESH)
+        return carry
+
+    lax.fori_loop(1, planes, greet_line, 0)
+    pl.semaphore_wait(barrier, members + planes - 2)
 
     def incoming(place):
         at = pl.ds(pl.multiple_of(EDGE + place * tile, 8), tile)
@@ -611,7 +632,7 @@
                 h = bar_block(4, xh_full, 2, t, base, size, c, bar)
                 lows.append(h.astype(BF))
             h = jnp.concatenate(lows, axis=1)
-            ghead[...] += nt_dot(low, beside([h[j] for j in range(size)]))
+            ghead[...] += nt_dot(beside([h[j] for j in range(size)]), low)
 
         for_blocks(rows, 8, block)
 
@@ -673,7 +694,9 @@
             for j, bar in enumerate(bar_rows(wb[layer], g, size)):
                 out[base + j] = bar
             h = beside([kept[t, pl.ds(base + j, 3)].reshape(3 * CH, LANES) for j in range(size)])
-            gw[layer] += nt_dot(g[:, LANES : (size + 1) * LANES], h)
+            gw[layer * 3 * CH : (layer + 1) * 3 * CH, :] += nt_dot(
+                g[:, LANES : (size + 1) * LANES], h
+            )
 
         for_blocks(count, 16, block)
 
@@ -688,14 +711,14 @@
             for j in range(size // 2):
                 half_bar[low + j] = pair_sum(ups[2 * j] + ups[2 * j + 1])
             h = beside([skip[t, pl.ds(base + j, 3)].reshape(3 * CH, LANES) for j in range(size)])
-            gw[4] += nt_dot(inner, h)
+            gw[4 * 3 * CH : 5 * 3 * CH, :] += nt_dot(inner, h)
             up = beside(
                 [
                     jnp.concatenate([h4[t, low + (j + ky - 1) // 2 + 1] for ky in range(3)], axis=0)
                     for j in range(size)
                 ]
             )
-            gw[3] += nt_dot(inner, up)
+            gw[3 * 3 * CH : 4 * 3 * CH, :] += nt_dot(inner, up)
 
         for_blocks(rows, 16, block)
 
@@ -787,9 +810,148 @@
 
     lax.fori_loop(0, STEPS, backward_step, 0)
 
+    mid_rows = (LAYERS + 1) * 3 * CH
+    gw[3 * CH : 9 * CH, :] = 0.5 * gw[3 * CH : 9 * CH, :]
+    lane = lane_of((CH, 3 * CH))
+    rest = jnp.concatenate([gw0[...], jnp.zeros((CH, 3 * CH - 48), F32)], axis=1)
+    for which in range(2):
+        for layer in range(LAYERS + 1):
+            column = jnp.sum(gnorm[which, layer], axis=1, keepdims=True)
+            if layer in HALF_SLOT:
+                column = 0.5 * column
+            rest = jnp.where(lane == 48 + 5 * which + layer, column, rest)
+    for c in range(2):
+        rest = jnp.where(lane == 58 + c, ghead[:, c : c + 1], rest)
+    gw[mid_rows : mid_rows + CH, :] = rest
+    g_send[...] = gw[...].astype(BF)
+    chunk = gw.shape[0] // members
+    piece = chunk // planes
+
+    def chunk_at(which):
+        return pl.ds(pl.multiple_of(which * chunk, 16), chunk)
+
+    def piece_at(which):
+        return pl.ds(pl.multiple_of(which * piece, 16), piece)
+
+    def part_at(which):
+        return pl.ds(pl.multiple_of(mine * chunk + which * piece, 16), piece)
+
+    m_plane[mine] = jnp.concatenate(
+        [jnp.sum(misc[k], axis=0, keepdims=True) for k in range(4)] + [jnp.zeros((4, LANES), F32)],
+        axis=0,
+    )
+
+    def plane_copies(d):
+        other = lax.rem(mine + d, members)
+        source = lax.rem(mine + members - d, members)
+        sends = [
+            (g_send.at[chunk_at(other)], p_recv.at[mine], p_ss.at[0, d], p_rs.at[0, mine]),
+            (m_plane.at[mine], m_plane.at[mine], p_ss.at[1, d], p_rs.at[1, mine]),
+        ]
+        lands = [
+            (p_recv.at[source], p_rs.at[0, source]),
+            (m_plane.at[source], p_rs.at[1, source]),
+        ]
+        return plane_id(d), sends, lands
+
+    def line_copies(d):
+        other = lax.rem(level + d, planes)
+        source = lax.rem(level + planes - d, planes)
+        sends = [
+            (z_send.at[piece_at(other)], z_recv.at[level], z_ss.at[0, d], z_rs.at[0, level]),
+            (m_line.at[level], m_line.at[level], z_ss.at[1, d], z_rs.at[1, level]),
+        ]
+        lands = [
+            (z_recv.at[source], z_rs.at[0, source]),
+            (m_line.at[source], z_rs.at[1, source]),
+        ]
+        return line_id(d), sends, lands
+
+    def line_gather(d):
+        source = lax.rem(level + planes - d, planes)
+        sends = [(g_all.at[part_at(level)], g_all.at[part_at(level)], z_ss.at[2, d], z_rs.at[2, level])]
+        lands = [(g_all.at[part_at(source)], z_rs.at[2, source])]
+        return line_id(d), sends, lands
+
+    def plane_gather(d):
+        source = lax.rem(mine + members - d, members)
+        sends = [(g_all.at[chunk_at(mine)], g_all.at[chunk_at(mine)], p_ss.at[2, d], p_rs.at[2, mine])]
+        lands = [(g_all.at[chunk_at(source)], p_rs.at[2, source])]
+        return plane_id(d), sends, lands
+
+    def exchange(copies, count):
+        def start(d, carry):
+            peer, sends, lands = copies(d)
+            for src, dst, sent, landed in sends:
+                pltpu.make_async_remote_copy(
+                    src_ref=src,
+                    dst_ref=dst,
+                    send_sem=sent,
+                    recv_sem=landed,
+                    device_id=peer,
+                    device_id_type=MESH,
+                ).start()
+            return carry
+
+        def finish(d, carry):
+            peer, sends, lands = copies(d)
+            for src, dst, sent, landed in sends:
+                pltpu.make_async_copy(src, src, sent).wait()
+            for dst, landed in lands:
+                pltpu.make_async_copy(dst, dst, landed).wait()
+            return carry
+
+        lax.fori_loop(1, count, start, 0)
+        lax.fori_loop(1, count, finish, 0)
+
+    exchange(plane_copies, members)
+    own_chunk = chunk_at(mine)
+
+    def add_chunk(d, carry):
+        gw[own_chunk, :] += p_recv[lax.rem(mine + d, members)].astype(F32)
+        return carry
+
+    lax.fori_loop(1, members, add_chunk, 0)
+    z_send[...] = gw[own_chunk, :].astype(BF)
+    m_line[level] = lax.fori_loop(
+        0, members, lambda k, total: total + m_plane[k], jnp.zeros((8, LANES), F32)
+    )
+    exchange(line_copies, planes)
+
+    def add_piece(d, total):
+        return total + z_recv[lax.rem(level + d, planes)].astype(F32)
+
+    total = lax.fori_loop(1, planes, add_piece, gw[part_at(level), :])
+    g_all[part_at(level), :] = total.astype(BF)
+    exchange(line_gather, planes)
+    exchange(plane_gather, members)
+
+    totals = lax.fori_loop(
+        0, planes, lambda k, total: total + m_line[k], jnp.zeros((8, LANES), F32)
+    )
+    totals = jnp.broadcast_to(jnp.sum(totals, axis=1, keepdims=True), (8, LANES))
+
+    def squares(i, total):
+        at = pl.ds(pl.multiple_of(i * 64, 64), 64)
+        block = g_all[at, :].astype(F32)
+        return total + jnp.sum((block * block).reshape(8, 8, 3 * CH), axis=0)
+
+    square = lax.fori_loop(0, gw.shape[0] // 64, squares, jnp.zeros((8, 3 * CH), F32))
+    square = jnp.sum(jnp.sum(square, axis=0, keepdims=True), axis=1, keepdims=True)
+    count = totals[1:2]
+    raw = square + totals[2:3] * totals[2:3] + totals[3:4] * totals[3:4]
+    norm = jnp.sqrt(raw) / count
+    factor = jnp.minimum(1.0, CLIP_NORM / norm) / count
+    scalars[...] = jnp.concatenate([totals[:4], norm, factor, totals[6:]], axis=0)
+
 
 def train(velocity, targets, meta, wf, wb, w0f, w0b, norms, headf, headb, bias):
     ranks = lax.axis_size("rows")
+    planes = lax.axis_size("batch") // 2
+    members = 2 * ranks
+    unit = 16 * members * planes
+    lines = -(-((LAYERS + 1) * 3 * CH + CH) // unit) * unit
+    chunk = lines // members
     parts = ranks // 2
     tile = velocity.shape[2]
     rows, half, ext = 2 * tile, tile, 2 * tile + 2 * EDGE
@@ -800,17 +962,19 @@
 
     args = (velocity, targets, meta, wf, wb, w0f, w0b, norms, headf, headb, bias)
     return pl.pallas_call(
-        functools.partial(train_kernel, ranks),
+        functools.partial(train_kernel, ranks, planes),
         out_shape=(
-            jax.ShapeDtypeStruct((LAYERS + 1, 3 * CH, 3 * CH), F32),
-            jax.ShapeDtypeStruct((CH, 48), F32),
-            jax.ShapeDtypeStruct((2, LAYERS + 1, CH, LANES), F32),
-            jax.ShapeDtypeStruct((16, CH), F32),
-            jax.ShapeDtypeStruct((4, 8, LANES), F32),
+            jax.ShapeDtypeStruct((lines, 3 * CH), BF),
+            jax.ShapeDtypeStruct((8, LANES), F32),
         ),
         in_specs=[vmem] * len(args),
-        out_specs=(vmem,) * 5,
+        out_specs=(vmem,) * 2,
         scratch_shapes=[
+            pltpu.VMEM((lines, 3 * CH), F32),
+            pltpu.VMEM((CH, 48), F32),
+            pltpu.VMEM((2, LAYERS + 1, CH, LANES), F32),
+            pltpu.VMEM((CH, 16), F32),
+            pltpu.VMEM((4, 8, LANES), F32),
             pltpu.VMEM((2, ext, LANES), F32),
             pltpu.VMEM((2, 2, rows, LANES), F32),
             pltpu.VMEM((2, 16, LANES), F32),
@@ -843,6 +1007,12 @@
             pltpu.VMEM((2, CH, LANES), F32),
             pltpu.VMEM((10, 16, LANES), F32),
             pltpu.VMEM((10, parts - 1, 16, LANES), F32),
+            pltpu.VMEM((lines, 3 * CH), BF),
+            pltpu.VMEM((members, chunk, 3 * CH), BF),
+            pltpu.VMEM((chunk, 3 * CH), BF),
+            pltpu.VMEM((planes, chunk // planes, 3 * CH), BF),
+            pltpu.VMEM((members, 8, LANES), F32),
+            pltpu.VMEM((planes, 8, LANES), F32),
             pltpu.SemaphoreType.DMA((2, 3)),
             pltpu.SemaphoreType.DMA((2, 3)),
             pltpu.SemaphoreType.DMA((3,)),
@@ -850,6 +1020,10 @@
             pltpu.SemaphoreType.DMA((13, 2)),
             pltpu.SemaphoreType.DMA((10, parts - 1)),
             pltpu.SemaphoreType.DMA((10, parts - 1)),
+            pltpu.SemaphoreType.DMA((3, members)),
+            pltpu.SemaphoreType.DMA((3, members)),
+            pltpu.SemaphoreType.DMA((3, planes)),
+            pltpu.SemaphoreType.DMA((3, planes)),
         ],
         compiler_params=pltpu.CompilerParams(
             collective_id=0, has_side_effects=True, vmem_limit_bytes=60 * 2**20
@@ -889,31 +1063,26 @@
     norms = jnp.broadcast_to(norm_params[..., None], norm_params.shape + (LANES,))
     headf = jnp.pad(head_params[:, :CH], ((0, 14), (0, 0))).astype(BF)
     bias = jnp.broadcast_to(head_params[:, CH:, None], (2, 1, LANES))
-    gw, gw0, gnorm, ghead, misc = train(
+    g_all, scalars = train(
         velocity, targets, meta, wf, wb, w0f, w0f.T, norms, headf, headf.T, bias
     )
-    halves = jnp.array([1.0, 0.5, 0.5, 1.0, 1.0], F32)
+    loss_sum, count, norm, factor = scalars[0, 0], scalars[1, 0], scalars[4, 0], scalars[5, 0]
+    mid_rows = (LAYERS + 1) * 3 * CH
     g_mid = jnp.transpose(
-        gw.reshape(LAYERS + 1, 3, CH, 3, CH) * halves[:, None, None, None, None], (0, 3, 1, 2, 4)
+        g_all[:mid_rows].reshape(LAYERS + 1, 3, CH, 3, CH), (0, 3, 1, 2, 4)
     ).reshape(w_mid.shape)
-    g_in = jnp.transpose(gw0.reshape(CH, 3, 16)[:, :, :9].reshape(CH, 3, 3, 3), (0, 3, 1, 2))
-    layer_halves = jnp.array([1.0, 1.0, 0.5, 0.5, 1.0], F32)
-    g_norm = jnp.sum(gnorm, axis=-1) * layer_halves[None, :, None]
-    sums = jnp.sum(misc, axis=(1, 2))
-    g_head = jnp.concatenate([ghead[:2], sums[2:4, None]], axis=1)
-    grads_in, grads_mid, grads_norm, grads_head, totals = lax.psum(
-        (g_in, g_mid, g_norm, g_head, sums[:2]), ("batch", "rows")
-    )
-    loss_sum, count = totals[0], totals[1]
-    grads = tuple(g / count for g in (grads_in, grads_mid, grads_norm, grads_head))
+    rest = g_all[mid_rows : mid_rows + CH].astype(F32)
+    g_in = rest[:, :48].reshape(CH, 3, 16)[:, :, :9].reshape(CH, 3, 3, 3)
+    g_in = jnp.transpose(g_in, (0, 3, 1, 2))
+    g_norm = rest[:, 48:58].T.reshape(norm_params.shape)
+    g_head = jnp.concatenate([rest[:, 58:60].T, scalars[2:4, :1]], axis=1)
+    grads = (g_in, g_mid, g_norm, g_head)
     params = (w_in, w_mid, norm_params, head_params)
-    norm = jnp.sqrt(sum((jnp.sum(g * g) for g in grads)))
-    scale = jnp.minimum(1.0, CLIP_NORM / norm)
     new_w, new_m, new_v = ([], [], [])
     for weight, moment, second, g, rate in zip(
         params, (m_in, m_mid, m_norm, m_head), (v_in, v_mid, v_norm, v_head), grads, RATES
     ):
-        g = g * scale
+        g = g.astype(F32) * factor
         moment_new = BETA_ONE * moment + (1 - BETA_ONE) * g
         second_new = BETA_TWO * second + (1 - BETA_TWO) * g * g
         mhat = moment_new / (1 - BETA_ONE**STEP_NUM)

time: 396 us -> 275 us (0.69)
  waiting for transfers between devices: 75 us -> 0 us
  blocking collectives: 40.7 us -> 0 us
  Pallas kernels: 214 us -> 240 us
  between operations: 18.1 us -> 0.9 us
  other arithmetic: 22.3 us -> 12.4 us
    psum x1 -> x0, waiting for transfers between devices: 75 us -> none  [shards(): lax.psum((g_in, g_mid, g_norm, g_head, sums[:2]), ('batch', 'rows'))]
    psum x1 -> x0, blocking collectives: 40.7 us -> none  [shards(): lax.psum((g_in, g_mid, g_norm, g_head, sums[:2]), ('batch', 'rows'))]
    pallas_call x1, Pallas kernels: 214 us -> 240 us  [train(): pl.pallas_call(functools.partial(train_kernel, ranks, planes), out_shape=...]
    reduce_sum x6 -> x0, other arithmetic: 10.3 us -> none  [the longest x4 8.56 us: shards(): norm = jnp.sqrt(sum((jnp.sum(g * g) for g in grads)))]
  transfers between devices with their start and end apart: 1 -> 0, of which waited for: 1 -> 0; matrix products, arithmetic and copies ran while one was open for 4% -> 0% of each run, Pallas kernels for 0% -> 0%
where the time goes in v2:
time: 275 us
  Pallas kernels  240 us (87%)
  local copies, waits for them, and re-layouts  21.8 us (8%)
  other arithmetic  12.4 us (5%)
    pallas_call x1, Pallas kernels, train(): pl.pallas_call(functools.partial(train_kernel, ranks, planes), out_shape=...  240 us

profile of v2, /device:TPU:0, one launch (start us, length us, event | category | flops | bytes accessed | tf_op | source)
XLA Modules:
  0.0 274.8 jit_solution(11989854634619600580)
XLA Ops:
  0.7 0.7 convert.12
  1.3 0.9 slice_reduce_fusion
  2.2 0.6 broadcast_in_dim.11.bias
  2.8 0.1 pad.16.clone
  2.9 0.8 concatenate.14
  3.7 0.8 add_convert_fusion
  4.4 0.7 copy.178
  5.1 0.7 convert_bitcast_fusion
  5.9 0.0 copy-start.2
  5.9 0.7 broadcast_in_dim.8.meta
  6.6 0.1 copy.202
  6.7 0.1 copy.219
  6.8 0.6 pad_bitcast_fusion.headb
  7.4 0.6 pad.11.clone.headf
  8.0 0.7 copy.180.w0f
  8.7 0.9 broadcast_in_dim.9.norms
  9.6 1.3 convert_element_type.48
  10.9 0.8 convert_element_type.49
  11.7 0.8 copy.175
  12.5 1.3 convert_element_type.53.wb
  13.8 0.6 copy.225
  14.5 1.3 convert_element_type.51.wf
  15.8 0.0 copy-start.3
  15.9 239.8 %train.1 = (bf16[1024,192]{1,0:T(8,128)(2,1)}, f32[8,128]{1,0:T(8,128)}) custom-call(f32[2,2,32,128]{3,2,1,0:T(8,128)} %vel.1, f32[2,2,2,32,128]{4,3,2,1,0:T(8,128)} %tgt.1, f32[2,16,128]{2,1,0:T(8,128)} %broadcast_in_dim.8.meta, bf16[5,192,192]{2,1,0:T(8,128)(2,1)} %convert_element_type.51.wf, bf16[5,192,192]{2,1,0:T(8,128)(2,1)} %convert_element_type.53.wb, ...), custom_call_target="tpu_custom_call" | custom-call | tf_op jit(solution)/shard_map/train/pallas_call | solution.py:964
  255.7 0.7 slice.49
  256.4 1.3 fusion.16
  257.7 0.8 slice_convert_fusion
  258.5 0.1 slice_bitcast_fusion
  258.6 0.1 copy.194
  258.7 0.0 copy-done.11
  258.7 1.3 fusion.7
  260.0 0.7 fusion.1
  260.7 0.1 copy.190
  260.8 0.1 copy.182
  260.9 0.7 slice_multiply_fusion.1
  261.6 0.6 copy.196
  262.2 0.6 copy.198
  262.8 0.6 copy.200
  263.5 0.6 copy.201
  264.1 0.6 copy.195
  264.7 0.6 copy.197
  265.3 0.6 copy.199
  265.9 0.7 convert_multiply_fusion
  266.6 0.3 copy.187
  266.9 0.9 mul.210
  267.9 0.8 copy.188
  268.7 1.5 mul.212
  270.2 4.6 %fusion.9 = (bf16[5,9,4096]{2,0,1:T(8,128)(2,1)}, f32[5,9,4096]{2,0,1:T(8,128)}, f32[5,9,4096]{2,0,1:T(8,128)}, f32[5,9,4096]{2,0,1:T(8,128)}) fusion(f32[5,9,4096]{2,0,1:T(8,128)S(1)} %copy-done, f32[5,9,4096]{2,0,1:T(8,128)} %mul.212, f32[5,9,4096]{2,0,1:T(8,128)} %param.25, f32[5,9,4096]{2,0,1:T(8,128)} %param.29), kind=kLoop, calls=%fused_computation.33 | loop fusion | flops 2949120 | bytes 5529600 | tf_op jit(solution)/shard_map/convert_element_type | solution.py:1098
  (30 shorter events, 0.2 us)
Async XLA Ops:
  5.9 5.9 %copy-start.2 = (bf16[64,3,16]{0,2,1:T(8,128)(2,1)}, bf16[64,3,16]{0,2,1:T(8,128)(2,1)S(1)}, u32[]{:S(2)}) copy-start(bf16[64,3,16]{0,2,1:T(8,128)(2,1)S(1)} %pad.10.clone) | copy-start | bytes 18436
  15.8 242.8 %copy-start.9 = (f32[2,65]{1,0:T(2,128)S(1)}, f32[2,65]{1,0:T(2,128)}, u32[]{:S(2)}) copy-start(f32[2,65]{1,0:T(2,128)} %param.23) | copy-start | bytes 1564
  15.8 242.8 %copy-start.10 = (f32[2,65]{1,0:T(2,128)S(1)}, f32[2,65]{1,0:T(2,128)}, u32[]{:S(2)}) copy-start(f32[2,65]{1,0:T(2,128)} %param.27) | copy-start | bytes 1564
  15.8 242.8 %copy-start.11 = (f32[2,65]{1,0:T(2,128)S(1)}, f32[2,65]{1,0:T(2,128)}, u32[]{:S(2)}) copy-start(f32[2,65]{1,0:T(2,128)} %param.31) | copy-start | bytes 1564
  15.8 245.7 %copy-start.4 = (f32[2,5,64]{2,0,1:T(2,128)S(1)}, f32[2,5,64]{2,0,1:T(2,128)}, u32[]{:S(2)}) copy-start(f32[2,5,64]{2,0,1:T(2,128)} %param.22) | copy-start | bytes 7684
  15.8 245.7 %copy-start.7 = (f32[2,5,64]{2,0,1:T(2,128)S(1)}, f32[2,5,64]{2,0,1:T(2,128)}, u32[]{:S(2)}) copy-start(f32[2,5,64]{2,0,1:T(2,128)} %param.26) | copy-start | bytes 7684
  15.8 245.7 %copy-start.8 = (f32[2,5,64]{2,0,1:T(2,128)S(1)}, f32[2,5,64]{2,0,1:T(2,128)}, u32[]{:S(2)}) copy-start(f32[2,5,64]{2,0,1:T(2,128)} %param.30) | copy-start | bytes 7684
  15.8 247.6 %copy-start.3 = (f32[64,3,3,3]{0,3,2,1:T(4,128)S(1)}, f32[64,3,3,3]{0,3,2,1:T(4,128)}, u32[]{:S(2)}) copy-start(f32[64,3,3,3]{0,3,2,1:T(4,128)} %param.20) | copy-start | bytes 20740
  15.9 247.6 %copy-start.5 = (f32[64,3,3,3]{0,3,2,1:T(4,128)S(1)}, f32[64,3,3,3]{0,3,2,1:T(4,128)}, u32[]{:S(2)}) copy-start(f32[64,3,3,3]{0,3,2,1:T(4,128)} %param.24) | copy-start | bytes 20740
  15.9 247.5 %copy-start.6 = (f32[64,3,3,3]{0,3,2,1:T(4,128)S(1)}, f32[64,3,3,3]{0,3,2,1:T(4,128)}, u32[]{:S(2)}) copy-start(f32[64,3,3,3]{0,3,2,1:T(4,128)} %param.28) | copy-start | bytes 20740
  255.6 10.3 %copy-start.1 = (bf16[1024,192]{1,0:T(8,128)(2,1)S(1)}, bf16[1024,192]{1,0:T(8,128)(2,1)}, u32[]{:S(2)}) copy-start(bf16[1024,192]{1,0:T(8,128)(2,1)} %get-tuple-element.20) | copy-start | bytes 1179652
  268.7 1.5 copy-start

commit v3 on v2

--- a/solution.py
+++ b/solution.py
@@ -31,6 +31,10 @@
 MESH = pl.DeviceIdType.MESH
 FULL_SLOT = {0: 0, 1: 1, 4: 2}
 HALF_SLOT = {2: 0, 3: 1}
+ACT_LINES = 32
+CONV_LINES = 32
+BAR_LINES = 16
+SUM_LINES = 32
 
 
 def nt_dot(a, b):
@@ -50,13 +54,12 @@
 
 
 def from_left(x, by):
-    return jnp.where(lane_of(x.shape) < by, 0.0, pltpu.roll(x, by, x.ndim - 1))
+    return jnp.where(lane_of(x.shape) < by, jnp.zeros((), x.dtype), pltpu.roll(x, by, x.ndim - 1))
 
 
 def from_right(x, by):
-    return jnp.where(
-        lane_of(x.shape) >= LANES - by, 0.0, pltpu.roll(x, LANES - by, x.ndim - 1)
-    )
+    moved = pltpu.roll(x, LANES - by, x.ndim - 1)
+    return jnp.where(lane_of(x.shape) >= LANES - by, jnp.zeros((), x.dtype), moved)
 
 
 def pair_sum(x):
@@ -106,8 +109,16 @@
 def train_kernel(
     ranks,
     planes,
+    keys,
+    boxes,
     vel,
     tgt,
+    w_in,
+    w_mid,
+    norm_params,
+    head,
+    g_all,
+    scalars,
     meta,
     wf,
     wb,
@@ -117,8 +128,9 @@
     headf,
     headb,
     bias,
-    g_all,
-    scalars,
+    lines,
+    wide,
+    small,
     gw,
     gw0,
     gnorm,
@@ -147,11 +159,11 @@
     inv_kept,
     zbuf,
     skip_bar,
-    half_bar,
     sg,
     sgh,
     edges,
     g_halo,
+    pool_mat,
     coef,
     acc,
     st_send,
@@ -221,6 +233,16 @@
         return carry
 
     lax.fori_loop(1, planes, greet_line, 0)
+
+    line_is = lax.broadcasted_iota(jnp.int32, (16, LANES), 0)
+    for j in range(2):
+        values = [keys[j, k] for k in range(2)]
+        values += [boxes[j, b, k] for b in range(2) for k in range(4)]
+        facts = jnp.zeros((16, LANES), F32)
+        for k, value in enumerate(values):
+            facts = jnp.where(line_is == k, value.astype(F32), facts)
+        meta[j] = facts
+
     pl.semaphore_wait(barrier, members + planes - 2)
 
     def incoming(place):
@@ -248,6 +270,55 @@
                     device_id=(to_batch, to_row),
                     device_id_type=MESH,
                 ).start()
+
+    low_lanes = lane_of((CH // 2, LANES)) < CH
+    for ky in range(3):
+        for kx in range(3):
+            for a in range(CH // 2):
+                lines[kx, a, : LAYERS + 1, :] = w_mid[3 * ky + kx, :, a * LANES : (a + 1) * LANES]
+        for k in range(LAYERS + 1):
+            left, mid, right = (lines[kx, :, k, :] for kx in range(3))
+            slab = 3 * k + ky
+            even, odd = pl.ds(0, CH // 2, 2), pl.ds(1, CH // 2, 2)
+            wide[0, slab, even, :] = jnp.where(low_lanes, left, pltpu.roll(mid, CH, 1))
+            wide[0, slab, odd, :] = jnp.where(low_lanes, pltpu.roll(left, CH, 1), mid)
+            wide[1, slab, even, :] = right
+            wide[1, slab, odd, :] = pltpu.roll(right, CH, 1)
+    low_lanes = lane_of((CH, LANES)) < CH
+    for k in range(LAYERS + 1):
+        for ky in range(3):
+            slab = 3 * k + ky
+            at = slice(ky * CH, (ky + 1) * CH)
+            first, last = wide[0, slab], wide[1, slab]
+            wf[k, at, :] = jnp.concatenate([first, last[:, :CH]], axis=1).astype(BF)
+            turned = jnp.concatenate([first, last], axis=0).T
+            left, mid = turned[:CH], turned[CH:]
+            first = jnp.where(low_lanes, left, pltpu.roll(mid, CH, 1))
+            last = pltpu.roll(left, CH, 1)
+            wb[k, at, :] = jnp.concatenate([first, last[:, :CH]], axis=1).astype(BF)
+    small[...] = jnp.zeros_like(small)
+    for ch in range(3):
+        for ky in range(3):
+            taps_in = w_in[ch, ky]
+            taps_in = jnp.concatenate([taps_in, jnp.zeros_like(taps_in)], axis=1)
+            small[pl.ds(16 * ky + ch, 3, 3), :] = taps_in
+    for layer in range(LAYERS + 1):
+        pair = norm_params[layer]
+        small[48 + 2 * layer : 50 + 2 * layer, :] = jnp.concatenate(
+            [pair, jnp.zeros_like(pair)], axis=1
+        )
+    pair = head[:, :CH]
+    small[64:66, :] = jnp.concatenate([pair, jnp.zeros_like(pair)], axis=1)
+    w0b[...] = small[:48, :CH].astype(BF)
+    headf[...] = small[64:80, :CH].astype(BF)
+    turned = small[...].T[:CH]
+    w0f[...] = turned[:, :48].astype(BF)
+    headb[...] = turned[:, 64:80].astype(BF)
+    for which in range(2):
+        for layer in range(LAYERS + 1):
+            at = 48 + 2 * layer + which
+            norms[which, layer] = jnp.broadcast_to(turned[:, at : at + 1], (CH, LANES))
+        bias[which] = jnp.broadcast_to(head[which : which + 1, CH : CH + 1], (1, LANES))
 
     for j in range(2):
         to_batch, to_row = owner(2 * core + j, row_at // 2)
@@ -331,25 +402,27 @@
         halo_start(*args)
         halo_wait(*args)
 
-    def group_totals(slot, first, second):
-        local = jnp.concatenate([group_rows(first), group_rows(second)], axis=0)
-        st_send[slot] = local
-        copies = []
-        for d in range(1, parts):
-            copies.append(
-                pltpu.make_async_remote_copy(
-                    src_ref=st_send.at[slot],
-                    dst_ref=st_recv.at[slot, d - 1],
-                    send_sem=st_ss.at[slot, d - 1],
-                    recv_sem=st_rs.at[slot, d - 1],
-                    device_id=owner(sample, lax.rem(part + d, parts)),
-                    device_id_type=MESH,
-                )
+    def group_copies(slot):
+        return [
+            pltpu.make_async_remote_copy(
+                src_ref=st_send.at[slot],
+                dst_ref=st_recv.at[slot, d - 1],
+                send_sem=st_ss.at[slot, d - 1],
+                recv_sem=st_rs.at[slot, d - 1],
+                device_id=owner(sample, lax.rem(part + d, parts)),
+                device_id_type=MESH,
             )
-        for copy in copies:
+            for d in range(1, parts)
+        ]
+
+    def group_start(slot, first, second):
+        st_send[slot] = jnp.concatenate([group_rows(first), group_rows(second)], axis=0)
+        for copy in group_copies(slot):
             copy.start()
-        total = local
-        for d, copy in enumerate(copies):
+
+    def group_finish(slot):
+        total = st_send[slot]
+        for d, copy in enumerate(group_copies(slot)):
             copy.wait()
             total = total + st_recv[slot, d]
         total = jnp.broadcast_to(jnp.sum(total, axis=1, keepdims=True), total.shape)
@@ -387,21 +460,26 @@
 
     ext_halo(10, u_ext)
 
+    source = lax.broadcasted_iota(jnp.int32, pool_mat.shape, 0) % LANES
+    target = lane_of(pool_mat.shape)
+    column = target % LANES + 2 * (target // LANES - 1)
+    pool_mat[...] = jnp.where(source // 2 == (column + 2) // 2 - 1, 0.25, 0.0).astype(BF)
+
     for kx in range(3):
         field = opened[...]
         s0[:, 3 * kx + 2, :] = (from_left(field, 1), field, from_right(field, 1))[kx]
 
-    def put_shifted(dst, at, x, by, order):
+    def put_shifted(dst, at, c, x, by, order):
         copies = (from_left(x, by), x, from_right(x, by))
         for place_at, which in enumerate(order):
-            dst[at, place_at * CH : (place_at + 1) * CH, :] = copies[which].astype(BF)
+            dst[at, slice(place_at * CH + c.start, place_at * CH + c.stop), :] = copies[which]
 
     FORWARD = (0, 1, 2)
     BACKWARD = (2, 1, 0)
 
     def spread_halo(dst, lines, count, by, order):
         for at, line in ((0, lines[0]), (count + 1, lines[1])):
-            put_shifted(dst, at, line.astype(F32), by, order)
+            put_shifted(dst, at, slice(0, CH), line, by, order)
 
     def for_blocks(count, size, body):
         size = min(size, count)
@@ -416,19 +494,20 @@
         return [slice(16 * c, 16 * c + 16) for c in range(CH // 16)]
 
     def make_norm(layer, t, sums, squares, count):
+        group_start(layer, sums, squares)
+        sums, squares = group_finish(layer)
         size = CH // GROUPS * count * LANES * parts
         mean = sums / size
         inverse = lax.rsqrt(squares / size - mean * mean + EPS_NORM)
-        coef[0] = spread(inverse)
-        coef[1] = spread(-mean * inverse)
-        coef[2] = norms[0, layer]
-        coef[3] = norms[1, layer]
-        inv_kept[t, layer] = coef[0]
+        scale = spread(inverse)
+        inv_kept[t, layer] = scale
+        scale = 0.5 * scale * norms[0, layer]
+        coef[0] = scale
+        coef[1] = 0.5 * norms[1, layer] - spread(mean) * scale
 
     def activate(z, c):
-        xhat = z * coef[0, c] + coef[1, c]
-        n = xhat * coef[2, c] + coef[3, c]
-        return xhat, n * (0.5 * jnp.tanh(0.5 * n) + 0.5)
+        n = z * coef[0, c] + coef[1, c]
+        return n, n * jnp.tanh(n) + n
 
     def conv_sums(count, size, rows_of):
         size = min(size, count)
@@ -471,68 +550,57 @@
         return result
 
     def finish_plain(t, layer, count, kept, xh, xh_at, dst, by, slot):
-        def edge(which, line):
-            xhat, h = activate(zbuf[line], slice(0, CH))
-            edges[slot, which] = h.astype(BF)
-
-        edge(0, 0)
-        edge(1, count - 1)
+        for which, line in enumerate((0, count - 1)):
+            edges[slot, which] = activate(zbuf[line], slice(0, CH))[1].astype(BF)
         args = (slot, edges.at[slot, 0], edges.at[slot, 1], kept.at[t, 0], kept.at[t, count + 1])
         halo_start(*args)
 
         def block(base, size):
+            at = pl.ds(base + 1, size)
             for c in channel_blocks():
-                xhat, h = activate(zbuf[pl.ds(base, size), c, :], c)
-                xh[xh_at, t, pl.ds(base, size), c, :] = xhat.astype(BF)
+                n, h = activate(zbuf[pl.ds(base, size), c, :], c)
+                xh[xh_at, t, pl.ds(base, size), c, :] = n.astype(BF)
                 low = h.astype(BF)
-                kept[t, pl.ds(base + 1, size), c, :] = low
-                at = pl.ds(base + 1, size)
-                dst[at, c, :] = from_left(h, by).astype(BF)
-                dst[at, slice(CH + c.start, CH + c.stop), :] = low
-                dst[at, slice(2 * CH + c.start, 2 * CH + c.stop), :] = from_right(h, by).astype(BF)
-
-        for_blocks(count, 8, block)
+                kept[t, at, c, :] = low
+                put_shifted(dst, at, c, low, by, FORWARD)
+
+        for_blocks(count, ACT_LINES, block)
         halo_wait(*args)
         spread_halo(dst, (kept[t, 0], kept[t, count + 1]), count, by, FORWARD)
 
-    def pool_of(first, second):
-        pair = first.astype(BF).astype(F32) + second.astype(BF).astype(F32)
-        return 0.25 * pair_sum(pair)
+    def pool_pairs(low, size):
+        pairs = jnp.concatenate(
+            [beside([low[2 * j], low[2 * j + 1]]) for j in range(size // 2)], axis=0
+        )
+        return nn_dot(pairs, pool_mat[...]).astype(BF).reshape(size // 2, CH, 3 * LANES)
 
     def finish_skip(t):
-        def edge(which, line):
-            xhat, first = activate(zbuf[line], slice(0, CH))
-            xhat, second = activate(zbuf[line + 1], slice(0, CH))
-            edges[1, which] = (first, second)[which].astype(BF)
-            edges[2, which] = pool_of(first, second).astype(BF)
-
-        edge(0, 0)
-        edge(1, rows - 2)
+        for which, line in enumerate((0, rows - 2)):
+            low = activate(zbuf[pl.ds(line, 2)], slice(0, CH))[1].astype(BF)
+            edges[1, which] = low[which]
+            edges[2, which] = pool_pairs(low, 2)[0, :, LANES : 2 * LANES]
         skip_args = (1, edges.at[1, 0], edges.at[1, 1], skip.at[t, 0], skip.at[t, rows + 1])
         pool_args = (2, edges.at[2, 0], edges.at[2, 1], pooled.at[t, 0], pooled.at[t, half + 1])
         halo_start(*pool_args)
         halo_start(*skip_args)
 
         def block(base, size):
+            at = pl.ds(base + 1, size)
+            lows = []
             for c in channel_blocks():
-                xhat, h = activate(zbuf[pl.ds(base, size), c, :], c)
-                xh_full[1, t, pl.ds(base, size), c, :] = xhat.astype(BF)
+                n, h = activate(zbuf[pl.ds(base, size), c, :], c)
+                xh_full[1, t, pl.ds(base, size), c, :] = n.astype(BF)
                 low = h.astype(BF)
-                at = pl.ds(base + 1, size)
                 skip[t, at, c, :] = low
-                sg[at, c, :] = from_left(h, 1).astype(BF)
-                sg[at, slice(CH + c.start, CH + c.stop), :] = low
-                sg[at, slice(2 * CH + c.start, 2 * CH + c.stop), :] = from_right(h, 1).astype(BF)
-                pairs = low.astype(F32).reshape(size // 2, 2, 16, LANES)
-                mean = 0.25 * pair_sum(pairs[:, 0] + pairs[:, 1])
-                at = pl.ds(base // 2 + 1, size // 2)
-                small = mean.astype(BF)
-                pooled[t, at, c, :] = small
-                sgh[at, c, :] = from_left(mean, 2).astype(BF)
-                sgh[at, slice(CH + c.start, CH + c.stop), :] = small
-                sgh[at, slice(2 * CH + c.start, 2 * CH + c.stop), :] = from_right(mean, 2).astype(BF)
-
-        for_blocks(rows, 8, block)
+                put_shifted(sg, at, c, low, 1, FORWARD)
+                lows.append(low)
+            small = pool_pairs(jnp.concatenate(lows, axis=1), size)
+            at = pl.ds(base // 2 + 1, size // 2)
+            pooled[t, at] = small[:, :, LANES : 2 * LANES]
+            for k in range(3):
+                sgh[at, k * CH : (k + 1) * CH, :] = small[:, :, k * LANES : (k + 1) * LANES]
+
+        for_blocks(rows, ACT_LINES, block)
         halo_wait(*pool_args)
         halo_wait(*skip_args)
         spread_halo(sgh, (pooled[t, 0], pooled[t, half + 1]), half, 2, FORWARD)
@@ -542,15 +610,15 @@
         def block(base, size):
             lows = []
             for c in channel_blocks():
-                xhat, h = activate(zbuf[pl.ds(base, size), c, :], c)
-                xh_full[2, t, pl.ds(base, size), c, :] = xhat.astype(BF)
+                n, h = activate(zbuf[pl.ds(base, size), c, :], c)
+                xh_full[2, t, pl.ds(base, size), c, :] = n.astype(BF)
                 lows.append(h.astype(BF))
             low = jnp.concatenate(lows, axis=1)
             force = nn_dot(headf[...], beside([low[j] for j in range(size)]))
             for j in range(size):
                 frows[base + j] = force[:, j * LANES : (j + 1) * LANES]
 
-        for_blocks(rows, 8, block)
+        for_blocks(rows, ACT_LINES, block)
 
     def forward_step(t, carry):
         for c in range(2):
@@ -566,15 +634,15 @@
             z = nn_dot(w0f[...], x)
             return [z[:, j * LANES : (j + 1) * LANES] for j in range(size)]
 
-        make_norm(0, t, *group_totals(0, *conv_sums(rows, 16, first_rows)), rows)
+        make_norm(0, t, *conv_sums(rows, CONV_LINES, first_rows), rows)
         finish_plain(t, 0, rows, h1, xh_full, 0, sg, 1, 0)
-        make_norm(1, t, *group_totals(1, *conv_sums(rows, 16, conv_of(sg, 0))), rows)
+        make_norm(1, t, *conv_sums(rows, CONV_LINES, conv_of(sg, 0)), rows)
         finish_skip(t)
-        make_norm(2, t, *group_totals(2, *conv_sums(half, 16, conv_of(sgh, 1))), half)
+        make_norm(2, t, *conv_sums(half, CONV_LINES, conv_of(sgh, 1)), half)
         finish_plain(t, 2, half, h3, xh_half, 0, sgh, 2, 3)
-        make_norm(3, t, *group_totals(3, *conv_sums(half, 16, conv_of(sgh, 2))), half)
+        make_norm(3, t, *conv_sums(half, CONV_LINES, conv_of(sgh, 2)), half)
         finish_plain(t, 3, half, h4, xh_half, 1, sgh, 1, 4)
-        make_norm(4, t, *group_totals(4, *conv_sums(rows, 16, conv_last)), rows)
+        make_norm(4, t, *conv_sums(rows, CONV_LINES, conv_last), rows)
         finish_last(t)
 
         for c in range(2):
@@ -599,62 +667,60 @@
 
     lax.fori_loop(0, STEPS, forward_step, 0)
 
-    def bar_block(layer, xh, xh_at, t, base, size, c, h_bar):
-        xhat = xh[xh_at, t, pl.ds(base, size), c, :].astype(F32)
-        n = xhat * norms[0, layer, c] + norms[1, layer, c]
-        sig = 0.5 * jnp.tanh(0.5 * n) + 0.5
-        n_bar = h_bar * (sig * (1.0 + n * (1.0 - sig)))
+    def bar_block(xh, xh_at, t, base, size, c, h_bar):
+        n = xh[xh_at, t, pl.ds(base, size), c, :].astype(F32)
+        bend = jnp.tanh(n)
+        moved = n * bend
+        n_bar = h_bar * ((1.0 + bend) * ((1.0 + n) - moved))
         zbuf[pl.ds(base, size), c, :] = n_bar
         acc[0, c, :] += jnp.sum(n_bar, axis=0)
-        acc[1, c, :] += jnp.sum(n_bar * xhat, axis=0)
-        return n * sig
-
-    def first_pass(layer, t, count, xh, xh_at, h_bar_of):
+        acc[1, c, :] += jnp.sum(n_bar * n, axis=0)
+        return n + moved
+
+    def clear_sums():
         acc[...] = jnp.zeros_like(acc)
 
-        def block(base, size):
-            for c in channel_blocks():
-                bar_block(layer, xh, xh_at, t, base, size, c, h_bar_of(base, size, c))
-
-        for_blocks(count, 8, block)
-
     def first_pass_last(t):
-        acc[...] = jnp.zeros_like(acc)
+        clear_sums()
 
         def block(base, size):
             low = beside([frows[base + j].astype(BF) for j in range(size)])
             h_bar = nn_dot(headb[...], low)
-            lows = []
-            for c in channel_blocks():
-                bar = jnp.stack(
-                    [h_bar[c, j * LANES : (j + 1) * LANES] for j in range(size)], axis=0
-                )
-                h = bar_block(4, xh_full, 2, t, base, size, c, bar)
-                lows.append(h.astype(BF))
+            bars = jnp.stack([h_bar[:, j * LANES : (j + 1) * LANES] for j in range(size)], axis=0)
+            lows = [
+                bar_block(xh_full, 2, t, base, size, c, bars[:, c, :]).astype(BF)
+                for c in channel_blocks()
+            ]
             h = jnp.concatenate(lows, axis=1)
             ghead[...] += nt_dot(beside([h[j] for j in range(size)]), low)
 
-        for_blocks(rows, 8, block)
-
-    def second_pass(layer, t, count, xh, xh_at, dst, by):
+        for_blocks(rows, BAR_LINES, block)
+
+    def sums_start(layer):
         gain = norms[0, layer]
-        sums, cross = acc[0], acc[1]
+        sums = 0.5 * acc[0]
+        cross = (acc[1] - norms[1, layer] * sums) / gain
+        group_start(5 + layer, gain * sums, gain * cross)
         gnorm[0, layer] += cross
         gnorm[1, layer] += sums
+
+    def second_pass(layer, t, count, xh, xh_at, dst, by):
         size_all = CH // GROUPS * count * LANES * parts
-        total, total_cross = group_totals(5 + layer, gain * sums, gain * cross)
+        total, total_cross = group_finish(5 + layer)
         inverse = inv_kept[t, layer]
-        coef[0] = gain * inverse
-        coef[1] = -inverse * spread(total_cross / size_all)
-        coef[2] = -inverse * spread(total / size_all)
+        gain = norms[0, layer]
+        slope = inverse * spread(total_cross / size_all) / gain
+        coef[0] = 0.5 * gain * inverse
+        coef[1] = -2.0 * slope
+        coef[2] = norms[1, layer] * slope - inverse * spread(total / size_all)
 
         def z_bar(at, c):
-            xhat = xh[xh_at, t, at, c, :].astype(F32)
-            return zbuf[at, c, :] * coef[0, c] + xhat * coef[1, c] + coef[2, c]
+            n = xh[xh_at, t, at, c, :].astype(F32)
+            return (zbuf[at, c, :] * coef[0, c] + n * coef[1, c] + coef[2, c]).astype(BF)
 
         slot = 5 + layer
         for which, line in enumerate((0, count - 1)):
-            edges[slot, which] = z_bar(line, slice(0, CH)).astype(BF)
+            edges[slot, which] = z_bar(line, slice(0, CH))
         args = (
             slot,
             edges.at[slot, 0],
@@ -668,13 +734,12 @@
             at = pl.ds(base + 1, size)
             for c in channel_blocks():
                 z = z_bar(pl.ds(base, size), c)
-                dst[at, slice(CH + c.start, CH + c.stop), :] = z.astype(BF)
                 if by:
-                    dst[at, c, :] = from_right(z, by).astype(BF)
-                    right = slice(2 * CH + c.start, 2 * CH + c.stop)
-                    dst[at, right, :] = from_left(z, by).astype(BF)
-
-        for_blocks(count, 8, block)
+                    put_shifted(dst, at, c, z, by, BACKWARD)
+                else:
+                    dst[at, slice(CH + c.start, CH + c.stop), :] = z
+
+        for_blocks(count, ACT_LINES, block)
         halo_wait(*args)
         if by:
             spread_halo(dst, (g_halo[layer, 0], g_halo[layer, 1]), count, by, BACKWARD)
@@ -688,53 +753,70 @@
             tap_rows(y, j + 2, 0) + tap_rows(y, j + 1, 1) + tap_rows(y, j, 2) for j in range(size)
         ]
 
-    def products(t, layer, count, src, kept, out):
+    def bars_of(layer, count, src, then):
+        clear_sums()
+
         def block(base, size):
             g = beside([src[base + j] for j in range(size + 2)])
-            for j, bar in enumerate(bar_rows(wb[layer], g, size)):
-                out[base + j] = bar
+            then(base, size, jnp.stack(bar_rows(wb[layer], g, size), axis=0))
+
+        for_blocks(count, BAR_LINES, block)
+
+    def weight_sums(at, t, count, src, kept):
+        def block(base, size):
+            g = beside([src[base + 1 + j] for j in range(size)])
             h = beside([kept[t, pl.ds(base + j, 3)].reshape(3 * CH, LANES) for j in range(size)])
-            gw[layer * 3 * CH : (layer + 1) * 3 * CH, :] += nt_dot(
-                g[:, LANES : (size + 1) * LANES], h
-            )
-
-        for_blocks(count, 16, block)
-
-    def products_last(t):
+            gw[at * 3 * CH : (at + 1) * 3 * CH, :] += nt_dot(g, h)
+
+        for_blocks(count, SUM_LINES, block)
+
+    def bars_last(t):
+        clear_sums()
+
         def block(base, size):
             g = beside([sg[base + j] for j in range(size + 2)])
-            inner = g[:, LANES : (size + 1) * LANES]
-            low = base // 2
             for j, bar in enumerate(bar_rows(wb[4], g, size)):
                 skip_bar[base + j] = bar
             ups = bar_rows(wb[3], g, size)
-            for j in range(size // 2):
-                half_bar[low + j] = pair_sum(ups[2 * j] + ups[2 * j + 1])
+            low = base // 2
+            bars = jnp.stack(
+                [pair_sum(ups[2 * j] + ups[2 * j + 1]) for j in range(size // 2)], axis=0
+            )
+            for c in channel_blocks():
+                bar_block(xh_half, 1, t, low, size // 2, c, bars[:, c, :])
+
+        for_blocks(rows, BAR_LINES, block)
+
+    def weight_sums_last(t):
+        def block(base, size):
+            g = beside([sg[base + 1 + j] for j in range(size)])
+            low = base // 2
             h = beside([skip[t, pl.ds(base + j, 3)].reshape(3 * CH, LANES) for j in range(size)])
-            gw[4 * 3 * CH : 5 * 3 * CH, :] += nt_dot(inner, h)
+            gw[4 * 3 * CH : 5 * 3 * CH, :] += nt_dot(g, h)
             up = beside(
                 [
                     jnp.concatenate([h4[t, low + (j + ky - 1) // 2 + 1] for ky in range(3)], axis=0)
                     for j in range(size)
                 ]
             )
-            gw[3 * 3 * CH : 4 * 3 * CH, :] += nt_dot(inner, up)
-
-        for_blocks(rows, 16, block)
-
-    def products_first(t):
+            gw[3 * 3 * CH : 4 * 3 * CH, :] += nt_dot(g, up)
+
+        for_blocks(rows, SUM_LINES, block)
+
+    def taps_first():
         def block(base, size):
             g = beside([sg[base + j, CH : 2 * CH, :] for j in range(size)])
             y = nn_dot(w0b[...], g)
             for j in range(size):
                 taps[base + j] = y[:, j * LANES : (j + 1) * LANES]
 
-        for_blocks(rows, 16, block)
+        for_blocks(rows, SUM_LINES, block)
         g = beside([sg[rows + j, CH : 2 * CH, :] for j in range(2)])
         y = nn_dot(w0b[...], g)
         for j in range(2):
             taps[rows + j] = y[:, j * LANES : (j + 1) * LANES]
 
+    def weight_sums_first(t):
         def weights(base, size):
             g = beside([sg[base + 1 + j, CH : 2 * CH, :] for j in range(size)])
             x = beside(
@@ -742,10 +824,18 @@
             )
             gw0[...] += nt_dot(g, x)
 
-        for_blocks(rows, 16, weights)
-
-    def backward_step(i, carry):
-        t = STEPS - 1 - i
+        for_blocks(rows, SUM_LINES, weights)
+
+    def w_args():
+        return (
+            12,
+            w_ext.at[:, pl.ds(EDGE, EDGE), :],
+            w_ext.at[:, pl.ds(rows, EDGE), :],
+            w_ext.at[:, pl.ds(0, EDGE), :],
+            w_ext.at[:, pl.ds(rows + EDGE, EDGE), :],
+        )
+
+    def pull_start(t):
         facts = m_own[0]
         at = (t + 1).astype(F32)
         open_own = opened[own, :]
@@ -755,7 +845,11 @@
                 live = (facts[k : k + 1] == at).astype(F32)
                 pull = pull + live * (u_kept[t, c] - t_own[k, c])
             w_ext[c, own, :] = open_own * (u_bar[c] + 2.0 * open_own * pull)
-        ext_halo(12, w_ext)
+        halo_start(*w_args())
+
+    def backward_step(i, carry):
+        t = STEPS - 1 - i
+        halo_wait(*w_args())
         grid = grid_mask[...]
         gr, gc = project(w_ext[0], w_ext[1], grid)
         gr, gc = grid * gr, grid * gc
@@ -778,26 +872,43 @@
             frows[:, c, :] = jnp.zeros((rows, LANES), F32)
 
         first_pass_last(t)
+        sums_start(4)
         second_pass(4, t, rows, xh_full, 2, sg, 1)
-        products_last(t)
-        first_pass(3, t, half, xh_half, 1, lambda b, s, c: half_bar[pl.ds(b, s), c, :])
+        bars_last(t)
+        sums_start(3)
+        weight_sums_last(t)
         second_pass(3, t, half, xh_half, 1, sgh, 2)
-        products(t, 2, half, sgh, h3, half_bar)
-        first_pass(2, t, half, xh_half, 0, lambda b, s, c: half_bar[pl.ds(b, s), c, :])
+
+        def into_two(base, size, bars):
+            for c in channel_blocks():
+                bar_block(xh_half, 0, t, base, size, c, bars[:, c, :])
+
+        bars_of(2, half, sgh, into_two)
+        sums_start(2)
+        weight_sums(2, t, half, sgh, h3)
         second_pass(2, t, half, xh_half, 0, sgh, 2)
-        products(t, 1, half, sgh, pooled, half_bar)
-
-        def skip_total(base, size, c):
-            bars = skip_bar[pl.ds(base, size), c, :].reshape(size // 2, 2, 16, LANES)
-            small = half_bar[pl.ds(base // 2, size // 2), c, :]
-            return (bars + 0.25 * small[:, None]).reshape(size, 16, LANES)
-
-        first_pass(1, t, rows, xh_full, 1, skip_total)
+
+        def into_one(base, size, bars):
+            at = pl.multiple_of(2 * base, 2)
+            for c in channel_blocks():
+                direct = skip_bar[pl.ds(at, 2 * size), c, :].reshape(size, 2, 16, LANES)
+                total = (direct + 0.25 * bars[:, None, c, :]).reshape(2 * size, 16, LANES)
+                bar_block(xh_full, 1, t, at, 2 * size, c, total)
+
+        bars_of(1, half, sgh, into_one)
+        sums_start(1)
+        weight_sums(1, t, half, sgh, pooled)
         second_pass(1, t, rows, xh_full, 1, sg, 1)
-        products(t, 0, rows, sg, h1, skip_bar)
-        first_pass(0, t, rows, xh_full, 0, lambda b, s, c: skip_bar[pl.ds(b, s), c, :])
+
+        def into_zero(base, size, bars):
+            for c in channel_blocks():
+                bar_block(xh_full, 0, t, base, size, c, bars[:, c, :])
+
+        bars_of(0, rows, sg, into_zero)
+        sums_start(0)
+        weight_sums(0, t, rows, sg, h1)
         second_pass(0, t, rows, xh_full, 0, sg, 0)
-        products_first(t)
+        taps_first()
         for c in range(2):
             columns = []
             for kx in range(3):
@@ -806,8 +917,15 @@
                     total = total + taps[pl.ds(2 - ky, rows), 16 * ky + 3 * kx + c, :]
                 columns.append(total)
             u_bar[c] += from_right(columns[0], 1) + columns[1] + from_left(columns[2], 1)
+
+        @pl.when(t > 0)
+        def _():
+            pull_start(t - 1)
+
+        weight_sums_first(t)
         return carry
 
+    pull_start(jnp.int32(STEPS - 1))
     lax.fori_loop(0, STEPS, backward_step, 0)
 
     mid_rows = (LAYERS + 1) * 3 * CH
@@ -945,7 +1063,7 @@
     scalars[...] = jnp.concatenate([totals[:4], norm, factor, totals[6:]], axis=0)
 
 
-def train(velocity, targets, meta, wf, wb, w0f, w0b, norms, headf, headb, bias):
+def train(keyframes, boxes, velocity, targets, w_in, w_mid, norm_params, head_params):
     ranks = lax.axis_size("rows")
     planes = lax.axis_size("batch") // 2
     members = 2 * ranks
@@ -960,16 +1078,29 @@
     def kept(count):
         return pltpu.VMEM((STEPS, count + 2, CH, LANES), BF)
 
-    args = (velocity, targets, meta, wf, wb, w0f, w0b, norms, headf, headb, bias)
+    smem = pl.BlockSpec(memory_space=pltpu.SMEM)
+    args = (keyframes, boxes, velocity, targets, w_in, w_mid, norm_params, head_params)
     return pl.pallas_call(
         functools.partial(train_kernel, ranks, planes),
         out_shape=(
             jax.ShapeDtypeStruct((lines, 3 * CH), BF),
             jax.ShapeDtypeStruct((8, LANES), F32),
         ),
-        in_specs=[vmem] * len(args),
+        in_specs=[smem] * 2 + [vmem] * 6,
         out_specs=(vmem,) * 2,
         scratch_shapes=[
+            pltpu.VMEM((2, 16, LANES), F32),
+            pltpu.VMEM((LAYERS + 1, 3 * CH, 3 * CH), BF),
+            pltpu.VMEM((LAYERS + 1, 3 * CH, 3 * CH), BF),
+            pltpu.VMEM((CH, 48), BF),
+            pltpu.VMEM((48, CH), BF),
+            pltpu.VMEM((2, LAYERS + 1, CH, LANES), F32),
+            pltpu.VMEM((16, CH), BF),
+            pltpu.VMEM((CH, 16), BF),
+            pltpu.VMEM((2, 1, LANES), F32),
+            pltpu.VMEM((3, CH // 2, 8, LANES), F32),
+            pltpu.VMEM((2, 3 * (LAYERS + 1), CH, LANES), F32),
+            pltpu.VMEM((LANES, LANES), F32),
             pltpu.VMEM((lines, 3 * CH), F32),
             pltpu.VMEM((CH, 48), F32),
             pltpu.VMEM((2, LAYERS + 1, CH, LANES), F32),
@@ -998,12 +1129,12 @@
             pltpu.VMEM((STEPS, LAYERS + 1, CH, LANES), F32),
             pltpu.VMEM((rows, CH, LANES), F32),
             pltpu.VMEM((rows, CH, LANES), F32),
-            pltpu.VMEM((half, CH, LANES), F32),
             pltpu.VMEM((rows + 2, 3 * CH, LANES), BF),
             pltpu.VMEM((half + 2, 3 * CH, LANES), BF),
             pltpu.VMEM((10, 2, CH, LANES), BF),
             pltpu.VMEM((LAYERS + 1, 2, CH, LANES), BF),
-            pltpu.VMEM((4, CH, LANES), F32),
+            pltpu.VMEM((2 * LANES, 3 * LANES), BF),
+            pltpu.VMEM((3, CH, LANES), F32),
             pltpu.VMEM((2, CH, LANES), F32),
             pltpu.VMEM((10, 16, LANES), F32),
             pltpu.VMEM((10, parts - 1, 16, LANES), F32),
@@ -1032,6 +1163,114 @@
     )(*args)
 
 
+def adam_kernel(g_all, scalars, *refs):
+    olds = [refs[3 * k : 3 * k + 3] for k in range(4)]
+    news = [refs[12 + 3 * k : 15 + 3 * k] for k in range(4)]
+    low_in, low_mid, low_head, wide, turned, lines = refs[24:]
+    factor = scalars[5:6, :]
+    at_step = pl.program_id(0)
+
+    def update(which, at, g, low=None):
+        weight, moment, second = (ref[at] for ref in olds[which])
+        moment = BETA_ONE * moment + (1 - BETA_ONE) * g
+        second = BETA_TWO * second + (1 - BETA_TWO) * g * g
+        mhat = moment / (1 - BETA_ONE**STEP_NUM)
+        vhat = second / (1 - BETA_TWO**STEP_NUM)
+        change = mhat / (jnp.sqrt(vhat) + ADAM_EPS) + DECAY * weight
+        weight = weight - RATES[which] * change
+        for ref, value in zip(news[which], (weight, moment, second)):
+            ref[at] = value
+        if low is not None:
+            low[at] = weight.astype(BF)
+
+    mid_rows = (LAYERS + 1) * 3 * CH
+
+    @pl.when(at_step == 0)
+    def _():
+        wide[0] = g_all[:mid_rows, :LANES].astype(F32) * factor
+        tail = g_all[:mid_rows, LANES:].astype(F32) * factor[:, :CH]
+        wide[1] = jnp.concatenate([tail, jnp.zeros_like(tail)], axis=1)
+        rest = g_all[mid_rows : mid_rows + CH, :LANES].astype(F32) * factor
+        rest = jnp.concatenate([rest, jnp.zeros_like(rest)], axis=0)
+        turned[...] = rest.T
+        for ch in range(3):
+            for ky in range(3):
+                g = turned[pl.ds(16 * ky + ch, 3, 3), :]
+                update(0, (ch, ky), g[:, :CH], low_in)
+        for layer in range(LAYERS + 1):
+            g = turned[pl.ds(48 + layer, 2, LAYERS + 1), :]
+            update(2, (layer,), g[:, :CH])
+        bias = scalars[2:4, :] * factor
+        g = jnp.where(lax.broadcasted_iota(jnp.int32, (2, LANES), 1) < CH, turned[58:60, :], bias)
+        update(3, (slice(None),), g[:, : CH + 1], low_head)
+
+    low_lanes = lax.broadcasted_iota(jnp.int32, (CH // 2, LANES), 1) < CH
+    for ky in range(3):
+
+        @pl.when(at_step == ky)
+        def _():
+            for k in range(LAYERS + 1):
+                for kx in range(3):
+                    base = k * 3 * CH + kx * CH
+                    even = wide[ky // 2, pl.ds(base, CH // 2, 2), :]
+                    odd = wide[ky // 2, pl.ds(base + 1, CH // 2, 2), :]
+                    if ky % 2:
+                        even = pltpu.roll(even, CH, 1)
+                    else:
+                        odd = pltpu.roll(odd, CH, 1)
+                    lines[kx, :, k, :] = jnp.where(low_lanes, even, odd)
+
+    for kx in range(3):
+        g = jnp.concatenate(
+            [lines[kx, a, : LAYERS + 1, :] for a in range(CH // 2)], axis=1
+        )
+        update(1, (kx,), g, low_mid)
+
+
+def adam(g_all, scalars, params, moments, seconds):
+    shapes = [w.shape for w in params]
+    whole = lambda shape: pl.BlockSpec(shape, lambda i: (0,) * len(shape))
+    mid = pl.BlockSpec((3,) + shapes[1][1:], lambda i: (i, 0, 0))
+    spec = lambda k: mid if k == 1 else whole(shapes[k])
+    states = [x for group in zip(params, moments, seconds) for x in group]
+    lows = (0, 1, 3)
+    return pl.pallas_call(
+        adam_kernel,
+        grid=(3,),
+        out_shape=tuple(jax.ShapeDtypeStruct(x.shape, F32) for x in states)
+        + tuple(jax.ShapeDtypeStruct(shapes[k], BF) for k in lows),
+        in_specs=[whole(g_all.shape), whole(scalars.shape)] + [spec(k // 3) for k in range(12)],
+        out_specs=tuple(spec(k // 3) for k in range(12)) + tuple(spec(k) for k in lows),
+        scratch_shapes=[
+            pltpu.VMEM((2, (LAYERS + 1) * 3 * CH, LANES), F32),
+            pltpu.VMEM((LANES, LANES), F32),
+            pltpu.VMEM((3, CH // 2, 8, LANES), F32),
+        ],
+        compiler_params=pltpu.CompilerParams(vmem_limit_bytes=40 * 2**20),
+        name="adam",
+    )(g_all, scalars, *states)
+
+
+def in_order(group):
+    first, mid, norm, head = group
+    return (
+        jnp.transpose(first, (1, 2, 3, 0)),
+        jnp.transpose(mid, (1, 0, 2)),
+        jnp.transpose(norm, (1, 0, 2)),
+        head,
+    )
+
+
+def out_of_order(group):
+    first, mid, norm, head = group
+    return (
+        jnp.transpose(first, (3, 0, 1, 2)),
+        jnp.transpose(mid, (1, 0, 2)),
+        jnp.transpose(norm, (1, 0, 2)),
+        head,
+    )
+
+
 def shards(
     velocity,
     targets,
@@ -1050,56 +1289,23 @@
     v_norm,
     v_head,
 ):
-    samples = velocity.shape[0]
-    facts = jnp.concatenate(
-        [keyframes, boxes.reshape(samples, 8), jnp.zeros((samples, 6), jnp.int32)], axis=1
-    ).astype(F32)
-    meta = jnp.broadcast_to(facts[:, :, None], (samples, 16, LANES))
-    mid = w_mid.reshape(LAYERS + 1, 3, 3, CH, CH)
-    wf = jnp.transpose(mid, (0, 1, 3, 2, 4)).reshape(LAYERS + 1, 3 * CH, 3 * CH).astype(BF)
-    wb = jnp.transpose(mid, (0, 1, 4, 2, 3)).reshape(LAYERS + 1, 3 * CH, 3 * CH).astype(BF)
-    first = jnp.transpose(w_in, (0, 2, 3, 1)).reshape(CH, 3, 9)
-    w0f = jnp.pad(first, ((0, 0), (0, 0), (0, 7))).reshape(CH, 48).astype(BF)
-    norms = jnp.broadcast_to(norm_params[..., None], norm_params.shape + (LANES,))
-    headf = jnp.pad(head_params[:, :CH], ((0, 14), (0, 0))).astype(BF)
-    bias = jnp.broadcast_to(head_params[:, CH:, None], (2, 1, LANES))
-    g_all, scalars = train(
-        velocity, targets, meta, wf, wb, w0f, w0f.T, norms, headf, headf.T, bias
-    )
-    loss_sum, count, norm, factor = scalars[0, 0], scalars[1, 0], scalars[4, 0], scalars[5, 0]
-    mid_rows = (LAYERS + 1) * 3 * CH
-    g_mid = jnp.transpose(
-        g_all[:mid_rows].reshape(LAYERS + 1, 3, CH, 3, CH), (0, 3, 1, 2, 4)
-    ).reshape(w_mid.shape)
-    rest = g_all[mid_rows : mid_rows + CH].astype(F32)
-    g_in = rest[:, :48].reshape(CH, 3, 16)[:, :, :9].reshape(CH, 3, 3, 3)
-    g_in = jnp.transpose(g_in, (0, 3, 1, 2))
-    g_norm = rest[:, 48:58].T.reshape(norm_params.shape)
-    g_head = jnp.concatenate([rest[:, 58:60].T, scalars[2:4, :1]], axis=1)
-    grads = (g_in, g_mid, g_norm, g_head)
-    params = (w_in, w_mid, norm_params, head_params)
-    new_w, new_m, new_v = ([], [], [])
-    for weight, moment, second, g, rate in zip(
-        params, (m_in, m_mid, m_norm, m_head), (v_in, v_mid, v_norm, v_head), grads, RATES
-    ):
-        g = g.astype(F32) * factor
-        moment_new = BETA_ONE * moment + (1 - BETA_ONE) * g
-        second_new = BETA_TWO * second + (1 - BETA_TWO) * g * g
-        mhat = moment_new / (1 - BETA_ONE**STEP_NUM)
-        vhat = second_new / (1 - BETA_TWO**STEP_NUM)
-        new_w.append(weight - rate * (mhat / (jnp.sqrt(vhat) + ADAM_EPS) + DECAY * weight))
-        new_m.append(moment_new)
-        new_v.append(second_new)
+    params = in_order((w_in, w_mid, norm_params, head_params))
+    moments = in_order((m_in, m_mid, m_norm, m_head))
+    seconds = in_order((v_in, v_mid, v_norm, v_head))
+    g_all, scalars = train(keyframes, boxes, velocity, targets, *params)
+    result = adam(g_all, scalars, params, moments, seconds)
+    new_w, new_m, new_v = (out_of_order(result[k:12:3]) for k in range(3))
+    low_in, low_mid, low_head = result[12:]
     return (
         *new_w,
         *new_m,
         *new_v,
-        new_w[0].astype(BF),
-        new_w[1].astype(BF),
-        new_w[3].astype(BF),
-        loss_sum,
-        count,
-        norm,
+        jnp.transpose(low_in, (3, 0, 1, 2)),
+        jnp.transpose(low_mid, (1, 0, 2)),
+        low_head,
+        scalars[0, 0],
+        scalars[1, 0],
+        scalars[4, 0],
     )
 
 

time: 275 us -> 200 us (0.73)
  Pallas kernels: 240 us -> 194 us
  local copies, waits for them, and re-layouts: 21.8 us -> 4.81 us
  other arithmetic: 12.4 us -> 0 us
    pallas_call x1, Pallas kernels: 240 us -> 191 us  [train(): pl.pallas_call(functools.partial(train_kernel, ranks, planes), out_shape=...]
    convert_element_type x6 -> x0, other arithmetic: 8.84 us -> none  [the longest x1 4.61 us: shards(): new_w[1].astype(BF)]
    convert_element_type x6 -> x0, local copies, waits for them, and re-layouts: 5.55 us -> none  [the longest x4 3.54 us: shards(): jnp.transpose(mid, (0, 1, 3, 2, 4)).reshape(LAYERS + 1, 3 * CH, 3 * CH)]
    mul x7 -> x0, local copies, waits for them, and re-layouts: 3.59 us -> none  [shards(): g = g.astype(F32) * factor]
    pallas_call x0 -> x1, Pallas kernels: none -> 3.39 us  [adam(): pl.pallas_call(adam_kernel, grid=(3,), out_shape=tuple((jax.ShapeDtypeStr...]
where the time goes in v3:
time: 200 us
  Pallas kernels  194 us (97%)
  local copies, waits for them, and re-layouts  4.81 us (2%)
    pallas_call x1, Pallas kernels, train(): pl.pallas_call(functools.partial(train_kernel, ranks, planes), out_shape=...  191 us
    unnamed x28, local copies, waits for them, and re-layouts  4.29 us

profile of v3, /device:TPU:0, one launch (start us, length us, event | category | flops | bytes accessed | tf_op | source)
XLA Modules:
  0.0 200.0 jit_solution(7673088395199557171)
XLA Ops:
  0.7 0.0 copy-start.4
  0.7 0.0 copy-start
  0.7 0.0 copy-start.5
  0.7 0.0 copy-start.11
  0.7 0.0 copy-start.6
  0.7 0.0 copy-start.7
  0.7 0.0 copy-start.9
  0.7 0.0 copy-start.10
  0.7 0.0 copy-start.12
  0.8 0.0 copy-start.13
  0.8 190.9 %train.1 = (bf16[1024,192]{1,0:T(8,128)(2,1)}, f32[8,128]{1,0:T(8,128)}) custom-call(s32[2,2]{1,0:T(2,128)} %keys.1, s32[2,2,4]{2,1,0:T(2,128)} %boxes.1, f32[2,2,32,128]{3,2,1,0:T(8,128)} %vel.1, f32[2,2,2,32,128]{4,3,2,1,0:T(8,128)} %tgt.1, f32[3,3,3,64]{3,2,1,0:T(4,128)} %bitcast.27, f32[9,5,4096]{2,1,0:T(8,128)} %bitcast.23, f32[5,2,64]{2,1,0:T(2,128)} %bitcast.29, ...), custom_call_target="tpu_custom_call" | custom-call | tf_op jit(solution)/shard_map/train/pallas_call | solution.py:1083
  191.7 0.0 copy-done.4
  191.7 0.0 copy-done
  191.7 0.0 copy-done.5
  191.7 0.0 copy-done.11
  191.7 0.0 copy-done.6
  191.8 0.0 copy-done.7
  191.8 0.0 copy-done.9
  191.8 0.0 copy-done.10
  191.8 0.0 copy-done.12
  191.8 0.0 copy-done.13
  191.8 0.0 copy-start.1
  191.8 1.3 copy-done.1
  193.1 0.0 copy-start.2
  193.1 1.3 copy-done.2
  194.4 0.0 copy-start.3
  194.4 1.0 copy-done.3
  195.4 0.0 copy-start.8
  195.4 0.7 copy-done.8
  196.1 3.4 %adam.1 = (f32[3,3,3,64]{3,2,1,0:T(4,128)}, f32[3,3,3,64]{3,2,1,0:T(4,128)}, f32[3,3,3,64]{3,2,1,0:T(4,128)}, f32[9,5,4096]{2,1,0:T(8,128)}, f32[9,5,4096]{2,1,0...) custom-call(bf16[1024,192]{1,0:T(8,128)(2,1)S(1)} %copy-done.3, ...), custom_call_target="tpu_custom_call" | custom-call | tf_op jit(solution)/shard_map/adam/pallas_call | solution.py:1237
  199.5 0.5 fusion
Async XLA Ops:
  0.7 191.0 %copy-start.4 = (f32[64,3,3,3]{0,3,2,1:T(4,128)S(1)}, f32[64,3,3,3]{0,3,2,1:T(4,128)}, u32[]{:S(2)}) copy-start(f32[64,3,3,3]{0,3,2,1:T(4,128)} %param.20) | copy-start | bytes 20740
  0.7 191.0 %copy-start = (f32[5,9,4096]{2,0,1:T(8,128)S(1)}, f32[5,9,4096]{2,0,1:T(8,128)}, u32[]{:S(2)}) copy-start(f32[5,9,4096]{2,0,1:T(8,128)} %param.21) | copy-start | bytes 2211844
  0.7 191.0 %copy-start.5 = (f32[2,5,64]{2,0,1:T(2,128)S(1)}, f32[2,5,64]{2,0,1:T(2,128)}, u32[]{:S(2)}) copy-start(f32[2,5,64]{2,0,1:T(2,128)} %param.22) | copy-start | bytes 7684
  0.7 191.0 %copy-start.11 = (f32[2,65]{1,0:T(2,128)S(1)}, f32[2,65]{1,0:T(2,128)}, u32[]{:S(2)}) copy-start(f32[2,65]{1,0:T(2,128)} %refs_9_.1) | copy-start | bytes 1564
  0.7 191.0 %copy-start.6 = (f32[64,3,3,3]{0,3,2,1:T(4,128)S(1)}, f32[64,3,3,3]{0,3,2,1:T(4,128)}, u32[]{:S(2)}) copy-start(f32[64,3,3,3]{0,3,2,1:T(4,128)} %param.24) | copy-start | bytes 20740
  0.7 191.0 %copy-start.7 = (f32[64,3,3,3]{0,3,2,1:T(4,128)S(1)}, f32[64,3,3,3]{0,3,2,1:T(4,128)}, u32[]{:S(2)}) copy-start(f32[64,3,3,3]{0,3,2,1:T(4,128)} %param.28) | copy-start | bytes 20740
  0.7 191.0 %copy-start.9 = (f32[2,5,64]{2,0,1:T(2,128)S(1)}, f32[2,5,64]{2,0,1:T(2,128)}, u32[]{:S(2)}) copy-start(f32[2,5,64]{2,0,1:T(2,128)} %param.26) | copy-start | bytes 7684
  0.7 191.0 %copy-start.10 = (f32[2,5,64]{2,0,1:T(2,128)S(1)}, f32[2,5,64]{2,0,1:T(2,128)}, u32[]{:S(2)}) copy-start(f32[2,5,64]{2,0,1:T(2,128)} %param.30) | copy-start | bytes 7684
  0.7 191.0 %copy-start.12 = (f32[2,65]{1,0:T(2,128)S(1)}, f32[2,65]{1,0:T(2,128)}, u32[]{:S(2)}) copy-start(f32[2,65]{1,0:T(2,128)} %refs_10_.1) | copy-start | bytes 1564
  0.8 191.0 %copy-start.13 = (f32[2,65]{1,0:T(2,128)S(1)}, f32[2,65]{1,0:T(2,128)}, u32[]{:S(2)}) copy-start(f32[2,65]{1,0:T(2,128)} %refs_11_.1) | copy-start | bytes 1564
  191.8 1.3 copy-start.1
  193.1 1.3 copy-start.2
  194.4 1.0 copy-start.3
  195.4 0.7 copy-start.8

commit v4 on v3

--- a/solution.py
+++ b/solution.py
@@ -31,10 +31,10 @@
 MESH = pl.DeviceIdType.MESH
 FULL_SLOT = {0: 0, 1: 1, 4: 2}
 HALF_SLOT = {2: 0, 3: 1}
-ACT_LINES = 32
-CONV_LINES = 32
-BAR_LINES = 16
-SUM_LINES = 32
+ACT_LINES = 64
+CONV_LINES = 64
+BAR_LINES = 32
+SUM_LINES = 64
 
 
 def nt_dot(a, b):
@@ -104,6 +104,22 @@
     return jnp.concatenate(
         [jnp.broadcast_to(x[g : g + 1], (CH // GROUPS, LANES)) for g in range(GROUPS)], axis=0
     )
+
+
+def gradient_lines(members):
+    groups = ((0,), (1, 2), (3, 4))
+    chunks, starts, at = [], [], []
+    start = 0
+    for group in groups:
+        place = start
+        for layer in group:
+            at.append(place)
+            place += 3 * CH
+        chunk = -(-(place - start) // (16 * members)) * 16
+        starts.append(start)
+        chunks.append(chunk)
+        start += chunk * members
+    return starts, chunks, at, start
 
 
 def train_kernel(
@@ -118,6 +134,7 @@
     norm_params,
     head,
     g_all,
+    small_out,
     scalars,
     meta,
     wf,
@@ -170,7 +187,6 @@
     st_recv,
     g_send,
     p_recv,
-    z_send,
     z_recv,
     m_plane,
     m_line,
@@ -212,6 +228,8 @@
 
     barrier = pltpu.get_barrier_semaphore()
     members = 2 * ranks
+    starts, chunks, line_at, all_lines = gradient_lines(members)
+    offsets = [sum(chunks[:k]) for k in range(3)]
     mine = core * ranks + row_at
 
     def plane_id(d):
@@ -242,34 +260,6 @@
         for k, value in enumerate(values):
             facts = jnp.where(line_is == k, value.astype(F32), facts)
         meta[j] = facts
-
-    pl.semaphore_wait(barrier, members + planes - 2)
-
-    def incoming(place):
-        at = pl.ds(pl.multiple_of(EDGE + place * tile, 8), tile)
-        here = pl.ds(pl.multiple_of(place * tile, 8), tile)
-        return u_ext.at[:, at, :], t_own.at[:, :, here, :], m_own.at[place]
-
-    place = lax.rem(row_at, 2)
-    for j in range(2):
-        to_batch, to_row = owner(2 * core + j, row_at // 2)
-        stays = (to_batch == batch_at) & (to_row == row_at)
-        for k, (src, dst) in enumerate(zip((vel.at[j], tgt.at[j], meta.at[j]), incoming(place))):
-
-            @pl.when(stays)
-            def _():
-                pltpu.make_async_copy(src, dst, in_local.at[k]).start()
-
-            @pl.when(jnp.logical_not(stays))
-            def _():
-                pltpu.make_async_remote_copy(
-                    src_ref=src,
-                    dst_ref=dst,
-                    send_sem=in_send.at[j, k],
-                    recv_sem=in_recv.at[place, k],
-                    device_id=(to_batch, to_row),
-                    device_id_type=MESH,
-                ).start()
 
     low_lanes = lane_of((CH // 2, LANES)) < CH
     for ky in range(3):
@@ -296,6 +286,34 @@
             first = jnp.where(low_lanes, left, pltpu.roll(mid, CH, 1))
             last = pltpu.roll(left, CH, 1)
             wb[k, at, :] = jnp.concatenate([first, last[:, :CH]], axis=1).astype(BF)
+    pl.semaphore_wait(barrier, members + planes - 2)
+
+    def incoming(place):
+        at = pl.ds(pl.multiple_of(EDGE + place * tile, 8), tile)
+        here = pl.ds(pl.multiple_of(place * tile, 8), tile)
+        return u_ext.at[:, at, :], t_own.at[:, :, here, :], m_own.at[place]
+
+    place = lax.rem(row_at, 2)
+    for j in range(2):
+        to_batch, to_row = owner(2 * core + j, row_at // 2)
+        stays = (to_batch == batch_at) & (to_row == row_at)
+        for k, (src, dst) in enumerate(zip((vel.at[j], tgt.at[j], meta.at[j]), incoming(place))):
+
+            @pl.when(stays)
+            def _():
+                pltpu.make_async_copy(src, dst, in_local.at[k]).start()
+
+            @pl.when(jnp.logical_not(stays))
+            def _():
+                pltpu.make_async_remote_copy(
+                    src_ref=src,
+                    dst_ref=dst,
+                    send_sem=in_send.at[j, k],
+                    recv_sem=in_recv.at[place, k],
+                    device_id=(to_batch, to_row),
+                    device_id_type=MESH,
+                ).start()
+
     small[...] = jnp.zeros_like(small)
     for ch in range(3):
         for ky in range(3):
@@ -483,6 +501,9 @@
 
     def for_blocks(count, size, body):
         size = min(size, count)
+        if size == count:
+            body(0, size)
+            return
 
         def step(i, carry):
             body(pl.multiple_of(i * size, size), size)
@@ -515,13 +536,15 @@
 
         def step(i, carry):
             sums, squares = carry
-            base = pl.multiple_of(i * size, size)
+            base = i * size
             for j, z in enumerate(rows_of(base, size)):
                 zbuf[base + j] = z
                 sums = sums + z
                 squares = squares + z * z
             return sums, squares
 
+        if size == count:
+            return step(0, (zero, zero))
         return lax.fori_loop(0, count // size, step, (zero, zero))
 
     def tap_rows(y, j, at):
@@ -766,7 +789,7 @@
         def block(base, size):
             g = beside([src[base + 1 + j] for j in range(size)])
             h = beside([kept[t, pl.ds(base + j, 3)].reshape(3 * CH, LANES) for j in range(size)])
-            gw[at * 3 * CH : (at + 1) * 3 * CH, :] += nt_dot(g, h)
+            gw[line_at[at] : line_at[at] + 3 * CH, :] += nt_dot(g, h)
 
         for_blocks(count, SUM_LINES, block)
 
@@ -792,14 +815,14 @@
             g = beside([sg[base + 1 + j] for j in range(size)])
             low = base // 2
             h = beside([skip[t, pl.ds(base + j, 3)].reshape(3 * CH, LANES) for j in range(size)])
-            gw[4 * 3 * CH : 5 * 3 * CH, :] += nt_dot(g, h)
+            gw[line_at[4] : line_at[4] + 3 * CH, :] += nt_dot(g, h)
             up = beside(
                 [
                     jnp.concatenate([h4[t, low + (j + ky - 1) // 2 + 1] for ky in range(3)], axis=0)
                     for j in range(size)
                 ]
             )
-            gw[3 * 3 * CH : 4 * 3 * CH, :] += nt_dot(g, up)
+            gw[line_at[3] : line_at[3] + 3 * CH, :] += nt_dot(g, up)
 
         for_blocks(rows, SUM_LINES, block)
 
@@ -825,6 +848,104 @@
             gw0[...] += nt_dot(g, x)
 
         for_blocks(rows, SUM_LINES, weights)
+
+    def chunk_at(p, which):
+        return pl.ds(pl.multiple_of(starts[p] + which * chunks[p], 16), chunks[p])
+
+    def strip(p):
+        return pl.ds(offsets[p], chunks[p])
+
+    def exchange_start(copies, count, *args):
+        def start(d, carry):
+            src, dst, sent, landed, peer = copies(d, *args)[0]
+            pltpu.make_async_remote_copy(
+                src_ref=src,
+                dst_ref=dst,
+                send_sem=sent,
+                recv_sem=landed,
+                device_id=peer,
+                device_id_type=MESH,
+            ).start()
+            return carry
+
+        lax.fori_loop(1, count, start, 0)
+
+    def exchange_finish(copies, count, *args):
+        def finish(d, carry):
+            (src, _, sent, _, _), (dst, landed) = copies(d, *args)
+            pltpu.make_async_copy(src, src, sent).wait()
+            pltpu.make_async_copy(dst, dst, landed).wait()
+            return carry
+
+        lax.fori_loop(1, count, finish, 0)
+
+    def around(d, here, count):
+        return lax.rem(here + d, count), lax.rem(here + count - d, count)
+
+    def chunk_plane(d, p):
+        other, source = around(d, mine, members)
+        send = (g_send.at[chunk_at(p, other)], p_recv.at[mine, strip(p)])
+        sems = (p_ss.at[p, d], p_rs.at[p, mine], plane_id(d))
+        return send + sems, (p_recv.at[source, strip(p)], p_rs.at[p, source])
+
+    def chunk_line(d, p):
+        other, source = around(d, level, planes)
+        block = z_recv.at[level, strip(p)]
+        sems = (z_ss.at[p, d], z_rs.at[p, level], line_id(d))
+        return (block, block) + sems, (z_recv.at[source, strip(p)], z_rs.at[p, source])
+
+    def chunk_back(d, p):
+        other, source = around(d, mine, members)
+        block = g_all.at[chunk_at(p, mine)]
+        sems = (p_ss.at[3 + p, d], p_rs.at[3 + p, mine], plane_id(d))
+        return (block, block) + sems, (g_all.at[chunk_at(p, source)], p_rs.at[3 + p, source])
+
+    def small_plane(d):
+        other, source = around(d, mine, members)
+        block = m_plane.at[mine]
+        sems = (p_ss.at[6, d], p_rs.at[6, mine], plane_id(d))
+        return (block, block) + sems, (m_plane.at[source], p_rs.at[6, source])
+
+    def small_line(d):
+        other, source = around(d, level, planes)
+        block = m_line.at[level]
+        sems = (z_ss.at[3, d], z_rs.at[3, level], line_id(d))
+        return (block, block) + sems, (m_line.at[source], z_rs.at[3, source])
+
+    def plane_start(p):
+        at = slice(starts[p], starts[p] + chunks[p] * members)
+        if p == 1:
+            gw[at, :] = 0.5 * gw[at, :]
+        g_send[at, :] = gw[at, :].astype(BF)
+        exchange_start(chunk_plane, members, p)
+
+    def plane_finish(p):
+        exchange_finish(chunk_plane, members, p)
+
+        def add(d, total):
+            return total + p_recv[lax.rem(mine + d, members), strip(p), :].astype(F32)
+
+        total = lax.fori_loop(1, members, add, gw[chunk_at(p, mine), :])
+        z_recv[level, strip(p), :] = total.astype(BF)
+        exchange_start(chunk_line, planes, p)
+
+    def line_finish(p):
+        exchange_finish(chunk_line, planes, p)
+
+        def add(k, total):
+            return total + z_recv[k, strip(p), :].astype(F32)
+
+        total = lax.fori_loop(0, planes, add, jnp.zeros((chunks[p], 3 * CH), F32))
+        g_all[chunk_at(p, mine), :] = total.astype(BF)
+        exchange_start(chunk_back, members, p)
+
+    def gather_finish(p):
+        exchange_finish(chunk_back, members, p)
+
+    def at_last(t, what, p):
+        @pl.when(t == 0)
+        def _():
+            what(p)
 
     def w_args():
         return (
@@ -877,6 +998,7 @@
         bars_last(t)
         sums_start(3)
         weight_sums_last(t)
+        at_last(t, plane_start, 2)
         second_pass(3, t, half, xh_half, 1, sgh, 2)
 
         def into_two(base, size, bars):
@@ -889,7 +1011,7 @@
         second_pass(2, t, half, xh_half, 0, sgh, 2)
 
         def into_one(base, size, bars):
-            at = pl.multiple_of(2 * base, 2)
+            at = 2 * base
             for c in channel_blocks():
                 direct = skip_bar[pl.ds(at, 2 * size), c, :].reshape(size, 2, 16, LANES)
                 total = (direct + 0.25 * bars[:, None, c, :]).reshape(2 * size, 16, LANES)
@@ -898,6 +1020,8 @@
         bars_of(1, half, sgh, into_one)
         sums_start(1)
         weight_sums(1, t, half, sgh, pooled)
+        at_last(t, plane_finish, 2)
+        at_last(t, plane_start, 1)
         second_pass(1, t, rows, xh_full, 1, sg, 1)
 
         def into_zero(base, size, bars):
@@ -907,157 +1031,72 @@
         bars_of(0, rows, sg, into_zero)
         sums_start(0)
         weight_sums(0, t, rows, sg, h1)
+        at_last(t, plane_start, 0)
         second_pass(0, t, rows, xh_full, 0, sg, 0)
-        taps_first()
-        for c in range(2):
-            columns = []
-            for kx in range(3):
-                total = jnp.zeros((rows, LANES), F32)
-                for ky in range(3):
-                    total = total + taps[pl.ds(2 - ky, rows), 16 * ky + 3 * kx + c, :]
-                columns.append(total)
-            u_bar[c] += from_right(columns[0], 1) + columns[1] + from_left(columns[2], 1)
 
         @pl.when(t > 0)
         def _():
+            taps_first()
+            for c in range(2):
+                columns = []
+                for kx in range(3):
+                    total = jnp.zeros((rows, LANES), F32)
+                    for ky in range(3):
+                        total = total + taps[pl.ds(2 - ky, rows), 16 * ky + 3 * kx + c, :]
+                    columns.append(total)
+                u_bar[c] += from_right(columns[0], 1) + columns[1] + from_left(columns[2], 1)
             pull_start(t - 1)
 
+        at_last(t, plane_finish, 1)
         weight_sums_first(t)
+        at_last(t, line_finish, 2)
         return carry
 
     pull_start(jnp.int32(STEPS - 1))
     lax.fori_loop(0, STEPS, backward_step, 0)
 
-    mid_rows = (LAYERS + 1) * 3 * CH
-    gw[3 * CH : 9 * CH, :] = 0.5 * gw[3 * CH : 9 * CH, :]
-    lane = lane_of((CH, 3 * CH))
-    rest = jnp.concatenate([gw0[...], jnp.zeros((CH, 3 * CH - 48), F32)], axis=1)
+    lane = lane_of((CH, CH))
+    small_sums = jnp.concatenate([gw0[...], jnp.zeros((CH, CH - 48), F32)], axis=1)
     for which in range(2):
         for layer in range(LAYERS + 1):
             column = jnp.sum(gnorm[which, layer], axis=1, keepdims=True)
             if layer in HALF_SLOT:
                 column = 0.5 * column
-            rest = jnp.where(lane == 48 + 5 * which + layer, column, rest)
+            small_sums = jnp.where(lane == 48 + 5 * which + layer, column, small_sums)
     for c in range(2):
-        rest = jnp.where(lane == 58 + c, ghead[:, c : c + 1], rest)
-    gw[mid_rows : mid_rows + CH, :] = rest
-    g_send[...] = gw[...].astype(BF)
-    chunk = gw.shape[0] // members
-    piece = chunk // planes
-
-    def chunk_at(which):
-        return pl.ds(pl.multiple_of(which * chunk, 16), chunk)
-
-    def piece_at(which):
-        return pl.ds(pl.multiple_of(which * piece, 16), piece)
-
-    def part_at(which):
-        return pl.ds(pl.multiple_of(mine * chunk + which * piece, 16), piece)
-
+        small_sums = jnp.where(lane == 58 + c, ghead[:, c : c + 1], small_sums)
     m_plane[mine] = jnp.concatenate(
-        [jnp.sum(misc[k], axis=0, keepdims=True) for k in range(4)] + [jnp.zeros((4, LANES), F32)],
+        [jnp.sum(misc[k], axis=0, keepdims=True) for k in range(4)]
+        + [jnp.zeros((4, LANES), F32), beside([small_sums[: CH // 2], small_sums[CH // 2 :]])],
         axis=0,
     )
-
-    def plane_copies(d):
-        other = lax.rem(mine + d, members)
-        source = lax.rem(mine + members - d, members)
-        sends = [
-            (g_send.at[chunk_at(other)], p_recv.at[mine], p_ss.at[0, d], p_rs.at[0, mine]),
-            (m_plane.at[mine], m_plane.at[mine], p_ss.at[1, d], p_rs.at[1, mine]),
-        ]
-        lands = [
-            (p_recv.at[source], p_rs.at[0, source]),
-            (m_plane.at[source], p_rs.at[1, source]),
-        ]
-        return plane_id(d), sends, lands
-
-    def line_copies(d):
-        other = lax.rem(level + d, planes)
-        source = lax.rem(level + planes - d, planes)
-        sends = [
-            (z_send.at[piece_at(other)], z_recv.at[level], z_ss.at[0, d], z_rs.at[0, level]),
-            (m_line.at[level], m_line.at[level], z_ss.at[1, d], z_rs.at[1, level]),
-        ]
-        lands = [
-            (z_recv.at[source], z_rs.at[0, source]),
-            (m_line.at[source], z_rs.at[1, source]),
-        ]
-        return line_id(d), sends, lands
-
-    def line_gather(d):
-        source = lax.rem(level + planes - d, planes)
-        sends = [(g_all.at[part_at(level)], g_all.at[part_at(level)], z_ss.at[2, d], z_rs.at[2, level])]
-        lands = [(g_all.at[part_at(source)], z_rs.at[2, source])]
-        return line_id(d), sends, lands
-
-    def plane_gather(d):
-        source = lax.rem(mine + members - d, members)
-        sends = [(g_all.at[chunk_at(mine)], g_all.at[chunk_at(mine)], p_ss.at[2, d], p_rs.at[2, mine])]
-        lands = [(g_all.at[chunk_at(source)], p_rs.at[2, source])]
-        return plane_id(d), sends, lands
-
-    def exchange(copies, count):
-        def start(d, carry):
-            peer, sends, lands = copies(d)
-            for src, dst, sent, landed in sends:
-                pltpu.make_async_remote_copy(
-                    src_ref=src,
-                    dst_ref=dst,
-                    send_sem=sent,
-                    recv_sem=landed,
-                    device_id=peer,
-                    device_id_type=MESH,
-                ).start()
-            return carry
-
-        def finish(d, carry):
-            peer, sends, lands = copies(d)
-            for src, dst, sent, landed in sends:
-                pltpu.make_async_copy(src, src, sent).wait()
-            for dst, landed in lands:
-                pltpu.make_async_copy(dst, dst, landed).wait()
-            return carry
-
-        lax.fori_loop(1, count, start, 0)
-        lax.fori_loop(1, count, finish, 0)
-
-    exchange(plane_copies, members)
-    own_chunk = chunk_at(mine)
-
-    def add_chunk(d, carry):
-        gw[own_chunk, :] += p_recv[lax.rem(mine + d, members)].astype(F32)
-        return carry
-
-    lax.fori_loop(1, members, add_chunk, 0)
-    z_send[...] = gw[own_chunk, :].astype(BF)
-    m_line[level] = lax.fori_loop(
-        0, members, lambda k, total: total + m_plane[k], jnp.zeros((8, LANES), F32)
-    )
-    exchange(line_copies, planes)
-
-    def add_piece(d, total):
-        return total + z_recv[lax.rem(level + d, planes)].astype(F32)
-
-    total = lax.fori_loop(1, planes, add_piece, gw[part_at(level), :])
-    g_all[part_at(level), :] = total.astype(BF)
-    exchange(line_gather, planes)
-    exchange(plane_gather, members)
-
-    totals = lax.fori_loop(
-        0, planes, lambda k, total: total + m_line[k], jnp.zeros((8, LANES), F32)
-    )
-    totals = jnp.broadcast_to(jnp.sum(totals, axis=1, keepdims=True), (8, LANES))
+    exchange_start(small_plane, members)
+    plane_finish(0)
+    line_finish(1)
+    exchange_finish(small_plane, members)
+    no_sums = jnp.zeros(m_line.shape[1:], F32)
+    m_line[level] = lax.fori_loop(0, members, lambda k, total: total + m_plane[k], no_sums)
+    exchange_start(small_line, planes)
+    line_finish(0)
+    exchange_finish(small_line, planes)
+    for p in (2, 1, 0):
+        gather_finish(p)
+
+    totals = lax.fori_loop(0, planes, lambda k, total: total + m_line[k], no_sums)
+    small_out[...] = totals[8:]
+    small_square = jnp.sum(sublanes(totals[8:] * totals[8:]), axis=0, keepdims=True)
+    small_square = jnp.sum(small_square, axis=1, keepdims=True)
+    totals = jnp.broadcast_to(jnp.sum(totals[:8], axis=1, keepdims=True), (8, LANES))
 
     def squares(i, total):
         at = pl.ds(pl.multiple_of(i * 64, 64), 64)
         block = g_all[at, :].astype(F32)
         return total + jnp.sum((block * block).reshape(8, 8, 3 * CH), axis=0)
 
-    square = lax.fori_loop(0, gw.shape[0] // 64, squares, jnp.zeros((8, 3 * CH), F32))
+    square = lax.fori_loop(0, all_lines // 64, squares, jnp.zeros((8, 3 * CH), F32))
     square = jnp.sum(jnp.sum(square, axis=0, keepdims=True), axis=1, keepdims=True)
     count = totals[1:2]
-    raw = square + totals[2:3] * totals[2:3] + totals[3:4] * totals[3:4]
+    raw = square + small_square + totals[2:3] * totals[2:3] + totals[3:4] * totals[3:4]
     norm = jnp.sqrt(raw) / count
     factor = jnp.minimum(1.0, CLIP_NORM / norm) / count
     scalars[...] = jnp.concatenate([totals[:4], norm, factor, totals[6:]], axis=0)
@@ -1067,9 +1106,7 @@
     ranks = lax.axis_size("rows")
     planes = lax.axis_size("batch") // 2
     members = 2 * ranks
-    unit = 16 * members * planes
-    lines = -(-((LAYERS + 1) * 3 * CH + CH) // unit) * unit
-    chunk = lines // members
+    starts, chunks, line_at, lines = gradient_lines(members)
     parts = ranks // 2
     tile = velocity.shape[2]
     rows, half, ext = 2 * tile, tile, 2 * tile + 2 * EDGE
@@ -1084,10 +1121,11 @@
         functools.partial(train_kernel, ranks, planes),
         out_shape=(
             jax.ShapeDtypeStruct((lines, 3 * CH), BF),
+            jax.ShapeDtypeStruct((CH // 2, LANES), F32),
             jax.ShapeDtypeStruct((8, LANES), F32),
         ),
         in_specs=[smem] * 2 + [vmem] * 6,
-        out_specs=(vmem,) * 2,
+        out_specs=(vmem,) * 3,
         scratch_shapes=[
             pltpu.VMEM((2, 16, LANES), F32),
             pltpu.VMEM((LAYERS + 1, 3 * CH, 3 * CH), BF),
@@ -1139,11 +1177,10 @@
             pltpu.VMEM((10, 16, LANES), F32),
             pltpu.VMEM((10, parts - 1, 16, LANES), F32),
             pltpu.VMEM((lines, 3 * CH), BF),
-            pltpu.VMEM((members, chunk, 3 * CH), BF),
-            pltpu.VMEM((chunk, 3 * CH), BF),
-            pltpu.VMEM((planes, chunk // planes, 3 * CH), BF),
-            pltpu.VMEM((members, 8, LANES), F32),
-            pltpu.VMEM((planes, 8, LANES), F32),
+            pltpu.VMEM((members, sum(chunks), 3 * CH), BF),
+            pltpu.VMEM((planes, sum(chunks), 3 * CH), BF),
+            pltpu.VMEM((members, 8 + CH // 2, LANES), F32),
+            pltpu.VMEM((planes, 8 + CH // 2, LANES), F32),
             pltpu.SemaphoreType.DMA((2, 3)),
             pltpu.SemaphoreType.DMA((2, 3)),
             pltpu.SemaphoreType.DMA((3,)),
@@ -1151,10 +1188,10 @@
             pltpu.SemaphoreType.DMA((13, 2)),
             pltpu.SemaphoreType.DMA((10, parts - 1)),
             pltpu.SemaphoreType.DMA((10, parts - 1)),
-            pltpu.SemaphoreType.DMA((3, members)),
-            pltpu.SemaphoreType.DMA((3, members)),
-            pltpu.SemaphoreType.DMA((3, planes)),
-            pltpu.SemaphoreType.DMA((3, planes)),
+            pltpu.SemaphoreType.DMA((7, members)),
+            pltpu.SemaphoreType.DMA((7, members)),
+            pltpu.SemaphoreType.DMA((4, planes)),
+            pltpu.SemaphoreType.DMA((4, planes)),
         ],
         compiler_params=pltpu.CompilerParams(
             collective_id=0, has_side_effects=True, vmem_limit_bytes=60 * 2**20
@@ -1163,11 +1200,11 @@
     )(*args)
 
 
-def adam_kernel(g_all, scalars, *refs):
+def adam_kernel(line_at, g_all, small, scalars, *refs):
     olds = [refs[3 * k : 3 * k + 3] for k in range(4)]
     news = [refs[12 + 3 * k : 15 + 3 * k] for k in range(4)]
-    low_in, low_mid, low_head, wide, turned, lines = refs[24:]
-    factor = scalars[5:6, :]
+    low_in, low_mid, low_head, loss, cells, norm, wide, turned, lines = refs[24:]
+    factor = scalars[5, 0]
     at_step = pl.program_id(0)
 
     def update(which, at, g, low=None):
@@ -1183,15 +1220,19 @@
         if low is not None:
             low[at] = weight.astype(BF)
 
-    mid_rows = (LAYERS + 1) * 3 * CH
-
     @pl.when(at_step == 0)
     def _():
-        wide[0] = g_all[:mid_rows, :LANES].astype(F32) * factor
-        tail = g_all[:mid_rows, LANES:].astype(F32) * factor[:, :CH]
-        wide[1] = jnp.concatenate([tail, jnp.zeros_like(tail)], axis=1)
-        rest = g_all[mid_rows : mid_rows + CH, :LANES].astype(F32) * factor
-        rest = jnp.concatenate([rest, jnp.zeros_like(rest)], axis=0)
+        loss[0, 0] = scalars[0, 0]
+        cells[0, 0] = scalars[1, 0]
+        norm[0, 0] = scalars[4, 0]
+        for k in range(LAYERS + 1):
+            at = pl.ds(line_at[k], 3 * CH)
+            to = pl.ds(k * 3 * CH, 3 * CH)
+            wide[0, to, :] = g_all[at, :LANES].astype(F32) * factor
+            tail = g_all[at, LANES:].astype(F32) * factor
+            wide[1, to, :] = jnp.concatenate([tail, jnp.zeros_like(tail)], axis=1)
+        rest = small[...] * factor
+        rest = jnp.concatenate([rest, pltpu.roll(rest, CH, 1), jnp.zeros((CH, LANES), F32)], axis=0)
         turned[...] = rest.T
         for ch in range(3):
             for ky in range(3):
@@ -1200,11 +1241,12 @@
         for layer in range(LAYERS + 1):
             g = turned[pl.ds(48 + layer, 2, LAYERS + 1), :]
             update(2, (layer,), g[:, :CH])
-        bias = scalars[2:4, :] * factor
-        g = jnp.where(lax.broadcasted_iota(jnp.int32, (2, LANES), 1) < CH, turned[58:60, :], bias)
+        line_is = lax.broadcasted_iota(jnp.int32, (2, LANES), 0)
+        bias = jnp.where(line_is == 0, scalars[2, 0] * factor, scalars[3, 0] * factor)
+        g = jnp.where(lane_of((2, LANES)) < CH, turned[58:60, :], bias)
         update(3, (slice(None),), g[:, : CH + 1], low_head)
 
-    low_lanes = lax.broadcasted_iota(jnp.int32, (CH // 2, LANES), 1) < CH
+    low_lanes = lane_of((CH // 2, LANES)) < CH
     for ky in range(3):
 
         @pl.when(at_step == ky)
@@ -1227,7 +1269,9 @@
         update(1, (kx,), g, low_mid)
 
 
-def adam(g_all, scalars, params, moments, seconds):
+def adam(g_all, small, scalars, params, moments, seconds):
+    line_at = gradient_lines(2 * lax.axis_size("rows"))[2]
+    smem = pl.BlockSpec(memory_space=pltpu.SMEM)
     shapes = [w.shape for w in params]
     whole = lambda shape: pl.BlockSpec(shape, lambda i: (0,) * len(shape))
     mid = pl.BlockSpec((3,) + shapes[1][1:], lambda i: (i, 0, 0))
@@ -1235,20 +1279,23 @@
     states = [x for group in zip(params, moments, seconds) for x in group]
     lows = (0, 1, 3)
     return pl.pallas_call(
-        adam_kernel,
+        functools.partial(adam_kernel, line_at),
         grid=(3,),
         out_shape=tuple(jax.ShapeDtypeStruct(x.shape, F32) for x in states)
-        + tuple(jax.ShapeDtypeStruct(shapes[k], BF) for k in lows),
-        in_specs=[whole(g_all.shape), whole(scalars.shape)] + [spec(k // 3) for k in range(12)],
-        out_specs=tuple(spec(k // 3) for k in range(12)) + tuple(spec(k) for k in lows),
+        + tuple(jax.ShapeDtypeStruct(shapes[k], BF) for k in lows)
+        + (jax.ShapeDtypeStruct((1, 1), F32),) * 3,
+        in_specs=[whole(g_all.shape), whole(small.shape), smem] + [spec(k // 3) for k in range(12)],
+        out_specs=tuple(spec(k // 3) for k in range(12))
+        + tuple(spec(k) for k in lows)
+        + (smem,) * 3,
         scratch_shapes=[
             pltpu.VMEM((2, (LAYERS + 1) * 3 * CH, LANES), F32),
             pltpu.VMEM((LANES, LANES), F32),
             pltpu.VMEM((3, CH // 2, 8, LANES), F32),
         ],
-        compiler_params=pltpu.CompilerParams(vmem_limit_bytes=40 * 2**20),
+        compiler_params=pltpu.CompilerParams(vmem_limit_bytes=60 * 2**20),
         name="adam",
-    )(g_all, scalars, *states)
+    )(g_all, small, scalars, *states)
 
 
 def in_order(group):
@@ -1292,10 +1339,10 @@
     params = in_order((w_in, w_mid, norm_params, head_params))
     moments = in_order((m_in, m_mid, m_norm, m_head))
     seconds = in_order((v_in, v_mid, v_norm, v_head))
-    g_all, scalars = train(keyframes, boxes, velocity, targets, *params)
-    result = adam(g_all, scalars, params, moments, seconds)
+    g_all, small, scalars = train(keyframes, boxes, velocity, targets, *params)
+    result = adam(g_all, small, scalars, params, moments, seconds)
     new_w, new_m, new_v = (out_of_order(result[k:12:3]) for k in range(3))
-    low_in, low_mid, low_head = result[12:]
+    low_in, low_mid, low_head, loss, cells, norm = result[12:]
     return (
         *new_w,
         *new_m,
@@ -1303,9 +1350,9 @@
         jnp.transpose(low_in, (3, 0, 1, 2)),
         jnp.transpose(low_mid, (1, 0, 2)),
         low_head,
-        scalars[0, 0],
-        scalars[1, 0],
-        scalars[4, 0],
+        loss.reshape(()),
+        cells.reshape(()),
+        norm.reshape(()),
     )
 
 

time: 200 us -> 178 us (0.89)
  Pallas kernels: 194 us -> 177 us
  local copies, waits for them, and re-layouts: 4.81 us -> 0 us
    pallas_call x1, Pallas kernels: 191 us -> 171 us  [train(): pl.pallas_call(functools.partial(train_kernel, ranks, planes), out_shape=...]
    unnamed x28 -> x0, local copies, waits for them, and re-layouts: 4.29 us -> none
    pallas_call x1, Pallas kernels: 3.39 us -> 6.29 us  [adam(): pl.pallas_call(functools.partial(adam_kernel, line_at), grid=(3,), out_sh...]
where the time goes in v4:
time: 178 us
  Pallas kernels  177 us (99%)
    pallas_call x1, Pallas kernels, train(): pl.pallas_call(functools.partial(train_kernel, ranks, planes), out_shape=...  171 us
    pallas_call x1, Pallas kernels, adam(): pl.pallas_call(functools.partial(adam_kernel, line_at), grid=(3,), out_sh...  6.29 us

profile of v4, /device:TPU:0, one launch (start us, length us, event | category | flops | bytes accessed | tf_op | source)
XLA Modules:
  0.0 178.1 jit_solution(9092983276269376844)
XLA Ops:
  0.7 171.0 %train.1 = (bf16[1024,192]{1,0:T(8,128)(2,1)}, f32[32,128]{1,0:T(8,128)}, f32[8,128]{1,0:T(8,128)}) custom-call(s32[2,2]{1,0:T(2,128)} %keys.1, s32[2,2,4]{2,1,0:T(2,128)} %boxes.1, f32[2,2,32,128]{3,2,1,0:T(8,128)} %vel.1, f32[2,2,2,32,128]{4,3,2,1,0:T(8,128)} %tgt.1, f32[3,3,3,64]{3,2,1,0:T(4,128)} %bitcast.27, f32[9,5,4096]{2,1,0:T(8,128)} %bitcast.23, ...), custom_call_target="tpu_custom_call" | custom-call | tf_op jit(solution)/shard_map/train/pallas_call | solution.py:1120
  171.7 6.3 %adam.1 = (f32[3,3,3,64]{3,2,1,0:T(4,128)}, f32[3,3,3,64]{3,2,1,0:T(4,128)}, f32[3,3,3,64]{3,2,1,0:T(4,128)}, f32[9,5,4096]{2,1,0:T(8,128)}, f32[9,5,4096]{2,1,0...) custom-call(bf16[1024,192]{1,0:T(8,128)(2,1)} %get-tuple-element.39., ...), custom_call_target="tpu_custom_call" | custom-call | tf_op jit(solution)/shard_map/adam/pallas_call | solution.py:1281

commit v5 on v4

--- a/solution.py
+++ b/solution.py
@@ -162,6 +162,8 @@
     s0b,
     q_ext,
     u_kept,
+    q_edge,
+    f_edge,
     w_ext,
     u_bar,
     frows,
@@ -221,6 +223,9 @@
     q_ext[...] = jnp.zeros_like(q_ext)
     w_ext[...] = jnp.zeros_like(w_ext)
     g_halo[...] = jnp.zeros_like(g_halo)
+    for count, shifted in ((rows, sg), (half, sgh)):
+        for at in (0, count + 1):
+            shifted[at] = jnp.zeros((3 * CH, LANES), BF)
     for kept, count in ((h1, rows), (skip, rows), (pooled, half), (h3, half), (h4, half)):
         for t in range(STEPS):
             kept[t, 0] = jnp.zeros((CH, LANES), BF)
@@ -294,10 +299,10 @@
         return u_ext.at[:, at, :], t_own.at[:, :, here, :], m_own.at[place]
 
     place = lax.rem(row_at, 2)
-    for j in range(2):
+    for j, k in ((0, 0), (1, 0), (0, 2), (1, 2), (0, 1), (1, 1)):
         to_batch, to_row = owner(2 * core + j, row_at // 2)
         stays = (to_batch == batch_at) & (to_row == row_at)
-        for k, (src, dst) in enumerate(zip((vel.at[j], tgt.at[j], meta.at[j]), incoming(place))):
+        for src, dst in [((vel, tgt, meta)[k].at[j], incoming(place)[k])]:
 
             @pl.when(stays)
             def _():
@@ -338,85 +343,114 @@
             norms[which, layer] = jnp.broadcast_to(turned[:, at : at + 1], (CH, LANES))
         bias[which] = jnp.broadcast_to(head[which : which + 1, CH : CH + 1], (1, LANES))
 
-    for j in range(2):
-        to_batch, to_row = owner(2 * core + j, row_at // 2)
-        stays = (to_batch == batch_at) & (to_row == row_at)
-        for k, src in enumerate((vel.at[j], tgt.at[j], meta.at[j])):
-
-            @pl.when(stays)
-            def _():
-                pltpu.make_async_copy(src, src, in_local.at[k]).wait()
-
-            @pl.when(jnp.logical_not(stays))
-            def _():
-                pltpu.make_async_copy(src, src, in_send.at[j, k]).wait()
-
-    for i in range(2):
-        from_batch = plane + sample // 2
-        from_row = 2 * part + i
-        stays = (from_batch == batch_at) & (from_row == row_at)
-        for k, dst in enumerate(incoming(i)):
-
-            @pl.when(jnp.logical_not(stays))
-            def _():
-                pltpu.make_async_copy(dst, dst, in_recv.at[i, k]).wait()
+    def arrive(which):
+        for i in range(2):
+            from_batch = plane + sample // 2
+            from_row = 2 * part + i
+            stays = (from_batch == batch_at) & (from_row == row_at)
+            for k, dst in enumerate(incoming(i)):
+                if k not in which:
+                    continue
+
+                @pl.when(jnp.logical_not(stays))
+                def _():
+                    pltpu.make_async_copy(dst, dst, in_recv.at[i, k]).wait()
+
+    def leave(which):
+        for j in range(2):
+            to_batch, to_row = owner(2 * core + j, row_at // 2)
+            stays = (to_batch == batch_at) & (to_row == row_at)
+            for k, src in enumerate((vel.at[j], tgt.at[j], meta.at[j])):
+                if k not in which:
+                    continue
+
+                @pl.when(stays)
+                def _():
+                    pltpu.make_async_copy(src, src, in_local.at[k]).wait()
+
+                @pl.when(jnp.logical_not(stays))
+                def _():
+                    pltpu.make_async_copy(src, src, in_send.at[j, k]).wait()
+
+    leave((0, 2))
+    arrive((0, 2))
 
     has_prev = part > 0
     has_next = part < parts - 1
     prev_id = owner(sample, jnp.maximum(part - 1, 0))
     next_id = owner(sample, jnp.minimum(part + 1, parts - 1))
 
-    def halo_copies(slot, low_src, high_src, top_dst, bottom_dst):
-        to_prev = pltpu.make_async_remote_copy(
-            src_ref=low_src,
-            dst_ref=bottom_dst,
+    two = parts == 2
+    near = 1 - part
+
+    def halo_copy(slot, src, dst, side):
+        return pltpu.make_async_remote_copy(
+            src_ref=src(side),
+            dst_ref=dst(1 - side),
+            send_sem=halo_send.at[slot, side],
+            recv_sem=halo_recv.at[slot, side],
+            device_id=(prev_id, next_id)[side],
+            device_id_type=MESH,
+        )
+
+    def only_copy(slot, src, dst):
+        return pltpu.make_async_remote_copy(
+            src_ref=src(near),
+            dst_ref=dst(part),
             send_sem=halo_send.at[slot, 0],
             recv_sem=halo_recv.at[slot, 0],
-            device_id=prev_id,
+            device_id=owner(sample, near),
             device_id_type=MESH,
         )
-        to_next = pltpu.make_async_remote_copy(
-            src_ref=high_src,
-            dst_ref=top_dst,
-            send_sem=halo_send.at[slot, 1],
-            recv_sem=halo_recv.at[slot, 1],
-            device_id=next_id,
-            device_id_type=MESH,
-        )
-        return to_prev, to_next
-
-    def halo_start(*args):
-        to_prev, to_next = halo_copies(*args)
+
+    def halo_start(slot, src, dst):
+        if two:
+            only_copy(slot, src, dst).start()
+            return
 
         @pl.when(has_prev)
         def _():
-            to_prev.start()
+            halo_copy(slot, src, dst, 0).start()
 
         @pl.when(has_next)
         def _():
-            to_next.start()
-
-    def halo_wait(*args):
-        to_prev, to_next = halo_copies(*args)
+            halo_copy(slot, src, dst, 1).start()
+
+    def halo_wait(slot, src, dst):
+        if two:
+            only_copy(slot, src, dst).wait_send()
+            landed = dst(near)
+            pltpu.make_async_copy(landed, landed, halo_recv.at[slot, 0]).wait()
+            return
 
         @pl.when(has_prev)
         def _():
-            to_prev.wait_send()
-            to_next.wait_recv()
+            halo_copy(slot, src, dst, 0).wait_send()
+            halo_copy(slot, src, dst, 1).wait_recv()
 
         @pl.when(has_next)
         def _():
-            to_next.wait_send()
-            to_prev.wait_recv()
+            halo_copy(slot, src, dst, 1).wait_send()
+            halo_copy(slot, src, dst, 0).wait_recv()
+
+    def edge_lines(count):
+        return [(0, near * count)] if two else [(0, 0), (1, count)]
+
+    def edge_source(slot):
+        return lambda side: edges.at[slot, 0 if two else side]
+
+    def ext_args(slot, ref):
+        def lines_at(start):
+            return ref.at[:, pl.ds(pl.multiple_of(start, 8), EDGE), :]
+
+        return (
+            slot,
+            lambda side: lines_at(EDGE + side * (rows - EDGE)),
+            lambda side: lines_at(side * (rows + EDGE)),
+        )
 
     def ext_halo(slot, ref):
-        args = (
-            slot,
-            ref.at[:, pl.ds(EDGE, EDGE), :],
-            ref.at[:, pl.ds(rows, EDGE), :],
-            ref.at[:, pl.ds(0, EDGE), :],
-            ref.at[:, pl.ds(rows + EDGE, EDGE), :],
-        )
+        args = ext_args(slot, ref)
         halo_start(*args)
         halo_wait(*args)
 
@@ -495,9 +529,12 @@
     FORWARD = (0, 1, 2)
     BACKWARD = (2, 1, 0)
 
-    def spread_halo(dst, lines, count, by, order):
-        for at, line in ((0, lines[0]), (count + 1, lines[1])):
-            put_shifted(dst, at, slice(0, CH), line, by, order)
+    def halo_sides():
+        return [near] if two else [0, 1]
+
+    def spread_halo(dst, line_of, count, by, order):
+        for side in halo_sides():
+            put_shifted(dst, side * (count + 1), slice(0, CH), line_of(side), by, order)
 
     def for_blocks(count, size, body):
         size = min(size, count)
@@ -573,9 +610,9 @@
         return result
 
     def finish_plain(t, layer, count, kept, xh, xh_at, dst, by, slot):
-        for which, line in enumerate((0, count - 1)):
+        for which, line in edge_lines(count - 1):
             edges[slot, which] = activate(zbuf[line], slice(0, CH))[1].astype(BF)
-        args = (slot, edges.at[slot, 0], edges.at[slot, 1], kept.at[t, 0], kept.at[t, count + 1])
+        args = (slot, edge_source(slot), lambda side: kept.at[t, side * (count + 1)])
         halo_start(*args)
 
         def block(base, size):
@@ -589,7 +626,7 @@
 
         for_blocks(count, ACT_LINES, block)
         halo_wait(*args)
-        spread_halo(dst, (kept[t, 0], kept[t, count + 1]), count, by, FORWARD)
+        spread_halo(dst, lambda side: kept[t, side * (count + 1)], count, by, FORWARD)
 
     def pool_pairs(low, size):
         pairs = jnp.concatenate(
@@ -598,12 +635,12 @@
         return nn_dot(pairs, pool_mat[...]).astype(BF).reshape(size // 2, CH, 3 * LANES)
 
     def finish_skip(t):
-        for which, line in enumerate((0, rows - 2)):
+        for which, line in edge_lines(rows - 2):
             low = activate(zbuf[pl.ds(line, 2)], slice(0, CH))[1].astype(BF)
-            edges[1, which] = low[which]
             edges[2, which] = pool_pairs(low, 2)[0, :, LANES : 2 * LANES]
-        skip_args = (1, edges.at[1, 0], edges.at[1, 1], skip.at[t, 0], skip.at[t, rows + 1])
-        pool_args = (2, edges.at[2, 0], edges.at[2, 1], pooled.at[t, 0], pooled.at[t, half + 1])
+            edges[1, which] = jnp.where(part == 0, low[1], low[0]) if two else low[which]
+        skip_args = (1, edge_source(1), lambda side: skip.at[t, side * (rows + 1)])
+        pool_args = (2, edge_source(2), lambda side: pooled.at[t, side * (half + 1)])
         halo_start(*pool_args)
         halo_start(*skip_args)
 
@@ -626,10 +663,26 @@
         for_blocks(rows, ACT_LINES, block)
         halo_wait(*pool_args)
         halo_wait(*skip_args)
-        spread_halo(sgh, (pooled[t, 0], pooled[t, half + 1]), half, 2, FORWARD)
-        spread_halo(sg, (skip[t, 0], skip[t, rows + 1]), rows, 1, FORWARD)
+        spread_halo(sgh, lambda side: pooled[t, side * (half + 1)], half, 2, FORWARD)
+        spread_halo(sg, lambda side: skip[t, side * (rows + 1)], rows, 1, FORWARD)
+
+    def push_args(t):
+        source, target = ext_args(11, q_ext.at[t])[1:]
+        return (11, (lambda side: q_edge) if two else source, target)
 
     def finish_last(t):
+        if two:
+            line = pl.multiple_of(near * (rows - EDGE), EDGE)
+            h = activate(zbuf[pl.ds(line, EDGE)], slice(0, CH))[1].astype(BF)
+            force = nn_dot(headf[...], beside([h[j] for j in range(EDGE)]))
+            for j in range(EDGE):
+                f_edge[j] = force[:, j * LANES : (j + 1) * LANES]
+            at = pl.ds(line + EDGE, EDGE)
+            for c in range(2):
+                force = f_edge[:, c, :] + bias[c]
+                q_edge[c] = (u_ext[c, at, :] + DT_FORCE * force) * opened[at, :]
+            halo_start(*push_args(t))
+
         def block(base, size):
             lows = []
             for c in channel_blocks():
@@ -671,7 +724,15 @@
         for c in range(2):
             force = frows[:, c, :] + bias[c]
             q_ext[t, c, own, :] = (u_ext[c, own, :] + DT_FORCE * force) * opened[own, :]
-        ext_halo(11, q_ext.at[t])
+        if not two:
+            halo_start(*push_args(t))
+        halo_wait(*push_args(t))
+
+        @pl.when(t == 0)
+        def _():
+            leave((1,))
+            arrive((1,))
+
         qr, qc = q_ext[t, 0], q_ext[t, 1]
         grid = grid_mask[...]
         vr = grid * (qr - DT_ADV * (qr * drows(qr) + qc * dcols(qr)))
@@ -714,10 +775,17 @@
                 bar_block(xh_full, 2, t, base, size, c, bars[:, c, :]).astype(BF)
                 for c in channel_blocks()
             ]
-            h = jnp.concatenate(lows, axis=1)
-            ghead[...] += nt_dot(beside([h[j] for j in range(size)]), low)
+            sg[pl.ds(base + 1, size), CH : 2 * CH, :] = jnp.concatenate(lows, axis=1)
 
         for_blocks(rows, BAR_LINES, block)
+
+    def head_sums():
+        def block(base, size):
+            h = beside([sg[base + 1 + j, CH : 2 * CH, :] for j in range(size)])
+            low = beside([frows[base + j].astype(BF) for j in range(size)])
+            ghead[...] += nt_dot(h, low)
+
+        for_blocks(rows, SUM_LINES, block)
 
     def sums_start(layer):
         gain = norms[0, layer]
@@ -742,15 +810,9 @@
             return (zbuf[at, c, :] * coef[0, c] + n * coef[1, c] + coef[2, c]).astype(BF)
 
         slot = 5 + layer
-        for which, line in enumerate((0, count - 1)):
+        for which, line in edge_lines(count - 1):
             edges[slot, which] = z_bar(line, slice(0, CH))
-        args = (
-            slot,
-            edges.at[slot, 0],
-            edges.at[slot, 1],
-            g_halo.at[layer, 0],
-            g_halo.at[layer, 1],
-        )
+        args = (slot, edge_source(slot), lambda side: g_halo.at[layer, side])
         halo_start(*args)
 
         def block(base, size):
@@ -765,13 +827,12 @@
         for_blocks(count, ACT_LINES, block)
         halo_wait(*args)
         if by:
-            spread_halo(dst, (g_halo[layer, 0], g_halo[layer, 1]), count, by, BACKWARD)
+            spread_halo(dst, lambda side: g_halo[layer, side], count, by, BACKWARD)
         else:
-            dst[0, CH : 2 * CH, :] = g_halo[layer, 0]
-            dst[count + 1, CH : 2 * CH, :] = g_halo[layer, 1]
-
-    def bar_rows(weight, g, size):
-        y = nn_dot(weight, g)
+            for side in halo_sides():
+                dst[side * (count + 1), CH : 2 * CH, :] = g_halo[layer, side]
+
+    def tap_sums(y, size):
         return [
             tap_rows(y, j + 2, 0) + tap_rows(y, j + 1, 1) + tap_rows(y, j, 2) for j in range(size)
         ]
@@ -781,7 +842,7 @@
 
         def block(base, size):
             g = beside([src[base + j] for j in range(size + 2)])
-            then(base, size, jnp.stack(bar_rows(wb[layer], g, size), axis=0))
+            then(base, size, jnp.stack(tap_sums(nn_dot(wb[layer], g), size), axis=0))
 
         for_blocks(count, BAR_LINES, block)
 
@@ -798,9 +859,10 @@
 
         def block(base, size):
             g = beside([sg[base + j] for j in range(size + 2)])
-            for j, bar in enumerate(bar_rows(wb[4], g, size)):
+            y = nn_dot(wb[3:5].reshape(6 * CH, 3 * CH), g)
+            for j, bar in enumerate(tap_sums(y[3 * CH :], size)):
                 skip_bar[base + j] = bar
-            ups = bar_rows(wb[3], g, size)
+            ups = tap_sums(y[: 3 * CH], size)
             low = base // 2
             bars = jnp.stack(
                 [pair_sum(ups[2 * j] + ups[2 * j + 1]) for j in range(size // 2)], axis=0
@@ -815,13 +877,13 @@
             g = beside([sg[base + 1 + j] for j in range(size)])
             low = base // 2
             h = beside([skip[t, pl.ds(base + j, 3)].reshape(3 * CH, LANES) for j in range(size)])
-            gw[line_at[4] : line_at[4] + 3 * CH, :] += nt_dot(g, h)
             up = beside(
                 [
                     jnp.concatenate([h4[t, low + (j + ky - 1) // 2 + 1] for ky in range(3)], axis=0)
                     for j in range(size)
                 ]
             )
+            gw[line_at[4] : line_at[4] + 3 * CH, :] += nt_dot(g, h)
             gw[line_at[3] : line_at[3] + 3 * CH, :] += nt_dot(g, up)
 
         for_blocks(rows, SUM_LINES, block)
@@ -942,19 +1004,8 @@
     def gather_finish(p):
         exchange_finish(chunk_back, members, p)
 
-    def at_last(t, what, p):
-        @pl.when(t == 0)
-        def _():
-            what(p)
-
     def w_args():
-        return (
-            12,
-            w_ext.at[:, pl.ds(EDGE, EDGE), :],
-            w_ext.at[:, pl.ds(rows, EDGE), :],
-            w_ext.at[:, pl.ds(0, EDGE), :],
-            w_ext.at[:, pl.ds(rows + EDGE, EDGE), :],
-        )
+        return ext_args(12, w_ext)
 
     def pull_start(t):
         facts = m_own[0]
@@ -968,8 +1019,12 @@
             w_ext[c, own, :] = open_own * (u_bar[c] + 2.0 * open_own * pull)
         halo_start(*w_args())
 
-    def backward_step(i, carry):
-        t = STEPS - 1 - i
+    def backward_step(t):
+        def at_last(what, p):
+            @pl.when(t == 0)
+            def _():
+                what(p)
+
         halo_wait(*w_args())
         grid = grid_mask[...]
         gr, gc = project(w_ext[0], w_ext[1], grid)
@@ -994,11 +1049,12 @@
 
         first_pass_last(t)
         sums_start(4)
+        head_sums()
         second_pass(4, t, rows, xh_full, 2, sg, 1)
         bars_last(t)
         sums_start(3)
         weight_sums_last(t)
-        at_last(t, plane_start, 2)
+        at_last(plane_start, 2)
         second_pass(3, t, half, xh_half, 1, sgh, 2)
 
         def into_two(base, size, bars):
@@ -1020,8 +1076,8 @@
         bars_of(1, half, sgh, into_one)
         sums_start(1)
         weight_sums(1, t, half, sgh, pooled)
-        at_last(t, plane_finish, 2)
-        at_last(t, plane_start, 1)
+        at_last(plane_finish, 2)
+        at_last(plane_start, 1)
         second_pass(1, t, rows, xh_full, 1, sg, 1)
 
         def into_zero(base, size, bars):
@@ -1031,9 +1087,8 @@
         bars_of(0, rows, sg, into_zero)
         sums_start(0)
         weight_sums(0, t, rows, sg, h1)
-        at_last(t, plane_start, 0)
+        at_last(plane_start, 0)
         second_pass(0, t, rows, xh_full, 0, sg, 0)
-
         @pl.when(t > 0)
         def _():
             taps_first()
@@ -1046,14 +1101,16 @@
                     columns.append(total)
                 u_bar[c] += from_right(columns[0], 1) + columns[1] + from_left(columns[2], 1)
             pull_start(t - 1)
-
-        at_last(t, plane_finish, 1)
+        at_last(plane_finish, 1)
         weight_sums_first(t)
-        at_last(t, line_finish, 2)
+        at_last(line_finish, 2)
+
+    pull_start(jnp.int32(STEPS - 1))
+    def step_back(i, carry):
+        backward_step(STEPS - 1 - i)
         return carry
 
-    pull_start(jnp.int32(STEPS - 1))
-    lax.fori_loop(0, STEPS, backward_step, 0)
+    lax.fori_loop(0, STEPS, step_back, 0)
 
     lane = lane_of((CH, CH))
     small_sums = jnp.concatenate([gw0[...], jnp.zeros((CH, CH - 48), F32)], axis=1)
@@ -1153,6 +1210,8 @@
             pltpu.VMEM((STEPS, ext, 16, LANES), BF),
             pltpu.VMEM((STEPS, 2, ext, LANES), F32),
             pltpu.VMEM((STEPS, 2, rows, LANES), F32),
+            pltpu.VMEM((2, EDGE, LANES), F32),
+            pltpu.VMEM((EDGE, 16, LANES), F32),
             pltpu.VMEM((2, ext, LANES), F32),
             pltpu.VMEM((2, rows, LANES), F32),
             pltpu.VMEM((rows, 16, LANES), F32),

time: 178 us -> 175 us (0.983)
  Pallas kernels: 177 us -> 174 us
    pallas_call x1, Pallas kernels: 171 us -> 168 us  [train(): pl.pallas_call(functools.partial(train_kernel, ranks, planes), out_shape=...]
where the time goes in v5:
time: 175 us
  Pallas kernels  174 us (99%)
    pallas_call x1, Pallas kernels, train(): pl.pallas_call(functools.partial(train_kernel, ranks, planes), out_shape=...  168 us
    pallas_call x1, Pallas kernels, adam(): pl.pallas_call(functools.partial(adam_kernel, line_at), grid=(3,), out_sh...  6.29 us

profile of v5, /device:TPU:0, one launch (start us, length us, event | category | flops | bytes accessed | tf_op | source)
XLA Modules:
  0.0 175.2 jit_solution(2078320024553803134)
XLA Ops:
  0.7 168.1 %train.1 = (bf16[1024,192]{1,0:T(8,128)(2,1)}, f32[32,128]{1,0:T(8,128)}, f32[8,128]{1,0:T(8,128)}) custom-call(s32[2,2]{1,0:T(2,128)} %keys.1, s32[2,2,4]{2,1,0:T(2,128)} %boxes.1, f32[2,2,32,128]{3,2,1,0:T(8,128)} %vel.1, f32[2,2,2,32,128]{4,3,2,1,0:T(8,128)} %tgt.1, f32[3,3,3,64]{3,2,1,0:T(4,128)} %bitcast.27, f32[9,5,4096]{2,1,0:T(8,128)} %bitcast.23, ...), custom_call_target="tpu_custom_call" | custom-call | tf_op jit(solution)/shard_map/train/pallas_call | solution.py:1177
  168.7 6.3 %adam.1 = (f32[3,3,3,64]{3,2,1,0:T(4,128)}, f32[3,3,3,64]{3,2,1,0:T(4,128)}, f32[3,3,3,64]{3,2,1,0:T(4,128)}, f32[9,5,4096]{2,1,0:T(8,128)}, f32[9,5,4096]{2,1,0...) custom-call(bf16[1024,192]{1,0:T(8,128)(2,1)} %get-tuple-element.39., ...), custom_call_target="tpu_custom_call" | custom-call | tf_op jit(solution)/shard_map/adam/pallas_call | solution.py:1340

commit v6 on v5

--- a/solution.py
+++ b/solution.py
@@ -1044,8 +1044,6 @@
             force_bar = DT_FORCE * passed
             misc[2 + c] += sublanes(force_bar)
             frows[:, c, :] = force_bar
-        for c in range(2, 16):
-            frows[:, c, :] = jnp.zeros((rows, LANES), F32)
 
         first_pass_last(t)
         sums_start(4)
@@ -1135,22 +1133,25 @@
     m_line[level] = lax.fori_loop(0, members, lambda k, total: total + m_plane[k], no_sums)
     exchange_start(small_line, planes)
     line_finish(0)
+
+    def squares(i, total):
+        at = pl.ds(pl.multiple_of(i * 128, 128), 128)
+        block = g_all[at, :].astype(F32)
+        return total + jnp.sum((block * block).reshape(16, 8, 3 * CH), axis=0)
+
+    gather_finish(2)
+    gather_finish(1)
+    early = starts[1] // 128
+    square = lax.fori_loop(early, all_lines // 128, squares, jnp.zeros((8, 3 * CH), F32))
     exchange_finish(small_line, planes)
-    for p in (2, 1, 0):
-        gather_finish(p)
-
     totals = lax.fori_loop(0, planes, lambda k, total: total + m_line[k], no_sums)
     small_out[...] = totals[8:]
     small_square = jnp.sum(sublanes(totals[8:] * totals[8:]), axis=0, keepdims=True)
     small_square = jnp.sum(small_square, axis=1, keepdims=True)
     totals = jnp.broadcast_to(jnp.sum(totals[:8], axis=1, keepdims=True), (8, LANES))
 
-    def squares(i, total):
-        at = pl.ds(pl.multiple_of(i * 64, 64), 64)
-        block = g_all[at, :].astype(F32)
-        return total + jnp.sum((block * block).reshape(8, 8, 3 * CH), axis=0)
-
-    square = lax.fori_loop(0, all_lines // 64, squares, jnp.zeros((8, 3 * CH), F32))
+    gather_finish(0)
+    square = lax.fori_loop(0, early, squares, square)
     square = jnp.sum(jnp.sum(square, axis=0, keepdims=True), axis=1, keepdims=True)
     count = totals[1:2]
     raw = square + small_square + totals[2:3] * totals[2:3] + totals[3:4] * totals[3:4]

time: 175 us -> 175 us (level)
  no operation moved by 1% of the time
where the time goes in v6:
time: 175 us
  Pallas kernels  174 us (99%)
    pallas_call x1, Pallas kernels, train(): pl.pallas_call(functools.partial(train_kernel, ranks, planes), out_shape=...  168 us
    pallas_call x1, Pallas kernels, adam(): pl.pallas_call(functools.partial(adam_kernel, line_at), grid=(3,), out_sh...  6.29 us

profile of v6, /device:TPU:0, one launch (start us, length us, event | category | flops | bytes accessed | tf_op | source)
XLA Modules:
  0.0 174.9 jit_solution(13961071105471010931)
XLA Ops:
  0.7 167.7 %train.1 = (bf16[1024,192]{1,0:T(8,128)(2,1)}, f32[32,128]{1,0:T(8,128)}, f32[8,128]{1,0:T(8,128)}) custom-call(s32[2,2]{1,0:T(2,128)} %keys.1, s32[2,2,4]{2,1,0:T(2,128)} %boxes.1, f32[2,2,32,128]{3,2,1,0:T(8,128)} %vel.1, f32[2,2,2,32,128]{4,3,2,1,0:T(8,128)} %tgt.1, f32[3,3,3,64]{3,2,1,0:T(4,128)} %bitcast.27, f32[9,5,4096]{2,1,0:T(8,128)} %bitcast.23, ...), custom_call_target="tpu_custom_call" | custom-call | tf_op jit(solution)/shard_map/train/pallas_call | solution.py:1178
  168.4 6.3 %adam.1 = (f32[3,3,3,64]{3,2,1,0:T(4,128)}, f32[3,3,3,64]{3,2,1,0:T(4,128)}, f32[3,3,3,64]{3,2,1,0:T(4,128)}, f32[9,5,4096]{2,1,0:T(8,128)}, f32[9,5,4096]{2,1,0...) custom-call(bf16[1024,192]{1,0:T(8,128)(2,1)} %get-tuple-element.39., ...), custom_call_target="tpu_custom_call" | custom-call | tf_op jit(solution)/shard_map/adam/pallas_call | solution.py:1341
